TPU v7x, 32 devices: a whole 2x2x4 slice. The times are simulated.
32 devices in a mesh: dp: 8 (over z, y), tensor: 4 (over x, core).
Axes of the slice: x: 2, y: 2, z: 4, core: 2. Of those that a mesh axis runs over, the one named last changes fastest.
Arguments:
- x_in: bfloat16 [8, 1024, 1536], P(None, 'dp'), may hold values from -6 to 6
- cotangent: bfloat16 [8, 1024, 1536], P('dp'), may hold values from -6 to 6
- lengths: int32 [8], replicated, may hold values from 128 to 1024, as said below
- deal_order: int32 [8], replicated, may hold values from 0 to 7, each once
- norm_gains: float32 [3, 1536], replicated, may hold values from 0.1 to 1.9
- proj_gate: bfloat16 [2, 1536, 3072], P(None, None, 'tensor'), may hold values from -0.15625 to 0.15625
- proj_value: bfloat16 [2, 1536, 3072], P(None, None, 'tensor'), may hold values from -0.15625 to 0.15625
- proj_state: bfloat16 [2, 1536, 256], replicated, may hold values from -0.15625 to 0.15625
- proj_step: bfloat16 [2, 1536, 48], P(None, None, 'tensor'), may hold values from -0.15625 to 0.15625
- proj_out: bfloat16 [2, 1536, 3072], P(None, None, 'tensor'), may hold values from -0.109375 to 0.109375
- conv_value: float32 [2, 5, 3072], P(None, None, 'tensor'), may hold values from -0.5 to 0.5
- conv_state: float32 [2, 5, 256], replicated, may hold values from -0.5 to 0.5
- step_bias: float32 [2, 48], P(None, 'tensor'), may hold values from -7 to -2
- decay_log: float32 [2, 48], P(None, 'tensor'), may hold values from -0.7 to 2.8
- skip_gain: float32 [2, 48], P(None, 'tensor'), may hold values from 0.5 to 1.5
- inner_gain: float32 [2, 3072], P(None, 'tensor'), may hold values from 0.1 to 1.9
Outputs:
- result: bfloat16 [8, 1024, 1536], P('dp')
- grad_x_in: bfloat16 [8, 1024, 1536], P(None, 'dp')
- grad_norm_gains: float32 [3, 1536], P(None, 'dp')
- grad_proj_gate: float32 [2, 1536, 3072], P(None, 'dp', 'tensor')
- grad_proj_value: float32 [2, 1536, 3072], P(None, 'dp', 'tensor')
- grad_proj_state: float32 [2, 1536, 256], P(None, 'dp')
- grad_proj_step: float32 [2, 1536, 48], P(None, 'dp', 'tensor')
- grad_proj_out: float32 [2, 1536, 3072], P(None, 'dp', 'tensor')
- grad_conv_value: float32 [2, 5, 3072], P(None, None, 'tensor')
- grad_conv_state: float32 [2, 5, 256], replicated
- grad_step_bias: float32 [2, 48], P(None, 'tensor')
- grad_decay_log: float32 [2, 48], P(None, 'tensor')
- grad_skip_gain: float32 [2, 48], P(None, 'tensor')
- grad_inner_gain: float32 [2, 3072], P(None, 'tensor')
Inputs may be any that keep to these rules, and one draw needn't show every extreme that they name: `lengths`: valid tokens of each sequence's slot of 1024; some sequence fills its slot and some has 128. A permutation of the 8 sequences; dealt position s holds sequence deal_order[s], and positions s * 1 onward go to index s of dp.
All inputs are finite; a program needn't handle non-finite values.
Results may differ from a plain program's by a relative error of at most 0.018.
Values may be sent and summed in bfloat16 or wider, within the bound.
No kernel may reach another device: no remote copies, remote signals or barrier semaphores. Data moves between devices by JAX's collectives and lax.ppermute only.
A program may use at most 256 MiB of HBM per device.

v0:
```python
import jax
import jax.numpy as jnp
from jax import lax
from jax.sharding import PartitionSpec as P

P_SIZE = 64
Q = 256


exact_mode = lax.Precision.HIGHEST
eps_norm = 1e-05


def causal_conv(values, conv_taps):
    tap_count = conv_taps.shape[0] - 1
    padded = jnp.pad(values, ((tap_count - 1, 0), (0, 0)))
    summed = conv_taps[tap_count] + jnp.zeros_like(values)
    for offset in range(tap_count):
        summed = summed + conv_taps[offset] * padded[offset : offset + values.shape[0]]
    return summed


def block_scan(per_head, step_size, decay, state_in, state_out):
    length, head_count, head_size = per_head.shape
    block_count = length // Q
    log_decay = -(step_size * decay[None, :])
    cumulative = jnp.cumsum(log_decay.reshape(block_count, Q, head_count), axis=1)
    scaled_x = (per_head * step_size[:, :, None]).reshape(block_count, Q, head_count, head_size)
    b_blocks = state_in.reshape(block_count, Q, -1)
    c_blocks = state_out.reshape(block_count, Q, -1)
    row_ids = lax.broadcasted_iota(jnp.int32, (Q, Q), 0)
    col_ids = lax.broadcasted_iota(jnp.int32, (Q, Q), 1)
    causal = row_ids >= col_ids
    gaps = cumulative[:, :, None, :] - cumulative[:, None, :, :]
    weights = jnp.exp(jnp.where(causal[None, :, :, None], gaps, -jnp.inf))
    scores = jnp.einsum("cin,cjn->cij", c_blocks, b_blocks, precision=exact_mode)
    within = jnp.einsum(
        "cijh,cjhp->cihp", scores[..., None] * weights, scaled_x, precision=exact_mode
    )
    to_end = jnp.exp(cumulative[:, -1:, :] - cumulative)
    states = jnp.einsum(
        "cjn,cjhp->chpn", b_blocks, scaled_x * to_end[..., None], precision=exact_mode
    )
    block_decay = jnp.exp(cumulative[:, -1, :])
    carried = jnp.zeros((head_count, head_size, b_blocks.shape[-1]), jnp.float32)
    entering = []
    for block_at in range(block_count):
        entering.append(carried)
        carried = carried * block_decay[block_at][:, None, None] + states[block_at]
    entering = jnp.stack(entering)
    across = (
        jnp.einsum("cin,chpn->cihp", c_blocks, entering, precision=exact_mode)
        * jnp.exp(cumulative)[..., None]
    )
    return (within + across).reshape(length, head_count, head_size)


def mixer_inner(
    gate_in, value_in, state_in, step_in, conv_value, conv_state, step_bias, decay_log, skip_gain
):
    values = jax.nn.silu(causal_conv(value_in, conv_value))
    states = jax.nn.silu(causal_conv(state_in, conv_state))
    state_width = states.shape[1] // 2
    step_size = jax.nn.softplus(step_in + step_bias)
    head_count = step_size.shape[1]
    per_head = values.reshape(values.shape[0], head_count, P_SIZE)
    mixed_out = block_scan(
        per_head, step_size, jnp.exp(decay_log), states[:, :state_width], states[:, state_width:]
    )
    mixed_out = mixed_out + skip_gain[:, None] * per_head
    return mixed_out.reshape(values.shape[0], -1) * jax.nn.silu(gate_in)


def local_mixer(
    gate_in, value_in, state_in, step_in, conv_value, conv_state, step_bias, decay_log, skip_gain
):

    def single(gate_seq, value_seq, state_seq, step_seq):
        return mixer_inner(
            gate_seq,
            value_seq,
            state_seq,
            step_seq,
            conv_value,
            conv_state,
            step_bias,
            decay_log,
            skip_gain,
        )

    return jax.vmap(single)(gate_in, value_in, state_in, step_in)


def norm_parts(hidden):
    row_scale = lax.rsqrt(jnp.mean(hidden * hidden, axis=-1, keepdims=True) + eps_norm)
    return (hidden * row_scale, row_scale)


def norm_back(grad_normed, normed, row_scale):
    return row_scale * (
        grad_normed - normed * jnp.mean(grad_normed * normed, axis=-1, keepdims=True)
    )


def matmul(left, right):
    return jnp.dot(left, right, preferred_element_type=jnp.float32)


def times_transposed(left, right):
    return lax.dot_general(
        left, right, (((1,), (1,)), ((), ())), preferred_element_type=jnp.float32
    )


def outer_rows(left, right):
    return lax.dot_general(
        left, right, (((0,), (0,)), ((), ())), preferred_element_type=jnp.float32
    )


def per_device(
    x_in,
    cotangent,
    lengths,
    deal_order,
    norm_gains,
    proj_gate,
    proj_value,
    proj_state,
    proj_step,
    proj_out,
    conv_value,
    conv_state,
    step_bias,
    decay_log,
    skip_gain,
    inner_gain,
):
    seq_count, slot_len, model_width = cotangent.shape
    row_count = seq_count * slot_len
    layer_count = proj_gate.shape[0]
    full_inner = proj_gate.shape[2] * lax.axis_size("tensor")
    first_seq = lax.axis_index("dp") * seq_count
    own_seqs = lax.dynamic_slice_in_dim(deal_order, first_seq, seq_count)
    own_length = jnp.take(lengths, own_seqs)
    positions = lax.broadcasted_iota(jnp.int32, (seq_count, slot_len), 1)
    valid = (positions < own_length[:, None]).astype(jnp.float32).reshape(row_count, 1)
    dealt = lax.all_to_all(
        jnp.take(x_in, deal_order, axis=0), "dp", split_axis=0, concat_axis=1, tiled=True
    )
    hidden = dealt.reshape(row_count, model_width).astype(jnp.float32) * valid
    grad_out = cotangent.reshape(row_count, model_width).astype(jnp.float32) * valid
    stored = []
    for index_layer in range(layer_count):
        normed, row_scale = norm_parts(hidden)
        lowered = (normed * norm_gains[index_layer]).astype(jnp.bfloat16)
        gate_in = matmul(lowered, proj_gate[index_layer]).reshape(seq_count, slot_len, -1)
        value_in = matmul(lowered, proj_value[index_layer]).reshape(seq_count, slot_len, -1)
        state_in = matmul(lowered, proj_state[index_layer]).reshape(seq_count, slot_len, -1)
        step_in = matmul(lowered, proj_step[index_layer]).reshape(seq_count, slot_len, -1)
        gated, pullback = jax.vjp(
            local_mixer,
            gate_in,
            value_in,
            state_in,
            step_in,
            conv_value[index_layer],
            conv_state[index_layer],
            step_bias[index_layer],
            decay_log[index_layer],
            skip_gain[index_layer],
        )
        gated = gated.reshape(row_count, -1)
        total_sq = lax.psum(jnp.sum(gated * gated, axis=1, keepdims=True), "tensor")
        gate_scale = lax.rsqrt(total_sq / full_inner + eps_norm)
        gate_out = (gated * gate_scale * inner_gain[index_layer]).astype(jnp.bfloat16)
        partial_value = times_transposed(gate_out, proj_out[index_layer])
        branch = lax.psum(partial_value, "tensor")
        stored.append((normed, row_scale, lowered, gated, gate_scale, gate_out, pullback))
        hidden = hidden + branch
    final_normed, final_scale = norm_parts(hidden)
    result = (final_normed * norm_gains[layer_count] * valid).astype(jnp.bfloat16)
    gain_final_grad = jnp.sum(grad_out * final_normed, axis=0)
    grad_hidden = norm_back(grad_out * norm_gains[layer_count], final_normed, final_scale)
    big_list = []
    small_list = []
    for index_layer in reversed(range(layer_count)):
        normed, row_scale, lowered, gated, gate_scale, gate_out, pullback = stored[index_layer]
        grad_branch = grad_hidden.astype(jnp.bfloat16)
        g_out = outer_rows(grad_branch, gate_out)
        grad_gate_out = matmul(grad_branch, proj_out[index_layer])
        g_inner = jnp.sum(grad_gate_out * gated * gate_scale, axis=0)
        grad_scaled = grad_gate_out * inner_gain[index_layer]
        back_stat = lax.psum(jnp.sum(grad_scaled * gated, axis=1, keepdims=True), "tensor")
        grad_gated = gate_scale * grad_scaled - gated * gate_scale**3 * back_stat / full_inner
        (
            back_gate,
            back_value,
            back_state,
            back_step,
            back_conv_value,
            back_conv_state,
            back_bias,
            back_decay,
            back_skip,
        ) = pullback(grad_gated.reshape(seq_count, slot_len, -1))
        back_state, back_conv_state = (
            lax.psum(back_state.astype(jnp.bfloat16), "tensor").astype(jnp.float32),
            lax.psum(back_conv_state.astype(jnp.bfloat16), "tensor").astype(jnp.float32),
        )
        low_gate = back_gate.reshape(row_count, -1).astype(jnp.bfloat16)
        low_value = back_value.reshape(row_count, -1).astype(jnp.bfloat16)
        low_state = back_state.reshape(row_count, -1).astype(jnp.bfloat16)
        low_step = back_step.reshape(row_count, -1).astype(jnp.bfloat16)
        g_gate = outer_rows(lowered, low_gate)
        g_value = outer_rows(lowered, low_value)
        g_state = outer_rows(lowered, low_state)
        g_step = outer_rows(lowered, low_step)
        head_terms = (
            times_transposed(low_gate, proj_gate[index_layer])
            + times_transposed(low_value, proj_value[index_layer])
            + times_transposed(low_step, proj_step[index_layer])
        )
        grad_lowered = lax.psum(head_terms, "tensor") + times_transposed(
            low_state, proj_state[index_layer]
        )
        g_gain = jnp.sum(grad_lowered * normed, axis=0)
        grad_hidden = grad_hidden + norm_back(
            grad_lowered * norm_gains[index_layer], normed, row_scale
        )
        if index_layer == layer_count - 1:
            gain_piece = jnp.stack([g_gain, gain_final_grad])
        else:
            gain_piece = g_gain[None]
        big_piece = (
            g_gate[None],
            g_value[None],
            g_state[None],
            g_step[None],
            g_out[None],
            gain_piece,
        )
        small_piece = (
            back_conv_value[None],
            back_conv_state[None],
            back_bias[None],
            back_decay[None],
            back_skip[None],
            g_inner[None],
        )
        big_list.insert(0, big_piece)
        small_list.insert(0, small_piece)
    big_all = [jnp.concatenate([item[member] for item in big_list], axis=0) for member in range(6)]
    small_all = [
        jnp.concatenate([item[member] for item in small_list], axis=0) for member in range(6)
    ]
    big_all = (
        lax.psum_scatter(
            big_all[0].astype(jnp.bfloat16), "dp", scatter_dimension=1, tiled=True
        ).astype(jnp.float32),
        lax.psum_scatter(
            big_all[1].astype(jnp.bfloat16), "dp", scatter_dimension=1, tiled=True
        ).astype(jnp.float32),
        lax.psum_scatter(
            big_all[2].astype(jnp.bfloat16), "dp", scatter_dimension=1, tiled=True
        ).astype(jnp.float32),
        lax.psum_scatter(
            big_all[3].astype(jnp.bfloat16), "dp", scatter_dimension=1, tiled=True
        ).astype(jnp.float32),
        lax.psum_scatter(
            big_all[4].astype(jnp.bfloat16), "dp", scatter_dimension=1, tiled=True
        ).astype(jnp.float32),
        lax.psum_scatter(
            big_all[5].astype(jnp.bfloat16), "dp", scatter_dimension=1, tiled=True
        ).astype(jnp.float32),
    )
    small_all = lax.psum(
        (small_all[0], small_all[1], small_all[2], small_all[3], small_all[4], small_all[5]), "dp"
    )
    grad_in = (grad_hidden * valid).astype(jnp.bfloat16)
    grad_in = grad_in.reshape(seq_count, slot_len, model_width)
    returned = lax.all_to_all(grad_in, "dp", split_axis=1, concat_axis=0, tiled=True)
    grad_x = jnp.zeros_like(returned).at[deal_order].set(returned)
    return (
        result.reshape(seq_count, slot_len, model_width),
        grad_x,
        big_all[5],
        big_all[0],
        big_all[1],
        big_all[2],
        big_all[3],
        big_all[4],
        small_all[0],
        small_all[1],
        small_all[2],
        small_all[3],
        small_all[4],
        small_all[5],
    )


def solution(mesh):
    return jax.shard_map(
        per_device,
        mesh=mesh,
        in_specs=(
            P(None, "dp", None),
            P("dp", None, None),
            P(),
            P(),
            P(),
            P(None, None, "tensor"),
            P(None, None, "tensor"),
            P(),
            P(None, None, "tensor"),
            P(None, None, "tensor"),
            P(None, None, "tensor"),
            P(),
            P(None, "tensor"),
            P(None, "tensor"),
            P(None, "tensor"),
            P(None, "tensor"),
        ),
        out_specs=(
            P("dp", None, None),
            P(None, "dp", None),
            P(None, "dp"),
            P(None, "dp", "tensor"),
            P(None, "dp", "tensor"),
            P(None, "dp", None),
            P(None, "dp", "tensor"),
            P(None, "dp", "tensor"),
            P(None, None, "tensor"),
            P(),
            P(None, "tensor"),
            P(None, "tensor"),
            P(None, "tensor"),
            P(None, "tensor"),
        ),
        check_vma=False,
    )
```

profile of v0, /device:TPU:0, one launch (start us, length us, event | category | flops | bytes accessed | tf_op | source)
XLA Modules:
  0.0 1693.6 jit_solution(11663970332939297385)
XLA Ops:
  15.5 7.4 all-to-all-start
  32.5 61.1 %all-to-all-done = bf16[8,128,1536]{2,1,0:T(8,128)(2,1)S(1)} async-done(((bf16[8,128,1536]{2,1,0:T(8,128)(2,1)}), bf16[8,128,1536]{2,1,0:T(8,128)(2,1)S(1)}, u32[]{:S(2)}, u32[]{:S(2)}) %all-to-all-start) | async-done | bytes 3145760 | tf_op jit(solution)/shard_map/all_to_all | solution.py:148
  131.2 5.7 fusion.166
  141.1 14.1 bitcast_add_fusion.3
  163.4 10.5 multiply_reduce_fusion.24
  180.1 8.0 fusion.106
  189.5 117.7 %all-reduce.69.cloned.1.call-done = f32[1024,1536]{1,0:T(8,128)} async-done(((f32[1024,1536]{1,0:T(8,128)}), f32[1024,1536]{1,0:T(8,128)}) %all-reduce.69.cloned.1.call-update) | async-done | bytes 6291472 | tf_op jit(solution)/shard_map/psum | solution.py:178
  320.5 6.0 fusion.102
  330.4 8.2 fusion.63
  350.3 5.7 fusion.169
  360.1 13.9 bitcast_add_fusion.2
  382.1 8.7 multiply_reduce_fusion.23
  390.7 6.2 psum.128
  397.6 7.9 fusion.94
  410.3 115.3 %all-reduce.71.cloned.1.call-done = f32[1024,1536]{1,0:T(8,128)} async-done(((f32[1024,1536]{1,0:T(8,128)}), f32[1024,1536]{1,0:T(8,128)}) %all-reduce.71.cloned.1.call-update) | async-done | bytes 6291472 | tf_op jit(solution)/shard_map/psum | solution.py:178
  535.3 7.7 multiply_reduce_fusion.7
  543.0 6.6 psum.130
  549.6 7.6 fusion.56
  571.6 7.5 fusion.173
  592.6 18.2 %fusion.11 = (f32[4,256,12]{1,2,0:T(8,128)}, f32[4,256,12]{1,2,0:T(8,128)}, f32[4,256,256]{2,1,0:T(8,128)S(1)}) fusion(f32[4,256,12]{1,2,0:T(8,128)S(1)} %copy-done.135, f32[4,256,256]{2,1,0:T(8,128)S(1)} %copy-done.92, pred[256,256]{1,0:T(8,128)(4,1)S(1)} %copy-done.139, f32[4,256,12,64]{1,0,3,2:T(4,128)S(1)} %copy-done.26, ...), kind=kOutput, calls=%fused_computation.21 | convolution fusion | flops 2444730368 | bytes 8650752 | tf_op jit(solution)/shard_map/transpose(jvp(vmap(cijh,cjhp->cihp)))/dot_general | solution.py:37
  625.8 6.1 fusion.59
  632.0 10.5 bitcast_add_fusion.1
  649.9 9.9 reduce-window.34
  675.9 10.5 multiply_reduce_fusion.12
  702.9 114.9 %all-reduce.73.cloned.1.call-done = f32[1024,1536]{1,0:T(8,128)} async-done(((f32[1024,1536]{1,0:T(8,128)}), f32[1024,1536]{1,0:T(8,128)}) %all-reduce.73.cloned.1.call-update) | async-done | bytes 6291472 | tf_op jit(solution)/shard_map/psum | solution.py:224
  817.8 7.6 multiply_reduce_fusion
  825.4 8.3 multiply_add_fusion
  833.7 8.6 multiply_reduce_fusion.8
  842.3 5.9 psum.133
  848.2 7.5 fusion.57
  879.1 7.5 fusion.172
  890.9 18.8 %fusion.13 = (f32[4,256,12]{1,2,0:T(8,128)}, f32[4,256,12]{1,2,0:T(8,128)}, f32[4,256,256]{2,1,0:T(8,128)}) fusion(f32[4,256,12]{1,2,0:T(8,128)S(1)} %copy-done.133, f32[4,256,256]{2,1,0:T(8,128)S(1)} %copy-done.90, pred[256,256]{1,0:T(8,128)(4,1)S(1)} %copy-done.141, f32[4,256,12,64]{1,0,3,2:T(4,128)S(1)} %copy-done.23, f32[4,256,12]{1,2,0:T(8,128)S(1)} %copy-done.84, ...), kind=kOutput, calls=%fused_computation.23 | convolution fusion | flops 2444730368 | bytes 8650752 | tf_op jit(solution)/shard_map/transpose(jvp(vmap(cijh,cjhp->cihp)))/dot_general | solution.py:37
  913.4 10.5 bitcast_add_fusion
  940.3 11.2 reduce-window.36
  992.6 9.9 multiply_reduce_fusion.16
  1029.3 118.0 %all-reduce.77.cloned.1.call-done = f32[1024,1536]{1,0:T(8,128)} async-done(((f32[1024,1536]{1,0:T(8,128)}), f32[1024,1536]{1,0:T(8,128)}) %all-reduce.77.cloned.1.call-update) | async-done | bytes 6291472 | tf_op jit(solution)/shard_map/psum | solution.py:224
  1147.3 7.9 multiply_reduce_fusion.1
  1159.2 8.6 fusion.71
  1167.9 5.8 fusion.70
  1198.1 5.8 multiply_convert_fusion
  1204.0 35.0 %copy.979 = bf16[1,1024,1536]{2,0,1:T(2,128)(2,1)} copy(bf16[1,1024,1536]{2,1,0:T(8,128)(2,1)S(1)} %bitcast.812) | data formatting | bytes 6291456 | tf_op jit(solution)/shard_map/reshape | solution.py:281
  1239.5 20.3 %reduce.88 = bf16[1024,1536]{1,0:T(8,128)(2,1)S(1)} reduce(bf16[1024,1,1536]{2,1,0:T(2,128)(2,1)} %bitcast.775, bf16[]{:T(256)} %broadcast.933), dimensions={1}, to_apply=%bitcast.758.reduce_sub_computation | reduce | bytes 6291458
  1270.8 6.5 all-reduce.61
  1277.5 100.9 %all-reduce.60 = (f32[2,5,768]{2,1,0:T(8,128)S(1)}, f32[2,5,256]{2,1,0:T(8,128)S(1)}, f32[2,12]{1,0:T(2,128)}, f32[2,12]{1,0:T(2,128)}, f32[2,12]{1,0:T(2,128)}, /*index=5*/f32[2,768]{1,0:T(2,128)}) all-reduce(f32[2,5,768]{2,1,0:T(8,128)S(1)} %pad_maximum_fusion.5, ...), channel_id=1, replica_groups=mesh['dp'=8,'tensor'=4] {'dp'}, use_global_device_ids=true, to_apply=%region_68.70 | all-reduce | flops 11848 | bytes 94784 | tf_op jit(solution)/shard_map/psum | solution.py:277
  1402.2 10.0 scatter_fusion
  1412.2 74.0 %reduce-scatter.17.cloned.1.call-done = bf16[2,192,768]{2,1,0:T(8,128)(2,1)} async-done(((bf16[2,1536,768]{2,1,0:T(8,128)(2,1)}), bf16[2,192,768]{2,1,0:T(8,128)(2,1)}) %reduce-scatter.17.cloned.1.call-update) | async-done | bytes 589840 | tf_op jit(solution)/shard_map/reduce_scatter | solution.py:270
  1488.4 97.0 %reduce-scatter.13.cloned.1.call-done = bf16[2,192,768]{2,1,0:T(8,128)(2,1)} async-done(((bf16[2,1536,768]{2,1,0:T(8,128)(2,1)}), bf16[2,192,768]{2,1,0:T(8,128)(2,1)}) %reduce-scatter.13.cloned.1.call-update) | async-done | bytes 589840 | tf_op jit(solution)/shard_map/reduce_scatter | solution.py:261
  1587.5 96.8 %reduce-scatter.11.cloned.1.call-done = bf16[2,192,768]{2,1,0:T(8,128)(2,1)} async-done(((bf16[2,1536,768]{2,1,0:T(8,128)(2,1)}), bf16[2,192,768]{2,1,0:T(8,128)(2,1)}) %reduce-scatter.11.cloned.1.call-update) | async-done | bytes 589840 | tf_op jit(solution)/shard_map/reduce_scatter | solution.py:258
  (852 shorter events, 394.3 us)
Async XLA Ops:
  15.4 15.1 copy-start.185
  15.5 15.7 copy-start.247
  15.5 15.7 copy-start.263
  15.5 16.2 copy-start.205
  15.5 16.9 copy-start.111
  15.5 78.1 %all-to-all-start = ((bf16[8,128,1536]{2,1,0:T(8,128)(2,1)}), bf16[8,128,1536]{2,1,0:T(8,128)(2,1)S(1)}, u32[]{:S(2)}, u32[]{:S(2)}) async-start(bf16[8,128,1536]{2,1,0:T(8,128)(2,1)} %broadcast_select_fusion), calls=%async_computation | async-start | bytes 6291456 | tf_op jit(solution)/shard_map/all_to_all | solution.py:148
  22.9 284.3 %all-reduce.69.cloned.1.call-start = ((), (), s32[]{:S(2)}) async-start(), calls=%async_computation.8 | async-start | bytes 12582912 | tf_op jit(solution)/shard_map/psum | solution.py:178
  30.5 65.8 %copy-start.120 = (f32[1536]{0:T(1024)}, f32[1536]{0:T(1024)S(1)}, u32[]{:S(2)}) copy-start(f32[1536]{0:T(1024)S(1)} %get-tuple-element.210) | copy-start | bytes 18436
  30.5 280.7 %copy-start.122 = (f32[1536]{0:T(1024)}, f32[1536]{0:T(1024)S(1)}, u32[]{:S(2)}) copy-start(f32[1536]{0:T(1024)S(1)} %get-tuple-element.211) | copy-start | bytes 18436
  31.7 64.6 %copy-start.222 = (f32[12]{0:T(128)}, f32[12]{0:T(128)S(1)}, u32[]{:S(2)}) copy-start(f32[12]{0:T(128)S(1)} %get-tuple-element.344) | copy-start | bytes 148
  32.5 63.8 %copy-start.105 = (bf16[1,1536,12]{1,0,2:T(2,128)(2,1)}, bf16[1,1536,12]{1,0,2:T(2,128)(2,1)S(1)}, u32[]{:S(2)}) copy-start(bf16[1,1536,12]{1,0,2:T(2,128)(2,1)S(1)} %get-tuple-element.295) | copy-start | bytes 110596
  32.5 283.4 %copy-start.107 = (bf16[1,1536,12]{1,0,2:T(2,128)(2,1)}, bf16[1,1536,12]{1,0,2:T(2,128)(2,1)S(1)}, u32[]{:S(2)}) copy-start(bf16[1,1536,12]{1,0,2:T(2,128)(2,1)S(1)} %get-tuple-element.294) | copy-start | bytes 110596
  93.6 213.6 %copy-start.3 = (bf16[8,128,1536]{2,1,0:T(8,128)(2,1)}, bf16[8,128,1536]{2,1,0:T(8,128)(2,1)S(1)}, u32[]{:S(2)}) copy-start(bf16[8,128,1536]{2,1,0:T(8,128)(2,1)S(1)} %all-to-all-done) | copy-start | bytes 9437188
  103.6 27.6 %copy-start.97 = (f32[4,256,12]{1,2,0:T(8,128)}, f32[4,256,12]{1,2,0:T(8,128)S(1)}, u32[]{:S(2)}) copy-start(f32[4,256,12]{1,2,0:T(8,128)S(1)} %copy.740) | copy-start | bytes 147460
  163.4 16.7 copy-start.160
  188.1 337.5 %all-reduce.71.cloned.1.call-start = ((), (), s32[]{:S(2)}) async-start(), calls=%async_computation.9 | async-start | bytes 12582912 | tf_op jit(solution)/shard_map/psum | solution.py:178
  313.9 68.2 %copy-start.10 = (bf16[1024,1536]{1,0:T(8,128)(2,1)}, bf16[1024,1536]{1,0:T(8,128)(2,1)S(1)}, u32[]{:S(2)}) copy-start(bf16[1024,1536]{1,0:T(8,128)(2,1)S(1)} %multiply_convert_fusion.2) | copy-start | bytes 9437188
  330.4 19.9 %copy-start.100 = (f32[4,256,12]{1,2,0:T(8,128)}, f32[4,256,12]{1,2,0:T(8,128)S(1)}, u32[]{:S(2)}) copy-start(f32[4,256,12]{1,2,0:T(8,128)S(1)} %copy.759) | copy-start | bytes 147460
  405.5 297.4 %all-reduce.75.cloned.1.call-start = ((), (), s32[]{:S(2)}) async-start(), calls=%async_computation.11 | async-start | bytes 1048576 | tf_op jit(solution)/shard_map/psum | solution.py:208
  571.6 15.5 copy-start.55
  583.5 30.3 %copy-start.65 = (f32[1,1,12,64,128]{4,3,2,1,0:T(8,128)}, f32[1,1,12,64,128]{4,3,2,1,0:T(8,128)S(1)}, u32[]{:S(2)}) copy-start(f32[1,1,12,64,128]{4,3,2,1,0:T(8,128)S(1)} %get-tuple-element.239) | copy-start | bytes 1179652
  583.5 30.2 %copy-start.66 = (f32[1,1,12,64,128]{4,3,2,1,0:T(8,128)}, f32[1,1,12,64,128]{4,3,2,1,0:T(8,128)S(1)}, u32[]{:S(2)}) copy-start(f32[1,1,12,64,128]{4,3,2,1,0:T(8,128)S(1)} %get-tuple-element.279) | copy-start | bytes 1179652
  592.6 19.3 %copy-start.32 = (f32[1,1024,128]{2,1,0:T(8,128)S(1)}, f32[1,1024,128]{2,1,0:T(8,128)}, u32[]{:S(2)}) copy-start(f32[1,1024,128]{2,1,0:T(8,128)} %get-tuple-element.288) | copy-start | bytes 1572868
  625.3 192.4 %all-reduce.73.cloned.1.call-start = ((), (), s32[]{:S(2)}) async-start(), calls=%async_computation.10 | async-start | bytes 12582912 | tf_op jit(solution)/shard_map/psum | solution.py:224
  663.9 30.0 %copy-start.109 = (bf16[1,1024,12]{1,2,0:T(8,128)(2,1)}, bf16[1,1024,12]{1,2,0:T(8,128)(2,1)S(1)}, u32[]{:S(2)}) copy-start(bf16[1,1024,12]{1,2,0:T(8,128)(2,1)S(1)} %get-tuple-element.229) | copy-start | bytes 73732
  697.6 120.2 %copy-start.123 = (f32[1536]{0:T(1024)S(1)}, f32[1536]{0:T(1024)}, u32[]{:S(2)}) copy-start(f32[1536]{0:T(1024)} %copy-done.122) | copy-start | bytes 18436
  697.6 120.1 %copy-start.130 = (f32[1024]{0:T(1024)S(1)}, f32[1024]{0:T(1024)}, u32[]{:S(2)}) copy-start(f32[1024]{0:T(1024)} %copy-done.129) | copy-start | bytes 12292
  697.6 327.8 %all-reduce.79.cloned.1.call-start = ((), (), s32[]{:S(2)}) async-start(), calls=%async_computation.13 | async-start | bytes 1048576 | tf_op jit(solution)/shard_map/psum | solution.py:208
  702.9 122.5 %copy-start.127 = (f32[1536]{0:T(1024)S(1)}, f32[1536]{0:T(1024)}, u32[]{:S(2)}) copy-start(f32[1536]{0:T(1024)} %get-tuple-element.209) | copy-start | bytes 18436
  702.9 122.5 %copy-start.159 = (f32[1024]{0:T(1024)S(1)}, f32[1024]{0:T(1024)}, u32[]{:S(2)}) copy-start(f32[1024]{0:T(1024)} %copy-done.158) | copy-start | bytes 12292
  702.9 122.5 %copy-start.196 = (f32[1024]{0:T(1024)S(1)}, f32[1024]{0:T(1024)}, u32[]{:S(2)}) copy-start(f32[1024]{0:T(1024)} %copy-done.195) | copy-start | bytes 12292
  833.7 14.5 copy-start.177
  875.5 34.1 %copy-start.61 = (f32[1,1,12,64,128]{4,3,2,1,0:T(8,128)}, f32[1,1,12,64,128]{4,3,2,1,0:T(8,128)S(1)}, u32[]{:S(2)}) copy-start(f32[1,1,12,64,128]{4,3,2,1,0:T(8,128)S(1)} %get-tuple-element.235) | copy-start | bytes 1179652
  875.5 34.1 %copy-start.63 = (f32[1,1,12,64,128]{4,3,2,1,0:T(8,128)}, f32[1,1,12,64,128]{4,3,2,1,0:T(8,128)S(1)}, u32[]{:S(2)}) copy-start(f32[1,1,12,64,128]{4,3,2,1,0:T(8,128)S(1)} %get-tuple-element.278) | copy-start | bytes 1179652
  890.8 18.8 %copy-start.31 = (f32[1,1024,128]{2,1,0:T(8,128)S(1)}, f32[1,1024,128]{2,1,0:T(8,128)}, u32[]{:S(2)}) copy-start(f32[1,1024,128]{2,1,0:T(8,128)} %get-tuple-element.290) | copy-start | bytes 1572868
  890.9 18.8 %copy-start.44 = (f32[1,4,256,12,64]{2,1,4,3,0:T(4,128)S(1)}, f32[1,4,256,12,64]{2,1,4,3,0:T(4,128)}, u32[]{:S(2)}) copy-start(f32[1,4,256,12,64]{2,1,4,3,0:T(4,128)} %reshape.1885) | copy-start | bytes 9437188
  991.7 155.6 %all-reduce.77.cloned.1.call-start = ((), (), s32[]{:S(2)}) async-start(), calls=%async_computation.12 | async-start | bytes 12582912 | tf_op jit(solution)/shard_map/psum | solution.py:224
  1013.6 366.1 %reduce-scatter.21.cloned.1.call-start = ((), (), s32[]{:S(2)}) async-start(), calls=%async_computation.19 | async-start | bytes 442368
  1020.8 126.4 %copy-start.4 = (bf16[8,128,1536]{2,1,0:T(8,128)(2,1)S(1)}, bf16[8,128,1536]{2,1,0:T(8,128)(2,1)}, u32[]{:S(2)}) copy-start(bf16[8,128,1536]{2,1,0:T(8,128)(2,1)} %copy-done.3) | copy-start | bytes 9437188
  1020.9 126.4 %copy-start.121 = (f32[1536]{0:T(1024)S(1)}, f32[1536]{0:T(1024)}, u32[]{:S(2)}) copy-start(f32[1536]{0:T(1024)} %copy-done.120) | copy-start | bytes 18436
  1020.9 126.4 %copy-start.142 = (f32[1024]{0:T(1024)S(1)}, f32[1024]{0:T(1024)}, u32[]{:S(2)}) copy-start(f32[1024]{0:T(1024)} %get-tuple-element.316) | copy-start | bytes 12292
  1020.9 360.4 %reduce-scatter.19.cloned.1.call-start = ((), (), s32[]{:S(2)}) async-start(), calls=%async_computation.18 | async-start | bytes 442368
  1156.2 231.7 %reduce-scatter.15.cloned.1.call-start = ((), (), s32[]{:S(2)}) async-start(), calls=%async_computation.16 | async-start | bytes 1769472 | tf_op jit(solution)/shard_map/reduce_scatter | solution.py:264
  1158.9 327.3 %reduce-scatter.17.cloned.1.call-start = ((), (), s32[]{:S(2)}) async-start(), calls=%async_computation.17 | async-start | bytes 5308416 | tf_op jit(solution)/shard_map/reduce_scatter | solution.py:270
  1176.3 409.1 %reduce-scatter.13.cloned.1.call-start = ((), (), s32[]{:S(2)}) async-start(), calls=%async_computation.15 | async-start | bytes 5308416 | tf_op jit(solution)/shard_map/reduce_scatter | solution.py:261
  1187.1 497.2 %reduce-scatter.11.cloned.1.call-start = ((), (), s32[]{:S(2)}) async-start(), calls=%async_computation.14 | async-start | bytes 5308416 | tf_op jit(solution)/shard_map/reduce_scatter | solution.py:258
  1264.4 125.1 %all-to-all-start.1 = ((bf16[8,2,98304]{2,1,0:T(2,128)(2,1)}), bf16[8,2,98304]{2,1,0:T(2,128)(2,1)S(1)}, u32[]{:S(2)}, u32[]{:S(2)}) async-start(bf16[8,2,98304]{2,1,0:T(2,128)(2,1)} %reshape.1976), calls=%async_computation.1 | async-start | bytes 6291456 | tf_op jit(solution)/shard_map/all_to_all | solution.py:282
  1402.2 284.3 %copy-start.1 = (bf16[8,128,1536]{2,1,0:T(8,128)(2,1)S(1)}, bf16[8,128,1536]{2,1,0:T(8,128)(2,1)}, u32[]{:S(2)}) copy-start(bf16[8,128,1536]{2,1,0:T(8,128)(2,1)} %param.17) | copy-start | bytes 9437188
  (240 other events, 1303.0 us)
Sparse Core Ops, SparseCore 0:
  188.3 118.9 all-reduce.68
  405.6 119.9 all-reduce.70
  625.4 33.5 all-reduce.74
  697.7 119.9 all-reduce.72
  991.8 33.5 all-reduce.78
  1027.6 119.5 all-reduce.76
  1151.1 61.5 reduce-scatter.20
  1216.5 60.6 reduce-scatter.18
  1280.6 107.2 reduce-scatter.14
  1391.8 94.3 reduce-scatter.16
  1490.3 94.9 reduce-scatter.12
  1589.3 94.9 reduce-scatter.10
where the time goes:
time: 1700 us; the launch traced here: 1690 us
  waiting for transfers between devices  805 us (47%)
  matrix products  299 us (18%)
  local copies, waits for them, and re-layouts  228 us (13%)
  other arithmetic  195 us (11%)
  blocking collectives  132 us (8%)
  between operations  20.9 us (1%)
    psum x2, waiting for transfers between devices, per_device(): branch = lax.psum(partial_value, 'tensor')  233 us
    psum x2, waiting for transfers between devices, per_device(): lax.psum(head_terms, 'tensor')  233 us
    psum x1, blocking collectives, per_device(): lax.psum((small_all[0], small_all[1], small_all[2], small_all[3], small_a...  101 us
    reduce_scatter x1, waiting for transfers between devices, per_device(): lax.psum_scatter(big_all[1].astype(jnp.bfloat16), 'dp', scatter_dimension...  97 us
    reduce_scatter x1, waiting for transfers between devices, per_device(): lax.psum_scatter(big_all[0].astype(jnp.bfloat16), 'dp', scatter_dimension...  96.8 us
    dot_general x6, matrix products, block_scan(): jnp.einsum('cijh,cjhp->cihp', scores[..., None] * weights, scaled_x, prec...  86 us
    reduce_scatter x1, waiting for transfers between devices, per_device(): lax.psum_scatter(big_all[4].astype(jnp.bfloat16), 'dp', scatter_dimension...  74 us
    all_to_all x1, waiting for transfers between devices, per_device(): lax.all_to_all(jnp.take(x_in, deal_order, axis=0), 'dp', split_axis=0, co...  61.1 us
  transfers between devices with their start and end apart: 14, of which 10 were waited for; matrix products, arithmetic and copies ran while one was open for 16% of the time, Pallas kernels for 0%

commit v1 on v0

v1 whole, which is shorter than its diff:
```python
import functools

import jax
import jax.numpy as jnp
from jax import lax
from jax.experimental import pallas as pl
from jax.experimental.pallas import tpu as pltpu
from jax.sharding import PartitionSpec as P

P_SIZE = 64
Q = 256
GC = 256
HG = GC // P_SIZE
LANES = 128
EPS = 1e-05
CHUNKS_F = 1
CHUNKS_B = 1
VMEM_LIMIT = 56 * 1024 * 1024

F32 = jnp.float32
BF16 = jnp.bfloat16


def nn(a, b):
    return jnp.dot(a, b, preferred_element_type=F32)


def nt(a, b):
    return lax.dot_general(a, b, (((1,), (1,)), ((), ())), preferred_element_type=F32)


def tn(a, b):
    return lax.dot_general(a, b, (((0,), (0,)), ((), ())), preferred_element_type=F32)


def exact(a, b):
    return jnp.dot(a, b, preferred_element_type=F32, precision=lax.Precision.HIGHEST)


def sigmoid(v):
    return 1.0 / (1.0 + jnp.exp(-v))


def softplus(v):
    return jnp.maximum(v, 0.0) + jnp.log1p(jnp.exp(-jnp.abs(v)))


def triangle(lower):
    rows = lax.broadcasted_iota(jnp.int32, (Q, Q), 0)
    cols = lax.broadcasted_iota(jnp.int32, (Q, Q), 1)
    return rows >= cols if lower else cols >= rows


def row_mean(v):
    return jnp.mean(v, axis=1, keepdims=True)


def col_sum(v):
    return jnp.sum(v, axis=0, keepdims=True)


def join_halves(dst, mine, theirs, core, half):
    width = mine.shape[-1]
    for m in range(Q // (2 * half)):
        own = pl.multiple_of(2 * half * m + half * core, 8)
        other = pl.multiple_of(2 * half * m + half * (1 - core), 8)
        dst[pl.ds(own, half), :width] = mine[half * m : half * m + half, :].astype(F32)
        dst[pl.ds(other, half), :width] = theirs[half * m : half * m + half, :].astype(F32)


def split_halves(src, keep, send, core, half):
    width = keep.shape[-1]
    for m in range(Q // (2 * half)):
        own = pl.multiple_of(2 * half * m + half * core, 8)
        keep[half * m : half * m + half, :] = src[pl.ds(own, half), :width].astype(keep.dtype)
        if send is not None:
            other = pl.multiple_of(2 * half * m + half * (1 - core), 8)
            send[half * m : half * m + half, :] = src[pl.ds(other, half), :width].astype(send.dtype)


def spread(per_head):
    lane = lax.broadcasted_iota(jnp.int32, (Q, LANES), 1)
    tiles = []
    for q in range(GC // LANES):
        left = jnp.broadcast_to(per_head[:, 2 * q : 2 * q + 1], (Q, LANES))
        right = jnp.broadcast_to(per_head[:, 2 * q + 1 : 2 * q + 2], (Q, LANES))
        tiles.append(jnp.where(lane < P_SIZE, left, right))
    return jnp.concatenate(tiles, axis=1)


def head_part(tile, parity):
    lane = lax.broadcasted_iota(jnp.int32, tile.shape, 1)
    return jnp.where((lane < P_SIZE) == (parity == 0), tile, jnp.zeros_like(tile))


def gather_heads(acc, cols, group):
    lane = lax.broadcasted_iota(jnp.int32, (cols.shape[0], LANES), 1)
    for j in range(HG):
        tile = head_part(cols[:, (j // 2) * LANES : (j // 2 + 1) * LANES], j % 2)
        total = jnp.sum(tile, axis=1, keepdims=True)
        acc = acc + jnp.where(lane == group * HG + j, total, 0.0)
    return acc


def conv_rows(buf, taps):
    out = taps[4:5, :] + taps[0:1, :] * buf[5 : 5 + Q, :]
    for k in range(1, 4):
        out = out + taps[k : k + 1, :] * buf[5 + k : 5 + k + Q, :]
    return out


def forward_kernel(first_layer, half, base, inner, scal, *refs):
    it = iter(refs)
    if first_layer:
        mine, theirs = next(it), next(it)
    else:
        hid_prev, mine, theirs = next(it), next(it), next(it)
    gain, w_gate, w_value, w_state, w_step, w_out = (next(it) for _ in range(6))
    taps_v, taps_s, bias, decay_log, skip, gain_in = (next(it) for _ in range(6))
    h_in, vt_in, st_in = (next(it) for _ in range(3))
    if not first_layer:
        hid_out = next(it)
    low_out, gate_out, vin_out, cv_out, y_out, sin_out, cs_out, dt_out, hs_out = (
        next(it) for _ in range(9)
    )
    h_last, vt_last, st_last, keep, send = (next(it) for _ in range(5))
    buf, acc, sq, vbuf, sbuf, b_s, c_s, bt_s, s_s, step_s, cum_s, cumt_s = (
        next(it) for _ in range(12)
    )

    i, g = pl.program_id(0), pl.program_id(1)
    core = scal[0]
    width = low_out.shape[1]

    @pl.when(g == 0)
    def _():
        @pl.when(i == 0)
        def _():
            h_last[...] = h_in[...]
            vt_last[...] = vt_in[...]
            st_last[...] = st_in[...]

        join_halves(buf, mine, theirs, core, half)
        if first_layer:
            token = base + i * Q + lax.broadcasted_iota(jnp.int32, (Q, 1), 0)
            hid = jnp.where(token < scal[1], buf[:, :width], 0.0)
        else:
            total = buf[:, width : width + 1] + buf[:, width + P_SIZE : width + P_SIZE + 1]
            hid = hid_prev[...] + lax.rsqrt(total / inner + EPS) * buf[:, :width]
            hid_out[...] = hid
        low_out[...] = (hid * lax.rsqrt(row_mean(hid * hid) + EPS) * gain[...]).astype(BF16)
        low = low_out[...]
        s_in = nn(low, w_state[...])
        sin_out[...] = s_in.astype(BF16)
        sbuf[0:8, :] = st_last[...]
        sbuf[8 : 8 + Q, :] = s_in
        st_last[...] = s_in[Q - 8 : Q, :]
        cs = conv_rows(sbuf, taps_s)
        cs_out[...] = cs
        states = cs * sigmoid(cs)
        b_val, c_val = states[:, :LANES], states[:, LANES:]
        b_s[...] = b_val.astype(BF16)
        c_s[...] = c_val.astype(BF16)
        bt_s[...] = b_val.T.astype(BF16)
        s_s[...] = nt(c_s[...], b_s[...])
        dt = nn(low, w_step[...])
        dt_out[...] = dt
        step = softplus(dt + bias[...])
        cum = -exact(triangle(True).astype(F32), step * jnp.exp(decay_log[...]))
        step_s[...] = step
        cum_s[...] = cum
        cumt_s[...] = cum.T
        acc[...] = jnp.zeros_like(acc)
        sq[...] = jnp.zeros_like(sq)

    low = low_out[...]
    gate = nn(low, w_gate[...])
    gate_out[...] = gate
    v_in = nn(low, w_value[...])
    vin_out[...] = v_in.astype(BF16)
    vbuf[0:8, :] = vt_last[g]
    vbuf[8 : 8 + Q, :] = v_in
    vt_last[g] = v_in[Q - 8 : Q, :]
    cv = conv_rows(vbuf, taps_v)
    cv_out[...] = cv
    val = cv * sigmoid(cv)
    cum_g = pltpu.roll(cum_s[...], lax.rem(LANES - g * HG, LANES), 1)
    step_g = pltpu.roll(step_s[...], lax.rem(LANES - g * HG, LANES), 1)
    cum_e = spread(cum_g)
    scaled = spread(step_g) * val
    scaled_b = scaled.astype(BF16)
    h_enter = h_last[g]
    hs_out[...] = h_enter
    y = nn(c_s[...], h_enter.astype(BF16)) * jnp.exp(cum_e)
    end = cum_e[Q - 1 : Q, :]
    to_end = (scaled * jnp.exp(end - cum_e)).astype(BF16)
    h_last[g] = h_enter * jnp.exp(end) + nn(bt_s[...], to_end)
    causal = triangle(True)
    tiles = []
    for q in range(GC // LANES):
        tile = jnp.zeros((Q, LANES), F32)
        for parity in range(2):
            j = 2 * q + parity
            gaps = cum_g[:, j : j + 1] - cumt_s[pl.ds(g * HG + j, 1), :]
            weights = jnp.exp(jnp.where(causal, gaps, -1e30))
            mix = (s_s[...] * weights).astype(BF16)
            tile = tile + nn(mix, head_part(scaled_b[:, q * LANES : (q + 1) * LANES], parity))
        tiles.append(tile)
    y = y + jnp.concatenate(tiles, axis=1)
    y_out[...] = y
    gated = (y + skip[...] * val) * (gate * sigmoid(gate))
    sq[...] += jnp.sum(gated * gated, axis=1, keepdims=True)
    acc[:, :width] += nt((gated * gain_in[...]).astype(BF16), w_out[...])

    @pl.when(g == pl.num_programs(1) - 1)
    def _():
        acc[:, width:] = jnp.broadcast_to(sq[:, 0:1], (Q, LANES))
        split_halves(acc, keep, send, core, half)


def backward_kernel(top, bottom, half, base, inner, scal, *refs):
    it = iter(refs)
    if top:
        hid_ref, cot = next(it), next(it)
    else:
        hid_ref, dh_prev, dl_mine, dl_theirs = (next(it) for _ in range(4))
    br_mine, br_theirs, gain = (next(it) for _ in range(3))
    w_gate, w_value, w_state, w_step, w_out = (next(it) for _ in range(5))
    taps_v, taps_s, bias, decay_log, skip, gain_in = (next(it) for _ in range(6))
    gate_ref, vin_ref, cv_ref, y_ref, sin_ref, cs_ref, dt_ref, hs_ref = (next(it) for _ in range(8))
    dh_c, av_c, as_c, ah_c, ag_c = (next(it) for _ in range(5))
    if top:
        result = next(it)
    dh_out, gb_out, go_out, dgate_out, dval_out, dst_out, dstep_out = (next(it) for _ in range(7))
    keep, send = next(it), next(it)
    d_state, acc_v, acc_s, acc_h, acc_g = (next(it) for _ in range(5))
    buf, acc, dst_s, db_s, dc_s, vbuf, sbuf = (next(it) for _ in range(7))
    b_s, c_s, ct_s, st_s, step_s, cum_s, cumt_s, rows_s, dcum_s, dstep_s, end_s = (
        next(it) for _ in range(11)
    )

    i, g = pl.program_id(0), pl.program_id(1)
    core = scal[0]
    width = gb_out.shape[1]

    @pl.when(g == 0)
    def _():
        @pl.when(i == 0)
        def _():
            d_state[...] = dh_c[...]
            acc_v[...] = av_c[...]
            acc_s[...] = as_c[...]
            acc_h[...] = ah_c[...]
            acc_g[...] = ag_c[...]

        if not top:
            join_halves(acc, dl_mine, dl_theirs, core, half)
        join_halves(buf, br_mine, br_theirs, core, half)
        total = buf[:, width : width + 1] + buf[:, width + P_SIZE : width + P_SIZE + 1]
        scale = lax.rsqrt(total / inner + EPS)
        if top:
            hid = hid_ref[...] + scale * buf[:, :width]
        else:
            hid = hid_ref[...]
        r = lax.rsqrt(row_mean(hid * hid) + EPS)
        normed = hid * r
        if top:
            token = base + (pl.num_programs(0) - 1 - i) * Q + lax.broadcasted_iota(jnp.int32, (Q, 1), 0)
            valid = token < scal[1]
            result[...] = jnp.where(valid, normed * gain[...], 0.0).astype(BF16)
            upper = jnp.where(valid, cot[...].astype(F32), 0.0)
        else:
            upper = acc[...]
        acc_g[0:1, :] += col_sum(upper * normed)
        dn = upper * gain[...]
        dh = r * (dn - normed * row_mean(dn * normed))
        if not top:
            dh = dh + dh_prev[...]
        gb = dh.astype(BF16)
        gb_out[...] = gb
        stat = jnp.sum(gb.astype(F32) * buf[:, :width], axis=1, keepdims=True)
        rows_s[:, 0:1] = scale
        rows_s[:, 1:2] = scale * scale * scale * stat / inner
        if bottom:
            acc[...] = dh
            split_halves(acc, dh_out, None, core, half)
        else:
            dh_out[...] = dh

        cs = cs_ref[...]
        states = cs * sigmoid(cs)
        b_val, c_val = states[:, :LANES], states[:, LANES:]
        b_s[...] = b_val.astype(BF16)
        c_s[...] = c_val.astype(BF16)
        ct_s[...] = c_val.T.astype(BF16)
        st_s[...] = nt(b_s[...], c_s[...])
        step = softplus(dt_ref[...] + bias[...])
        cum = -exact(triangle(True).astype(F32), step * jnp.exp(decay_log[...]))
        step_s[...] = step
        cum_s[...] = cum
        cumt_s[...] = cum.T
        acc[...] = jnp.zeros_like(acc)
        dst_s[...] = jnp.zeros_like(dst_s)
        db_s[...] = jnp.zeros_like(db_s)
        dc_s[...] = jnp.zeros_like(dc_s)
        dcum_s[...] = jnp.zeros_like(dcum_s)
        dstep_s[...] = jnp.zeros_like(dstep_s)
        end_s[...] = jnp.zeros_like(end_s)

    scale, coef = rows_s[:, 0:1], rows_s[:, 1:2]
    d_go = nn(gb_out[...], w_out[...])
    cv = cv_ref[...]
    sig_v = sigmoid(cv)
    val = cv * sig_v
    gate = gate_ref[...]
    sig_g = sigmoid(gate)
    silu_g = gate * sig_g
    y = y_ref[...]
    mixed = y + skip[...] * val
    gated = mixed * silu_g
    normed_gate = gated * scale
    acc_v[g, 5:6, :] += col_sum(d_go * normed_gate)
    go_out[...] = (normed_gate * gain_in[...]).astype(BF16)
    d_gated = scale * (d_go * gain_in[...]) - gated * coef
    d_gate = (d_gated * mixed * (sig_g * (1.0 + gate * (1.0 - sig_g)))).astype(BF16)
    dgate_out[...] = d_gate
    d_y = d_gated * silu_g
    acc_v[g, 6:7, :] += col_sum(d_y * val)
    d_y_b = d_y.astype(BF16)
    d_y_r = d_y_b.astype(F32)

    cum_g = pltpu.roll(cum_s[...], lax.rem(LANES - g * HG, LANES), 1)
    step_g = pltpu.roll(step_s[...], lax.rem(LANES - g * HG, LANES), 1)
    cum_e = spread(cum_g)
    step_e = spread(step_g)
    scaled = step_e * val
    scaled_b = scaled.astype(BF16)
    scaled_r = scaled_b.astype(F32)
    causal_t = triangle(False)
    tiles = []
    for q in range(GC // LANES):
        tile = jnp.zeros((Q, LANES), F32)
        x_tile = scaled_b[:, q * LANES : (q + 1) * LANES]
        g_tile = d_y_b[:, q * LANES : (q + 1) * LANES]
        for parity in range(2):
            j = 2 * q + parity
            gaps = cumt_s[pl.ds(g * HG + j, 1), :] - cum_g[:, j : j + 1]
            weights = jnp.exp(jnp.where(causal_t, gaps, -1e30))
            mix = (st_s[...] * weights).astype(BF16)
            part = head_part(g_tile, parity)
            tile = tile + nn(mix, part)
            dst_s[...] += nt(x_tile, part) * weights
        tiles.append(tile)
    d_x = jnp.concatenate(tiles, axis=1)
    end = cum_e[Q - 1 : Q, :]
    exp_end = jnp.exp(end)
    to_end = jnp.exp(end - cum_e)
    h_enter = hs_ref[...]
    d_out = d_state[g]
    d_out_b = d_out.astype(BF16)
    d_across = (d_y * jnp.exp(cum_e)).astype(BF16)
    dc_s[...] += nt(d_across, h_enter.astype(BF16))
    db_s[...] += nt((scaled * to_end).astype(BF16), d_out_b)
    d_x_end = to_end * nn(b_s[...], d_out_b)
    d_state[g] = nn(ct_s[...], d_across) + exp_end * d_out
    end_s[...] = gather_heads(
        end_s[...],
        jnp.broadcast_to(col_sum(scaled_r * d_x_end) + exp_end * col_sum(h_enter * d_out), (8, GC)),
        g,
    )
    d_x = d_x + d_x_end
    dcum_s[...] = gather_heads(dcum_s[...], d_y_r * y - scaled_r * d_x, g)
    dstep_s[...] = gather_heads(dstep_s[...], val * d_x, g)
    d_val = skip[...] * d_y + step_e * d_x
    d_cv = d_val * (sig_v * (1.0 + cv * (1.0 - sig_v)))
    vbuf[0:Q, :] = d_cv
    vbuf[Q : Q + 8, :] = acc_v[g, 8:16, :]
    acc_v[g, 8:16, :] = d_cv[0:8, :]
    v_in = vin_ref[...].astype(F32)
    d_vin = taps_v[3:4, :] * d_cv
    acc_v[g, 3:4, :] += col_sum(v_in * d_cv)
    acc_v[g, 4:5, :] += col_sum(d_cv)
    for k in range(3):
        shifted = vbuf[3 - k : 3 - k + Q, :]
        d_vin = d_vin + taps_v[k : k + 1, :] * shifted
        acc_v[g, k : k + 1, :] += col_sum(v_in * shifted)
    d_vin_b = d_vin.astype(BF16)
    dval_out[...] = d_vin_b
    acc[...] += nt(d_gate, w_gate[...]) + nt(d_vin_b, w_value[...])

    @pl.when(g == pl.num_programs(1) - 1)
    def _():
        decay = jnp.exp(decay_log[...])
        step = step_s[...]
        d_log = exact(triangle(False).astype(F32), dcum_s[...]) + end_s[0:1, :]
        acc_h[1:2, :] += col_sum(d_log * step) * (-decay)
        d_step = (dstep_s[...] - decay * d_log) * sigmoid(dt_ref[...] + bias[...])
        acc_h[0:1, :] += col_sum(d_step)
        d_step_b = d_step.astype(BF16)
        dstep_out[...] = d_step_b
        d_scores = dst_s[...]
        d_b = db_s[...] + nn(d_scores.astype(BF16), c_s[...])
        d_c = dc_s[...] + nn(d_scores.T.astype(BF16), b_s[...])
        cs = cs_ref[...]
        sig_s = sigmoid(cs)
        d_cs = jnp.concatenate([d_b, d_c], axis=1) * (sig_s * (1.0 + cs * (1.0 - sig_s)))
        sbuf[0:Q, :] = d_cs
        sbuf[Q : Q + 8, :] = acc_s[8:16, :]
        acc_s[8:16, :] = d_cs[0:8, :]
        s_in = sin_ref[...].astype(F32)
        d_sin = taps_s[3:4, :] * d_cs
        acc_s[3:4, :] += col_sum(s_in * d_cs)
        acc_s[4:5, :] += col_sum(d_cs)
        for k in range(3):
            shifted = sbuf[3 - k : 3 - k + Q, :]
            d_sin = d_sin + taps_s[k : k + 1, :] * shifted
            acc_s[k : k + 1, :] += col_sum(s_in * shifted)
        d_sin_b = d_sin.astype(BF16)
        dst_out[...] = d_sin_b
        acc[...] += nt(d_sin_b, w_state[...]) + nt(d_step_b, w_step[...])
        split_halves(acc, keep, send, core, half)


def layer_specs(l, width):
    return [
        pl.BlockSpec((None, width, GC), lambda i, g, l=l: (l, 0, g)),
        pl.BlockSpec((None, width, GC), lambda i, g, l=l: (l, 0, g)),
        pl.BlockSpec((None, width, 2 * LANES), lambda i, g, l=l: (l, 0, 0)),
        pl.BlockSpec((None, width, LANES), lambda i, g, l=l: (l, 0, 0)),
        pl.BlockSpec((None, width, GC), lambda i, g, l=l: (l, 0, g)),
        pl.BlockSpec((None, 5, GC), lambda i, g, l=l: (l, 0, g)),
        pl.BlockSpec((None, 5, 2 * LANES), lambda i, g, l=l: (l, 0, 0)),
        pl.BlockSpec((None, 1, LANES), lambda i, g, l=l: (l, 0, 0)),
        pl.BlockSpec((None, 1, LANES), lambda i, g, l=l: (l, 0, 0)),
        pl.BlockSpec((None, 1, GC), lambda i, g, l=l: (l, 0, g)),
        pl.BlockSpec((None, 1, GC), lambda i, g, l=l: (l, 0, g)),
    ]


def whole(shape):
    return pl.BlockSpec(shape, lambda i, g: (0,) * len(shape))


def shape(dims, dtype=F32):
    return jax.ShapeDtypeStruct(dims, dtype)


def forward_call(l, base, half, inner, scal, hid_prev, mine, theirs, gains, weights, carry):
    first = hid_prev is None
    width = weights[0].shape[1]
    groups = weights[0].shape[2] // GC
    cols = groups * GC
    rows = mine.shape[0] * 2
    chunks = rows // Q
    wide = mine.shape[1]

    def block(h, w):
        return pl.BlockSpec((h, w), lambda i, g: (i, 0))

    def grouped(h, w):
        return pl.BlockSpec((h, w), lambda i, g: (i, g))

    in_specs = [pl.BlockSpec(memory_space=pltpu.SMEM)]
    args = [scal]
    if not first:
        in_specs.append(block(Q, width))
        args.append(hid_prev)
    in_specs += [block(Q // 2, wide), block(Q // 2, wide)]
    args += [mine, theirs]
    in_specs.append(pl.BlockSpec((None, 1, width), lambda i, g, l=l: (l, 0, 0)))
    args.append(gains)
    in_specs += layer_specs(l, width)
    args += list(weights)
    carry_shapes = [(groups, LANES, GC), (groups, 8, GC), (8, 2 * LANES)]
    in_specs += [whole(s) for s in carry_shapes]
    args += list(carry)
    out_specs, out_shape = [], []
    if not first:
        out_specs.append(block(Q, width))
        out_shape.append(shape((rows, width)))
    out_specs += [
        block(Q, width),
        grouped(Q, GC),
        grouped(Q, GC),
        grouped(Q, GC),
        grouped(Q, GC),
        block(Q, 2 * LANES),
        block(Q, 2 * LANES),
        block(Q, LANES),
        pl.BlockSpec((None, None, LANES, GC), lambda i, g: (i, g, 0, 0)),
    ]
    out_shape += [
        shape((rows, width), BF16),
        shape((rows, cols)),
        shape((rows, cols), BF16),
        shape((rows, cols)),
        shape((rows, cols)),
        shape((rows, 2 * LANES), BF16),
        shape((rows, 2 * LANES)),
        shape((rows, LANES)),
        shape((chunks, groups, LANES, GC)),
    ]
    out_specs += [whole(s) for s in carry_shapes]
    out_shape += [shape(s) for s in carry_shapes]
    out_specs += [block(Q // 2, width + LANES)] * 2
    out_shape += [shape((rows // 2, width + LANES))] * 2
    scratch = [
        pltpu.VMEM((Q, width + LANES), F32),
        pltpu.VMEM((Q, width + LANES), F32),
        pltpu.VMEM((Q, LANES), F32),
        pltpu.VMEM((Q + 8, GC), F32),
        pltpu.VMEM((Q + 8, 2 * LANES), F32),
        pltpu.VMEM((Q, LANES), BF16),
        pltpu.VMEM((Q, LANES), BF16),
        pltpu.VMEM((LANES, Q), BF16),
        pltpu.VMEM((Q, Q), F32),
        pltpu.VMEM((Q, LANES), F32),
        pltpu.VMEM((Q, LANES), F32),
        pltpu.VMEM((LANES, Q), F32),
    ]
    outs = pl.pallas_call(
        functools.partial(forward_kernel, first, half, base, inner),
        grid=(chunks, groups),
        in_specs=in_specs,
        out_specs=out_specs,
        out_shape=out_shape,
        scratch_shapes=scratch,
        compiler_params=pltpu.CompilerParams(
            dimension_semantics=("arbitrary", "arbitrary"), vmem_limit_bytes=VMEM_LIMIT
        ),
        cost_estimate=pl.CostEstimate(
            flops=rows * 14_000_000, bytes_accessed=20_000_000, transcendentals=rows * 4000
        ),
        name="layer_forward",
    )(*args)
    hid = None
    if not first:
        hid, outs = outs[0], outs[1:]
    return hid, outs[0], tuple(outs[1:9]), tuple(outs[9:12]), outs[12], outs[13]


def backward_call(l, top, bottom, base, half, inner, scal, lead, branch, gains, weights, saved, carry):
    width = weights[0].shape[1]
    groups = weights[0].shape[2] // GC
    cols = groups * GC
    rows = branch[0].shape[0] * 2
    chunks = rows // Q

    def block(h, w):
        return pl.BlockSpec((h, w), lambda i, g: (chunks - 1 - i, 0))

    def grouped(h, w):
        return pl.BlockSpec((h, w), lambda i, g: (chunks - 1 - i, g))

    in_specs = [pl.BlockSpec(memory_space=pltpu.SMEM)]
    if top:
        in_specs += [block(Q, width), block(Q, width)]
    else:
        in_specs += [block(Q, width), block(Q, width), block(Q // 2, width), block(Q // 2, width)]
    in_specs += [block(Q // 2, width + LANES)] * 2
    in_specs.append(pl.BlockSpec((None, 1, width), lambda i, g, l=l: (l + 1, 0, 0)))
    in_specs += layer_specs(l, width)
    in_specs += [
        grouped(Q, GC),
        grouped(Q, GC),
        grouped(Q, GC),
        grouped(Q, GC),
        block(Q, 2 * LANES),
        block(Q, 2 * LANES),
        block(Q, LANES),
        pl.BlockSpec((None, None, LANES, GC), lambda i, g: (chunks - 1 - i, g, 0, 0)),
    ]
    carry_shapes = [(groups, LANES, GC), (groups, 16, GC), (16, 2 * LANES), (8, LANES), (8, width)]
    in_specs += [whole(s) for s in carry_shapes]
    out_specs, out_shape = [], []
    if top:
        out_specs.append(block(Q, width))
        out_shape.append(shape((rows, width), BF16))
    dh_rows = Q // 2 if bottom else Q
    out_specs += [
        block(dh_rows, width),
        block(Q, width),
        grouped(Q, GC),
        grouped(Q, GC),
        grouped(Q, GC),
        block(Q, 2 * LANES),
        block(Q, LANES),
        block(Q // 2, width),
        block(Q // 2, width),
    ]
    out_shape += [
        shape((chunks * dh_rows, width)),
        shape((rows, width), BF16),
        shape((rows, cols), BF16),
        shape((rows, cols), BF16),
        shape((rows, cols), BF16),
        shape((rows, 2 * LANES), BF16),
        shape((rows, LANES), BF16),
        shape((rows // 2, width)),
        shape((rows // 2, width)),
    ]
    out_specs += [whole(s) for s in carry_shapes]
    out_shape += [shape(s) for s in carry_shapes]
    scratch = [
        pltpu.VMEM((Q, width + LANES), F32),
        pltpu.VMEM((Q, width), F32),
        pltpu.VMEM((Q, Q), F32),
        pltpu.VMEM((Q, LANES), F32),
        pltpu.VMEM((Q, LANES), F32),
        pltpu.VMEM((Q + 8, GC), F32),
        pltpu.VMEM((Q + 8, 2 * LANES), F32),
        pltpu.VMEM((Q, LANES), BF16),
        pltpu.VMEM((Q, LANES), BF16),
        pltpu.VMEM((LANES, Q), BF16),
        pltpu.VMEM((Q, Q), F32),
        pltpu.VMEM((Q, LANES), F32),
        pltpu.VMEM((Q, LANES), F32),
        pltpu.VMEM((LANES, Q), F32),
        pltpu.VMEM((Q, LANES), F32),
        pltpu.VMEM((Q, LANES), F32),
        pltpu.VMEM((Q, LANES), F32),
        pltpu.VMEM((8, LANES), F32),
    ]
    outs = pl.pallas_call(
        functools.partial(backward_kernel, top, bottom, half, base, inner),
        grid=(chunks, groups),
        in_specs=in_specs,
        out_specs=out_specs,
        out_shape=out_shape,
        scratch_shapes=scratch,
        compiler_params=pltpu.CompilerParams(
            dimension_semantics=("arbitrary", "arbitrary"), vmem_limit_bytes=VMEM_LIMIT
        ),
        cost_estimate=pl.CostEstimate(
            flops=rows * 20_000_000, bytes_accessed=25_000_000, transcendentals=rows * 4000
        ),
        name="layer_backward",
    )(scal, *lead, *branch, gains, *weights, *saved, *carry)
    result = None
    if top:
        result, outs = outs[0], outs[1:]
    dh, gb, go, dgate, dval, dst, dstep, keep, send = outs[:9]
    return result, dh, gb, go, (dgate, dval, dst, dstep), keep, send, tuple(outs[9:])


def pairs(axis, bit):
    return [(i, i ^ bit) for i in range(lax.axis_size(axis))]


def sum_pairs(value, axis, bit):
    return value + lax.ppermute(value, axis, pairs(axis, bit))


def two_terms(wide, width):
    main = wide[:, :width].astype(BF16)
    if wide.shape[1] == width:
        return main
    tail = wide[:, width:]
    lead = lax.reduce_precision(tail, 8, 7)
    lane = lax.broadcasted_iota(jnp.int32, tail.shape, 1)
    tail = jnp.where(lane < P_SIZE, lead, tail - lead).astype(BF16)
    return jnp.concatenate([main, tail], axis=1)


def sum_tensor_half(keep, send, width):
    chip = keep + lax.ppermute(send, "tensor", pairs("tensor", 1))
    own = lax.optimization_barrier(two_terms(chip, width))
    other = lax.ppermute(own, "tensor", pairs("tensor", 2))
    return own.astype(F32) + other.astype(F32)


def both_halves(half_rows):
    return half_rows, lax.ppermute(half_rows, "tensor", pairs("tensor", 1))


def pad_lanes(v):
    return jnp.pad(v, [(0, 0)] * (v.ndim - 1) + [(0, LANES - v.shape[-1])])


def per_device(
    x_in,
    cotangent,
    lengths,
    deal_order,
    norm_gains,
    proj_gate,
    proj_value,
    proj_state,
    proj_step,
    proj_out,
    conv_value,
    conv_state,
    step_bias,
    decay_log,
    skip_gain,
    inner_gain,
):
    _, slot_len, width = cotangent.shape
    layers = proj_gate.shape[0]
    cols = proj_gate.shape[2]
    heads = step_bias.shape[1]
    inner = cols * lax.axis_size("tensor")
    dp = lax.axis_size("dp")
    groups = cols // GC
    half = x_in.shape[1] // 2
    me = lax.axis_index("dp")
    core = lax.rem(lax.axis_index("tensor"), 2)
    length = jnp.take(lengths, lax.dynamic_index_in_dim(deal_order, me, keepdims=False))
    scal = jnp.stack([core, length]).astype(jnp.int32)

    x_half = lax.dynamic_slice_in_dim(x_in, core * half, half, axis=1)
    x_dealt = jnp.take(x_half, deal_order, axis=0)
    x_mine = lax.all_to_all(x_dealt, "dp", split_axis=0, concat_axis=0, tiled=True)
    x_mine = x_mine.reshape(slot_len // 2, width)
    x_mine, x_theirs = both_halves(x_mine)

    gains = norm_gains[:, None, :]
    weights = (
        proj_gate,
        proj_value,
        proj_state,
        pad_lanes(proj_step),
        proj_out,
        conv_value,
        conv_state,
        pad_lanes(step_bias)[:, None, :],
        pad_lanes(decay_log)[:, None, :],
        jnp.repeat(skip_gain, P_SIZE, axis=1)[:, None, :],
        inner_gain[:, None, :],
    )
    cot = cotangent.reshape(slot_len, width)

    rows_f = CHUNKS_F * Q
    calls_f = slot_len // rows_f
    hids, lows, saves, branches = [], [], [], []
    lead = [
        (None, x_mine[c * rows_f // 2 : (c + 1) * rows_f // 2], x_theirs[c * rows_f // 2 : (c + 1) * rows_f // 2])
        for c in range(calls_f)
    ]
    for l in range(layers):
        carry = (
            jnp.zeros((groups, LANES, GC), F32),
            jnp.zeros((groups, 8, GC), F32),
            jnp.zeros((8, 2 * LANES), F32),
        )
        hid_l, low_l, save_l, branch_l = [], [], [], []
        for c in range(calls_f):
            hid, low, saved, carry, keep, send = forward_call(
                l, c * rows_f, half, inner, scal, *lead[c], gains, weights, carry
            )
            hid_l.append(hid)
            low_l.append(low)
            save_l.append(saved)
            branch_l.append(both_halves(sum_tensor_half(keep, send, width)))
        hids.append(hid_l)
        lows.append(low_l)
        saves.append(save_l)
        branches.append(branch_l)
        if l == 0:
            lead = []
            for c in range(calls_f):
                token = c * rows_f + lax.broadcasted_iota(jnp.int32, (rows_f, 1), 0)
                x_rows = join_rows(x_mine, x_theirs, core, half, c * rows_f // 2, rows_f // 2)
                hid_l[c] = jnp.where(token < length, x_rows.astype(F32), 0.0)
        lead = [(hid_l[c], *branch_l[c]) for c in range(calls_f)]

    results = [None] * calls_f
    d_hids = [None] * calls_f
    d_lows = [None] * calls_f
    gain_grads, v_grads, s_grads, h_grads, scattered = [], [], [], [], []
    for l in reversed(range(layers)):
        top, bottom = l == layers - 1, l == 0
        carry = (
            jnp.zeros((groups, LANES, GC), F32),
            jnp.zeros((groups, 16, GC), F32),
            jnp.zeros((16, 2 * LANES), F32),
            jnp.zeros((8, LANES), F32),
            jnp.zeros((8, width), F32),
        )
        gbs, gos, ds = [None] * calls_f, [None] * calls_f, [None] * calls_f
        new_d_hids, new_d_lows = [None] * calls_f, [None] * calls_f
        for c in reversed(range(calls_f)):
            base = c * rows_f
            if top:
                first = (hids[l][c], cot[base : base + rows_f])
            else:
                first = (hids[l + 1][c], d_hids[c], *d_lows[c])
            result, dh, gb, go, d_in, keep, send, carry = backward_call(
                l, top, bottom, base, half, inner, scal, first, branches[l][c], gains, weights, saves[l][c], carry
            )
            if top:
                results[c] = result
            gbs[c], gos[c], ds[c] = gb, go, d_in
            new_d_hids[c] = dh
            summed = sum_tensor_half(keep, send, width)
            new_d_lows[c] = summed if bottom else both_halves(summed)
        d_hids, d_lows = new_d_hids, new_d_lows
        _, acc_v, acc_s, acc_h, acc_g = carry
        gain_grads.insert(0, acc_g[0])
        v_grads.insert(0, acc_v)
        s_grads.insert(0, acc_s[:5])
        h_grads.insert(0, acc_h[:2])
        low = jnp.concatenate(lows[l], axis=0)
        d_all = jnp.concatenate([jnp.concatenate(parts, axis=1) for parts in ds], axis=0)
        g_in = tn(low, d_all).astype(BF16)
        g_out = tn(jnp.concatenate(gbs, axis=0), jnp.concatenate(gos, axis=0)).astype(BF16)
        pieces = [g_out, g_in]
        scattered.insert(
            0, [lax.psum_scatter(p, "dp", scatter_dimension=0, tiled=True) for p in pieces]
        )

    d_low = jnp.concatenate(d_lows, axis=0)
    d_hid = jnp.concatenate(d_hids, axis=0)
    token = (
        lax.broadcasted_iota(jnp.int32, (dp, half, 1), 0) * (2 * half)
        + lax.broadcasted_iota(jnp.int32, (dp, half, 1), 1)
        + core * half
    ).reshape(slot_len // 2, 1)
    valid = (token < length).astype(F32)
    hid = x_mine.astype(F32) * valid
    r = lax.rsqrt(row_mean(hid * hid) + EPS)
    normed = hid * r
    gain_first = jnp.sum(d_low * normed, axis=0)
    dn = d_low * norm_gains[0]
    d_hid = d_hid + r * (dn - normed * row_mean(dn * normed))
    grad_in = (d_hid * valid).astype(BF16).reshape(dp, half, width)
    returned = lax.all_to_all(grad_in, "dp", split_axis=0, concat_axis=0, tiled=True)
    mine, theirs = both_halves(returned)
    grad_x = jnp.where(
        core == 0, jnp.concatenate([mine, theirs], axis=1), jnp.concatenate([theirs, mine], axis=1)
    )
    inverse = jnp.sum(
        jnp.where(deal_order[None, :] == jnp.arange(dp)[:, None], jnp.arange(dp)[None, :], 0), axis=1
    )
    grad_x = jnp.take(grad_x, inverse, axis=0)

    v_all = jnp.stack(v_grads)
    v_all = jnp.swapaxes(v_all, 1, 2).reshape(layers, 16, cols)
    s_all = jnp.stack(s_grads)
    h_all = jnp.stack(h_grads)
    gain_first = sum_pairs(gain_first, "tensor", 1)
    gain_all = jnp.stack([gain_first] + gain_grads)
    for bit in (1, 2):
        s_all = sum_pairs(s_all, "tensor", bit)
    small = jnp.concatenate(
        [v_all[:, :7].reshape(-1), s_all.reshape(-1), h_all.reshape(-1), gain_all.reshape(-1)]
    )
    small = small.reshape(-1, LANES)
    bit = 1
    while bit < dp:
        small = sum_pairs(small, "dp", bit)
        bit *= 2
    small = small.reshape(-1)
    n_v, n_s, n_h = layers * 7 * cols, s_all.size, h_all.size
    v_sum = small[:n_v].reshape(layers, 7, cols)
    s_sum = small[n_v : n_v + n_s].reshape(s_all.shape)
    h_sum = small[n_v + n_s : n_v + n_s + n_h].reshape(h_all.shape)
    gain_sum = small[n_v + n_s + n_h :].reshape(gain_all.shape)
    piece = width // dp
    gain_own = lax.dynamic_slice_in_dim(gain_sum, me * piece, piece, axis=1)

    g_out = jnp.stack([s[0] for s in scattered]).astype(F32)
    g_in = jnp.stack([s[1] for s in scattered]).astype(F32)
    g_gate, g_value = g_in[:, :, :cols], g_in[:, :, cols : 2 * cols]
    g_state = g_in[:, :, 2 * cols : 2 * cols + 2 * LANES]
    for bit in (1, 2):
        g_state = sum_pairs(g_state, "tensor", bit)
    g_step = g_in[:, :, 2 * cols + 2 * LANES :][:, :, :heads]
    skip_grad = v_sum[:, 6].reshape(layers, heads, P_SIZE).sum(axis=2)
    return (
        jnp.concatenate(results, axis=0)[None],
        grad_x,
        gain_own,
        g_gate,
        g_value,
        g_state,
        g_step,
        g_out,
        v_sum[:, :5],
        s_sum,
        h_sum[:, 0, :heads],
        h_sum[:, 1, :heads],
        skip_grad,
        v_sum[:, 5],
    )


def join_rows(mine, theirs, core, half, start, count):
    own = mine[start : start + count].reshape(-1, half, mine.shape[1])
    other = theirs[start : start + count].reshape(-1, half, mine.shape[1])
    first = jnp.where(core == 0, own, other)
    second = jnp.where(core == 0, other, own)
    return jnp.concatenate([first, second], axis=1).reshape(2 * count, mine.shape[1])


def solution(mesh):
    return jax.shard_map(
        per_device,
        mesh=mesh,
        in_specs=(
            P(None, "dp", None),
            P("dp", None, None),
            P(),
            P(),
            P(),
            P(None, None, "tensor"),
            P(None, None, "tensor"),
            P(),
            P(None, None, "tensor"),
            P(None, None, "tensor"),
            P(None, None, "tensor"),
            P(),
            P(None, "tensor"),
            P(None, "tensor"),
            P(None, "tensor"),
            P(None, "tensor"),
        ),
        out_specs=(
            P("dp", None, None),
            P(None, "dp", None),
            P(None, "dp"),
            P(None, "dp", "tensor"),
            P(None, "dp", "tensor"),
            P(None, "dp", None),
            P(None, "dp", "tensor"),
            P(None, "dp", "tensor"),
            P(None, None, "tensor"),
            P(),
            P(None, "tensor"),
            P(None, "tensor"),
            P(None, "tensor"),
            P(None, "tensor"),
        ),
        check_vma=False,
    )
```

time: 1700 us -> 841 us (0.49)
  waiting for transfers between devices: 805 us -> 358 us
  matrix products: 299 us -> 41.5 us
  Pallas kernels: 0 us -> 247 us
  local copies, waits for them, and re-layouts: 228 us -> 48.5 us
  other arithmetic: 195 us -> 42.1 us
  blocking collectives: 132 us -> 44.1 us
  starting transfers between devices: 14.3 us -> 33.4 us
    psum x6 -> x0, waiting for transfers between devices: 470 us -> none  [the longest x2 233 us: per_device(): branch = lax.psum(partial_value, 'tensor')]
    dot_general x54 -> x4, matrix products: 299 us -> 41.5 us  [tn(): lax.dot_general(a, b, (((0,), (0,)), ((), ())), preferred_element_type=F32)]
    pallas_call x0 -> x16, Pallas kernels: none -> 247 us  [the longest x8 142 us: backward_call(): pl.pallas_call(functools.partial(backward_kernel, top, bottom, half, base...]
    ppermute x0 -> x54, waiting for transfers between devices: none -> 140 us  [the longest x16 124 us: sum_tensor_half(): other = lax.ppermute(own, 'tensor', pairs('tensor', 2))]
    psum x6 -> x0, blocking collectives: 132 us -> none  [the longest x1 101 us: per_device(): lax.psum((small_all[0], small_all[1], small_all[2], small_all[3], small_a...]
    reduce_scatter x4, waiting for transfers between devices: 273 us -> 152 us  [per_device(): lax.psum_scatter(p, 'dp', scatter_dimension=0, tiled=True)]
    reshape x22 -> x7, local copies, waits for them, and re-layouts: 94 us -> 0.06 us  [the longest x1 0.02 us: per_device(): gain_all.reshape(-1)]
    reduce_sum x22 -> x4, other arithmetic: 68.4 us -> 3 us  [the longest x1 1.7 us: per_device(): gain_first = jnp.sum(d_low * normed, axis=0)]
  transfers between devices with their start and end apart: 14 -> 59, of which waited for: 10 -> 24; matrix products, arithmetic and copies ran while one was open for 16% -> 12% of each run, Pallas kernels for 0% -> 28%
where the time goes in v1:
time: 841 us; the launch traced here: 833 us
  waiting for transfers between devices  358 us (43%)
  Pallas kernels  247 us (29%)
  local copies, waits for them, and re-layouts  48.5 us (6%)
  blocking collectives  44.1 us (5%)
  other arithmetic  42.1 us (5%)
  matrix products  41.5 us (5%)
  starting transfers between devices  33.4 us (4%)
  between operations  18.5 us (2%)
    reduce_scatter x4, waiting for transfers between devices, per_device(): lax.psum_scatter(p, 'dp', scatter_dimension=0, tiled=True)  152 us
    pallas_call x8, Pallas kernels, backward_call(): pl.pallas_call(functools.partial(backward_kernel, top, bottom, half, base...  142 us
    ppermute x16, waiting for transfers between devices, sum_tensor_half(): other = lax.ppermute(own, 'tensor', pairs('tensor', 2))  124 us
    pallas_call x8, Pallas kernels, forward_call(): pl.pallas_call(functools.partial(forward_kernel, first, half, base, inner...  105 us
    all_to_all x1, waiting for transfers between devices, per_device(): lax.all_to_all(grad_in, 'dp', split_axis=0, concat_axis=0, tiled=True)  65.7 us
    all_to_all x1, blocking collectives, per_device(): lax.all_to_all(x_dealt, 'dp', split_axis=0, concat_axis=0, tiled=True)  44.1 us
    dot_general x4, matrix products, tn(): lax.dot_general(a, b, (((0,), (0,)), ((), ())), preferred_element_type=F32)  41.5 us
    unnamed x191, local copies, waits for them, and re-layouts  20.3 us
  transfers between devices with their start and end apart: 59, of which 24 were waited for; matrix products, arithmetic and copies ran while one was open for 12% of the time, Pallas kernels for 28%

profile of v1, /device:TPU:0, one launch (start us, length us, event | category | flops | bytes accessed | tf_op | source)
XLA Modules:
  0.0 833.1 jit_solution(8065490526534831116)
XLA Ops:
  12.7 44.1 %all_to_all.10 = bf16[8,64,1536]{2,1,0:T(8,128)(2,1)S(1)} all-to-all(bf16[8,64,1536]{2,1,0:T(8,128)(2,1)S(1)} %broadcast_select_fusion.1), channel_id=1, replica_groups=mesh['dp'=8,'tensor'=4] {'dp'}, dimensions={0} | all-to-all | bytes 3145728 | tf_op jit(solution)/shard_map/all_to_all | solution.py:713
  72.3 12.3 %layer_forward.8 = (bf16[256,1536]{1,0:T(8,128)(2,1)}, f32[256,768]{1,0:T(8,128)}, bf16[256,768]{1,0:T(8,128)(2,1)}, f32[256,768]{1,0:T(8,128)}, f32[256,768]{1,...) custom-call(s32[2]{0:T(128)} %pad_add_fusion.scal, ...), custom_call_target="tpu_custom_call" | custom-call | flops 3584000000 | bytes 20000000 | tf_op jit(solution)/shard_map/layer_forward/pallas_call | solution.py:521
  85.0 12.3 %layer_forward.10 = (bf16[256,1536]{1,0:T(8,128)(2,1)}, f32[256,768]{1,0:T(8,128)}, bf16[256,768]{1,0:T(8,128)(2,1)}, f32[256,768]{1,0:T(8,128)}, f32[256,768]{1...) custom-call(s32[2]{0:T(128)} %pad_add_fusion.scal, ...), custom_call_target="tpu_custom_call" | custom-call | flops 3584000000 | bytes 20000000 | tf_op jit(solution)/shard_map/layer_forward/pallas_call | solution.py:521
  97.5 12.5 %layer_forward.12 = (bf16[256,1536]{1,0:T(8,128)(2,1)}, f32[256,768]{1,0:T(8,128)}, bf16[256,768]{1,0:T(8,128)(2,1)}, f32[256,768]{1,0:T(8,128)}, f32[256,768]{1...) custom-call(s32[2]{0:T(128)} %pad_add_fusion.scal, ...), custom_call_target="tpu_custom_call" | custom-call | flops 3584000000 | bytes 20000000 | tf_op jit(solution)/shard_map/layer_forward/pallas_call | solution.py:521
  110.5 12.3 %layer_forward.14 = (bf16[256,1536]{1,0:T(8,128)(2,1)}, f32[256,768]{1,0:T(8,128)}, bf16[256,768]{1,0:T(8,128)(2,1)}, f32[256,768]{1,0:T(8,128)}, f32[256,768]{1...) custom-call(s32[2]{0:T(128)} %pad_add_fusion.scal, ...), custom_call_target="tpu_custom_call" | custom-call | flops 3584000000 | bytes 20000000 | tf_op jit(solution)/shard_map/layer_forward/pallas_call | solution.py:521
  128.3 9.3 %collective-permute-done.2 = bf16[128,1664]{1,0:T(8,128)(2,1)S(1)} collective-permute-done((bf16[128,1664]{1,0:T(8,128)(2,1)S(1)}, bf16[128,1664]{1,0:T(8,128)(2,1)S(1)}, u32[]{:S(2)}, u32[]{:S(2)}) %collective-permute-start.2) | collective-permute-done | bytes 426016 | tf_op jit(solution)/shard_map/ppermute | solution.py:668
  141.1 14.0 %layer_forward.9 = (f32[256,1536]{1,0:T(8,128)}, bf16[256,1536]{1,0:T(8,128)(2,1)}, f32[256,768]{1,0:T(8,128)}, bf16[256,768]{1,0:T(8,128)(2,1)}, f32[256,768]{1...) custom-call(s32[2]{0:T(128)} %pad_add_fusion.scal, ...), custom_call_target="tpu_custom_call" | custom-call | flops 3584000000 | bytes 20000000 | tf_op jit(solution)/shard_map/layer_forward/pallas_call | solution.py:521
  164.6 8.9 %collective-permute-done.8 = bf16[128,1664]{1,0:T(8,128)(2,1)S(1)} collective-permute-done((bf16[128,1664]{1,0:T(8,128)(2,1)S(1)}, bf16[128,1664]{1,0:T(8,128)(2,1)S(1)}, u32[]{:S(2)}, u32[]{:S(2)}) %collective-permute-start.8) | collective-permute-done | bytes 426016 | tf_op jit(solution)/shard_map/ppermute | solution.py:668
  173.7 17.5 %collective-permute-done.14 = bf16[128,1664]{1,0:T(8,128)(2,1)S(1)} collective-permute-done((bf16[128,1664]{1,0:T(8,128)(2,1)S(1)}, bf16[128,1664]{1,0:T(8,128)(2,1)S(1)}, u32[]{:S(2)}, u32[]{:S(2)}) %collective-permute-start.14) | collective-permute-done | bytes 426016 | tf_op jit(solution)/shard_map/ppermute | solution.py:668
  194.6 13.8 %layer_forward.11 = (f32[256,1536]{1,0:T(8,128)}, bf16[256,1536]{1,0:T(8,128)(2,1)}, f32[256,768]{1,0:T(8,128)}, bf16[256,768]{1,0:T(8,128)(2,1)}, f32[256,768]{...) custom-call(s32[2]{0:T(128)} %pad_add_fusion.scal, ...), custom_call_target="tpu_custom_call" | custom-call | flops 3584000000 | bytes 20000000 | tf_op jit(solution)/shard_map/layer_forward/pallas_call | solution.py:521
  209.5 14.1 %layer_forward.13 = (f32[256,1536]{1,0:T(8,128)}, bf16[256,1536]{1,0:T(8,128)(2,1)}, f32[256,768]{1,0:T(8,128)}, bf16[256,768]{1,0:T(8,128)(2,1)}, f32[256,768]{...) custom-call(s32[2]{0:T(128)} %pad_add_fusion.scal, ...), custom_call_target="tpu_custom_call" | custom-call | flops 3584000000 | bytes 20000000 | tf_op jit(solution)/shard_map/layer_forward/pallas_call | solution.py:521
  225.1 13.9 %layer_forward.15 = (f32[256,1536]{1,0:T(8,128)}, bf16[256,1536]{1,0:T(8,128)(2,1)}, f32[256,768]{1,0:T(8,128)}, bf16[256,768]{1,0:T(8,128)(2,1)}, f32[256,768]{...) custom-call(s32[2]{0:T(128)} %pad_add_fusion.scal, ...), custom_call_target="tpu_custom_call" | custom-call | flops 3584000000 | bytes 20000000 | tf_op jit(solution)/shard_map/layer_forward/pallas_call | solution.py:521
  245.9 9.9 %collective-permute-done.23 = bf16[128,1664]{1,0:T(8,128)(2,1)S(1)} collective-permute-done((bf16[128,1664]{1,0:T(8,128)(2,1)S(1)}, bf16[128,1664]{1,0:T(8,128)(2,1)S(1)}, u32[]{:S(2)}, u32[]{:S(2)}) %collective-permute-start.23) | collective-permute-done | bytes 426016 | tf_op jit(solution)/shard_map/ppermute | solution.py:668
  256.0 8.9 %collective-permute-done.17 = bf16[128,1664]{1,0:T(8,128)(2,1)S(1)} collective-permute-done((bf16[128,1664]{1,0:T(8,128)(2,1)S(1)}, bf16[128,1664]{1,0:T(8,128)(2,1)S(1)}, u32[]{:S(2)}, u32[]{:S(2)}) %collective-permute-start.17) | collective-permute-done | bytes 426016 | tf_op jit(solution)/shard_map/ppermute | solution.py:668
  265.1 8.2 collective-permute-done.11
  276.1 17.6 %layer_backward.8 = (bf16[256,1536]{1,0:T(8,128)(2,1)}, f32[256,1536]{1,0:T(8,128)}, bf16[256,1536]{1,0:T(8,128)(2,1)}, bf16[256,768]{1,0:T(8,128)(2,1)}, bf16[2...) custom-call(s32[2]{0:T(128)} %pad_add_fusion.scal, ...), custom_call_target="tpu_custom_call" | custom-call | flops 5120000000 | bytes 25000000 | tf_op jit(solution)/shard_map/layer_backward/pallas_call | solution.py:624
  295.1 17.4 %layer_backward.9 = (bf16[256,1536]{1,0:T(8,128)(2,1)}, f32[256,1536]{1,0:T(8,128)}, bf16[256,1536]{1,0:T(8,128)(2,1)}, bf16[256,768]{1,0:T(8,128)(2,1)}, bf16[2...) custom-call(s32[2]{0:T(128)} %pad_add_fusion.scal, ...), custom_call_target="tpu_custom_call" | custom-call | flops 5120000000 | bytes 25000000 | tf_op jit(solution)/shard_map/layer_backward/pallas_call | solution.py:624
  313.6 17.9 %layer_backward.10 = (bf16[256,1536]{1,0:T(8,128)(2,1)}, f32[256,1536]{1,0:T(8,128)}, bf16[256,1536]{1,0:T(8,128)(2,1)}, bf16[256,768]{1,0:T(8,128)(2,1)}, bf16[...) custom-call(s32[2]{0:T(128)} %pad_add_fusion.scal, ...), custom_call_target="tpu_custom_call" | custom-call | flops 5120000000 | bytes 25000000 | tf_op jit(solution)/shard_map/layer_backward/pallas_call | solution.py:624
  332.9 17.9 %layer_backward.11 = (bf16[256,1536]{1,0:T(8,128)(2,1)}, f32[256,1536]{1,0:T(8,128)}, bf16[256,1536]{1,0:T(8,128)(2,1)}, bf16[256,768]{1,0:T(8,128)(2,1)}, bf16[...) custom-call(s32[2]{0:T(128)} %pad_add_fusion.scal, ...), custom_call_target="tpu_custom_call" | custom-call | flops 5120000000 | bytes 25000000 | tf_op jit(solution)/shard_map/layer_backward/pallas_call | solution.py:624
  351.0 5.4 convolution_convert_fusion.2
  364.9 4.9 collective-permute-done.35
  370.0 8.2 collective-permute-done.32
  378.5 8.2 collective-permute-done.29
  386.9 7.7 collective-permute-done.26
  395.8 17.6 %layer_backward.12 = (f32[128,1536]{1,0:T(8,128)}, bf16[256,1536]{1,0:T(8,128)(2,1)}, bf16[256,768]{1,0:T(8,128)(2,1)}, bf16[256,768]{1,0:T(8,128)(2,1)}, bf16[2...) custom-call(s32[2]{0:T(128)} %pad_add_fusion.scal, ...), custom_call_target="tpu_custom_call" | custom-call | flops 5120000000 | bytes 25000000 | tf_op jit(solution)/shard_map/layer_backward/pallas_call | solution.py:624
  414.3 17.7 %layer_backward.13 = (f32[128,1536]{1,0:T(8,128)}, bf16[256,1536]{1,0:T(8,128)(2,1)}, bf16[256,768]{1,0:T(8,128)(2,1)}, bf16[256,768]{1,0:T(8,128)(2,1)}, bf16[2...) custom-call(s32[2]{0:T(128)} %pad_add_fusion.scal, ...), custom_call_target="tpu_custom_call" | custom-call | flops 5120000000 | bytes 25000000 | tf_op jit(solution)/shard_map/layer_backward/pallas_call | solution.py:624
  432.9 17.9 %layer_backward.14 = (f32[128,1536]{1,0:T(8,128)}, bf16[256,1536]{1,0:T(8,128)(2,1)}, bf16[256,768]{1,0:T(8,128)(2,1)}, bf16[256,768]{1,0:T(8,128)(2,1)}, bf16[2...) custom-call(s32[2]{0:T(128)} %pad_add_fusion.scal, ...), custom_call_target="tpu_custom_call" | custom-call | flops 5120000000 | bytes 25000000 | tf_op jit(solution)/shard_map/layer_backward/pallas_call | solution.py:624
  451.7 17.9 %layer_backward.15 = (f32[128,1536]{1,0:T(8,128)}, bf16[256,1536]{1,0:T(8,128)(2,1)}, bf16[256,768]{1,0:T(8,128)(2,1)}, bf16[256,768]{1,0:T(8,128)(2,1)}, bf16[2...) custom-call(s32[2]{0:T(128)} %pad_add_fusion.scal, ...), custom_call_target="tpu_custom_call" | custom-call | flops 5120000000 | bytes 25000000 | tf_op jit(solution)/shard_map/layer_backward/pallas_call | solution.py:624
  469.7 5.5 convolution_convert_fusion.3
  475.3 15.2 %convolution_convert_fusion = bf16[1536,1920]{1,0:T(8,128)(2,1)} fusion(bf16[256,128]{1,0:T(8,128)(2,1)} %get-tuple-element.445, bf16[256,256]{1,0:T(8,128)(2,1)} %get-tuple-element.444, bf16[256,768]{1,0:T(8,128)(2,1)} %get-tuple-element.443, bf16[256,768]{1,0:T(8,128)(2,1)S(1)} %copy-done.81, bf16[256,128]{1,0:T(8,128)(2,1)} %get-tuple-element.441, ...), kind=kOutput, calls=%fused_computation.2 | convolution fusion | flops 6118244352 | bytes 12976128 | tf_op jit(solution)/shard_map/dot_general | solution.py:33
  492.5 15.5 %convolution_convert_fusion.1 = bf16[1536,1920]{1,0:T(8,128)(2,1)} fusion(bf16[256,128]{1,0:T(8,128)(2,1)} %get-tuple-element.425, bf16[256,256]{1,0:T(8,128)(2,1)} %get-tuple-element.424, bf16[256,768]{1,0:T(8,128)(2,1)} %get-tuple-element.423, bf16[256,768]{1,0:T(8,128)(2,1)S(1)} %copy-done.82, bf16[256,128]{1,0:T(8,128)(2,1)} %get-tuple-element.421, ...), kind=kOutput, calls=%fused_computation.3 | convolution fusion | flops 6118244352 | bytes 12976128 | tf_op jit(solution)/shard_map/dot_general | solution.py:33
  517.3 7.4 collective-permute-done.44
  524.8 8.3 collective-permute-done.42
  533.3 8.3 collective-permute-done.40
  541.7 7.6 collective-permute-done.38
  551.3 2.5 multiply_convert_fusion
  553.9 4.0 all-to-all-start.1
  562.3 2.2 collective-permute-done.47
  566.8 65.7 %all-to-all-done.1 = bf16[8,64,1536]{2,1,0:T(8,128)(2,1)S(1)} async-done(((bf16[8,64,1536]{2,1,0:T(8,128)(2,1)}), bf16[8,64,1536]{2,1,0:T(8,128)(2,1)S(1)}, u32[]{:S(2)}, u32[]{:S(2)}) %all-to-all-start.1) | async-done | bytes 1572896 | tf_op jit(solution)/shard_map/all_to_all | solution.py:827
  632.5 5.6 collective-permute-done.50
  638.2 3.1 maximum_bitcast_fusion
  641.4 2.9 collective-permute-done.51
  648.2 2.2 maximum_convert_fusion.1
  652.4 2.6 gather_fusion.1
  655.1 36.8 %reduce-scatter.7.cloned.1.call-done = bf16[192,1920]{1,0:T(8,128)(2,1)} async-done(((bf16[1536,1920]{1,0:T(8,128)(2,1)}), bf16[192,1920]{1,0:T(8,128)(2,1)}) %reduce-scatter.7.cloned.1.call-update) | async-done | bytes 737296 | tf_op jit(solution)/shard_map/reduce_scatter | solution.py:809
  691.8 115.1 %reduce-scatter.5.cloned.1.call-done = bf16[192,1920]{1,0:T(8,128)(2,1)} async-done(((bf16[1536,1920]{1,0:T(8,128)(2,1)}), bf16[192,1920]{1,0:T(8,128)(2,1)}) %reduce-scatter.5.cloned.1.call-update) | async-done | bytes 737296 | tf_op jit(solution)/shard_map/reduce_scatter | solution.py:809
  816.6 3.3 fusion.120
  819.9 4.6 collective-permute-done.53
  (436 shorter events, 107.9 us)
Async XLA Ops:
  7.2 641.0 %reduce-scatter.11.cloned.1.call-start = ((), (), s32[]{:S(2)}) async-start(), calls=%async_computation.9 | async-start | bytes 2654208 | tf_op jit(solution)/shard_map/reduce_scatter | solution.py:809
  56.8 10.3 %collective-permute-start = (bf16[512,1536]{1,0:T(8,128)(2,1)S(1)}, bf16[512,1536]{1,0:T(8,128)(2,1)}, u32[]{:S(2)}, u32[]{:S(2)}) collective-permute-start(bf16[512,1536]{1,0:T(8,128)(2,1)S(1)} %bitcast.77), channel_id=1, source_target_pairs={{0,1},{1,0},{2,3},{3,2},{4,5},{5,4},{6,7},{7,6},{8,9},{9,8},{10,11... | collective-permute-start | bytes 4718600 | tf_op jit(solution)/shard_map/ppermute | solution.py:673
  84.6 38.5 %collective-permute-start.1 = (f32[128,1664]{1,0:T(8,128)}, f32[128,1664]{1,0:T(8,128)S(1)}, u32[]{:S(2)}, u32[]{:S(2)}) collective-permute-start(f32[128,1664]{1,0:T(8,128)} %get-tuple-element.239), channel_id=1, source_target_pairs={{0,1},{1,0},{2,3},{3,2},{4,5},{5,4},{6,7},{7,6},{8,9},{9,8},{10,11... | collective-permute-start | bytes 2555912 | tf_op jit(solution)/shard_map/ppermute | solution.py:666
  97.3 62.3 %collective-permute-start.7 = (f32[128,1664]{1,0:T(8,128)}, f32[128,1664]{1,0:T(8,128)S(1)}, u32[]{:S(2)}, u32[]{:S(2)}) collective-permute-start(f32[128,1664]{1,0:T(8,128)} %get-tuple-element.255), channel_id=1, source_target_pairs={{0,1},{1,0},{2,3},{3,2},{4,5},{5,4},{6,7},{7,6},{8,9},{9,8},{10,11... | collective-permute-start | bytes 2555912 | tf_op jit(solution)/shard_map/ppermute | solution.py:666
  110.1 49.3 %collective-permute-start.13 = (f32[128,1664]{1,0:T(8,128)}, f32[128,1664]{1,0:T(8,128)S(1)}, u32[]{:S(2)}, u32[]{:S(2)}) collective-permute-start(f32[128,1664]{1,0:T(8,128)} %get-tuple-element.274), channel_id=1, source_target_pairs={{0,1},{1,0},{2,3},{3,2},{4,5},{5,4},{6,7},{7,6},{8,9},{9,8},{10,11... | collective-permute-start | bytes 2555912 | tf_op jit(solution)/shard_map/ppermute | solution.py:666
  122.9 35.1 %collective-permute-start.19 = (f32[128,1664]{1,0:T(8,128)}, f32[128,1664]{1,0:T(8,128)}, u32[]{:S(2)}, u32[]{:S(2)}) collective-permute-start(f32[128,1664]{1,0:T(8,128)} %get-tuple-element.293), channel_id=1, source_target_pairs={{0,1},{1,0},{2,3},{3,2},{4,5},{5,4},{6,7},{7,6},{8,9},{9,8},{10,11... | collective-permute-start | bytes 2555912 | tf_op jit(solution)/shard_map/ppermute | solution.py:666
  125.4 12.2 %collective-permute-start.2 = (bf16[128,1664]{1,0:T(8,128)(2,1)S(1)}, bf16[128,1664]{1,0:T(8,128)(2,1)S(1)}, u32[]{:S(2)}, u32[]{:S(2)}) collective-permute-start(bf16[128,1664]{1,0:T(8,128)(2,1)S(1)} %pad_maximum_fusion.6), channel_id=1, source_target_pairs={{0,2},{1,3},{2,0},{3,1},{4,6},{5,7},{6,4},{7,5},{8,10},{9,11},{10,... | collective-permute-start | bytes 1277960 | tf_op jit(solution)/shard_map/ppermute | solution.py:668
  160.8 12.7 %collective-permute-start.8 = (bf16[128,1664]{1,0:T(8,128)(2,1)S(1)}, bf16[128,1664]{1,0:T(8,128)(2,1)S(1)}, u32[]{:S(2)}, u32[]{:S(2)}) collective-permute-start(bf16[128,1664]{1,0:T(8,128)(2,1)S(1)} %pad_maximum_fusion.8), channel_id=1, source_target_pairs={{0,2},{1,3},{2,0},{3,1},{4,6},{5,7},{6,4},{7,5},{8,10},{9,11},{10,... | collective-permute-start | bytes 1277960 | tf_op jit(solution)/shard_map/ppermute | solution.py:668
  162.4 29.0 %collective-permute-start.20 = (bf16[128,1664]{1,0:T(8,128)(2,1)S(1)}, bf16[128,1664]{1,0:T(8,128)(2,1)S(1)}, u32[]{:S(2)}, u32[]{:S(2)}) collective-permute-start(bf16[128,1664]{1,0:T(8,128)(2,1)S(1)} %pad_maximum_fusion.12), channel_id=1, source_target_pairs={{0,2},{1,3},{2,0},{3,1},{4,6},{5,7},{6,4},{7,5},{8,10},{9,11},{10,... | collective-permute-start | bytes 1277960 | tf_op jit(solution)/shard_map/ppermute | solution.py:668
  163.1 28.2 %collective-permute-start.14 = (bf16[128,1664]{1,0:T(8,128)(2,1)S(1)}, bf16[128,1664]{1,0:T(8,128)(2,1)S(1)}, u32[]{:S(2)}, u32[]{:S(2)}) collective-permute-start(bf16[128,1664]{1,0:T(8,128)(2,1)S(1)} %pad_maximum_fusion.10), channel_id=1, source_target_pairs={{0,2},{1,3},{2,0},{3,1},{4,6},{5,7},{6,4},{7,5},{8,10},{9,11},{10,... | collective-permute-start | bytes 1277960 | tf_op jit(solution)/shard_map/ppermute | solution.py:668
  173.6 20.0 %collective-permute-start.9 = (f32[128,1664]{1,0:T(8,128)S(1)}, f32[128,1664]{1,0:T(8,128)S(1)}, u32[]{:S(2)}, u32[]{:S(2)}) collective-permute-start(f32[128,1664]{1,0:T(8,128)S(1)} %convert_add_fusion.5.refs_1_.refs_4_), channel_id=1, source_target_pairs={{0,1},{1,0},{2,3},{3,2},{4,5},{5,4},{6,7},{7,6},{8,9},{9,8},{10,11... | collective-permute-start | bytes 2555912 | tf_op jit(solution)/shard_map/ppermute | solution.py:673
  191.3 17.2 %collective-permute-start.15 = (f32[128,1664]{1,0:T(8,128)S(1)}, f32[128,1664]{1,0:T(8,128)S(1)}, u32[]{:S(2)}, u32[]{:S(2)}) collective-permute-start(f32[128,1664]{1,0:T(8,128)S(1)} %convert_add_fusion.3.refs_1_.refs_4_), channel_id=1, source_target_pairs={{0,1},{1,0},{2,3},{3,2},{4,5},{5,4},{6,7},{7,6},{8,9},{9,8},{10,11... | collective-permute-start | bytes 2555912 | tf_op jit(solution)/shard_map/ppermute | solution.py:673
  191.5 32.6 %collective-permute-start.21 = (f32[128,1664]{1,0:T(8,128)S(1)}, f32[128,1664]{1,0:T(8,128)S(1)}, u32[]{:S(2)}, u32[]{:S(2)}) collective-permute-start(f32[128,1664]{1,0:T(8,128)S(1)} %convert_add_fusion.1.refs_1_.refs_4_), channel_id=1, source_target_pairs={{0,1},{1,0},{2,3},{3,2},{4,5},{5,4},{6,7},{7,6},{8,9},{9,8},{10,11... | collective-permute-start | bytes 2555912 | tf_op jit(solution)/shard_map/ppermute | solution.py:673
  192.1 48.7 %collective-permute-start.5 = (bf16[128,1664]{1,0:T(8,128)(2,1)S(1)}, bf16[128,1664]{1,0:T(8,128)(2,1)S(1)}, u32[]{:S(2)}, u32[]{:S(2)}) collective-permute-start(bf16[128,1664]{1,0:T(8,128)(2,1)S(1)} %pad_maximum_fusion.7), channel_id=1, source_target_pairs={{0,2},{1,3},{2,0},{3,1},{4,6},{5,7},{6,4},{7,5},{8,10},{9,11},{10,... | collective-permute-start | bytes 1277960 | tf_op jit(solution)/shard_map/ppermute | solution.py:668
  208.5 33.9 %collective-permute-start.10 = (f32[128,1664]{1,0:T(8,128)}, f32[128,1664]{1,0:T(8,128)S(1)}, u32[]{:S(2)}, u32[]{:S(2)}) collective-permute-start(f32[128,1664]{1,0:T(8,128)} %get-tuple-element.261), channel_id=1, source_target_pairs={{0,1},{1,0},{2,3},{3,2},{4,5},{5,4},{6,7},{7,6},{8,9},{9,8},{10,11... | collective-permute-start | bytes 2555912 | tf_op jit(solution)/shard_map/ppermute | solution.py:666
  223.6 18.2 %collective-permute-start.16 = (f32[128,1664]{1,0:T(8,128)}, f32[128,1664]{1,0:T(8,128)S(1)}, u32[]{:S(2)}, u32[]{:S(2)}) collective-permute-start(f32[128,1664]{1,0:T(8,128)} %get-tuple-element.280), channel_id=1, source_target_pairs={{0,1},{1,0},{2,3},{3,2},{4,5},{5,4},{6,7},{7,6},{8,9},{9,8},{10,11... | collective-permute-start | bytes 2555912 | tf_op jit(solution)/shard_map/ppermute | solution.py:666
  240.9 91.1 %collective-permute-start.6 = (f32[128,1664]{1,0:T(8,128)S(1)}, f32[128,1664]{1,0:T(8,128)S(1)}, u32[]{:S(2)}, u32[]{:S(2)}) collective-permute-start(f32[128,1664]{1,0:T(8,128)S(1)} %convert_add_fusion.6.refs_2_), channel_id=1, source_target_pairs={{0,1},{1,0},{2,3},{3,2},{4,5},{5,4},{6,7},{7,6},{8,9},{9,8},{10,11... | collective-permute-start | bytes 2555912 | tf_op jit(solution)/shard_map/ppermute | solution.py:673
  243.1 12.7 %collective-permute-start.23 = (bf16[128,1664]{1,0:T(8,128)(2,1)S(1)}, bf16[128,1664]{1,0:T(8,128)(2,1)S(1)}, u32[]{:S(2)}, u32[]{:S(2)}) collective-permute-start(bf16[128,1664]{1,0:T(8,128)(2,1)S(1)} %pad_maximum_fusion.13), channel_id=1, source_target_pairs={{0,2},{1,3},{2,0},{3,1},{4,6},{5,7},{6,4},{7,5},{8,10},{9,11},{10,... | collective-permute-start | bytes 1277960 | tf_op jit(solution)/shard_map/ppermute | solution.py:668
  243.7 21.2 %collective-permute-start.17 = (bf16[128,1664]{1,0:T(8,128)(2,1)S(1)}, bf16[128,1664]{1,0:T(8,128)(2,1)S(1)}, u32[]{:S(2)}, u32[]{:S(2)}) collective-permute-start(bf16[128,1664]{1,0:T(8,128)(2,1)S(1)} %pad_maximum_fusion.11), channel_id=1, source_target_pairs={{0,2},{1,3},{2,0},{3,1},{4,6},{5,7},{6,4},{7,5},{8,10},{9,11},{10,... | collective-permute-start | bytes 1277960 | tf_op jit(solution)/shard_map/ppermute | solution.py:668
  245.3 28.0 %collective-permute-start.11 = (bf16[128,1664]{1,0:T(8,128)(2,1)S(1)}, bf16[128,1664]{1,0:T(8,128)(2,1)S(1)}, u32[]{:S(2)}, u32[]{:S(2)}) collective-permute-start(bf16[128,1664]{1,0:T(8,128)(2,1)S(1)} %pad_maximum_fusion.9), channel_id=1, source_target_pairs={{0,2},{1,3},{2,0},{3,1},{4,6},{5,7},{6,4},{7,5},{8,10},{9,11},{10,... | collective-permute-start | bytes 1277960 | tf_op jit(solution)/shard_map/ppermute | solution.py:668
  255.9 17.6 %collective-permute-start.24 = (f32[128,1664]{1,0:T(8,128)S(1)}, f32[128,1664]{1,0:T(8,128)S(1)}, u32[]{:S(2)}, u32[]{:S(2)}) collective-permute-start(f32[128,1664]{1,0:T(8,128)S(1)} %convert_add_fusion.refs_2_), channel_id=1, source_target_pairs={{0,1},{1,0},{2,3},{3,2},{4,5},{5,4},{6,7},{7,6},{8,9},{9,8},{10,11... | collective-permute-start | bytes 2555912 | tf_op jit(solution)/shard_map/ppermute | solution.py:673
  265.0 29.2 %collective-permute-start.18 = (f32[128,1664]{1,0:T(8,128)S(1)}, f32[128,1664]{1,0:T(8,128)S(1)}, u32[]{:S(2)}, u32[]{:S(2)}) collective-permute-start(f32[128,1664]{1,0:T(8,128)S(1)} %convert_add_fusion.2.refs_2_), channel_id=1, source_target_pairs={{0,1},{1,0},{2,3},{3,2},{4,5},{5,4},{6,7},{7,6},{8,9},{9,8},{10,11... | collective-permute-start | bytes 2555912 | tf_op jit(solution)/shard_map/ppermute | solution.py:673
  273.4 39.3 %collective-permute-start.12 = (f32[128,1664]{1,0:T(8,128)S(1)}, f32[128,1664]{1,0:T(8,128)S(1)}, u32[]{:S(2)}, u32[]{:S(2)}) collective-permute-start(f32[128,1664]{1,0:T(8,128)S(1)} %convert_add_fusion.4.refs_2_), channel_id=1, source_target_pairs={{0,1},{1,0},{2,3},{3,2},{4,5},{5,4},{6,7},{7,6},{8,9},{9,8},{10,11... | collective-permute-start | bytes 2555912 | tf_op jit(solution)/shard_map/ppermute | solution.py:673
  293.8 62.7 %collective-permute-start.34 = (f32[128,1536]{1,0:T(8,128)}, f32[128,1536]{1,0:T(8,128)}, u32[]{:S(2)}, u32[]{:S(2)}) collective-permute-start(f32[128,1536]{1,0:T(8,128)} %get-tuple-element.362), channel_id=1, source_target_pairs={{0,1},{1,0},{2,3},{3,2},{4,5},{5,4},{6,7},{7,6},{8,9},{9,8},{10,11... | collective-permute-start | bytes 2359304 | tf_op jit(solution)/shard_map/ppermute | solution.py:666
  312.5 45.9 %collective-permute-start.31 = (f32[128,1536]{1,0:T(8,128)}, f32[128,1536]{1,0:T(8,128)S(1)}, u32[]{:S(2)}, u32[]{:S(2)}) collective-permute-start(f32[128,1536]{1,0:T(8,128)} %get-tuple-element.351), channel_id=1, source_target_pairs={{0,1},{1,0},{2,3},{3,2},{4,5},{5,4},{6,7},{7,6},{8,9},{9,8},{10,11... | collective-permute-start | bytes 2359304 | tf_op jit(solution)/shard_map/ppermute | solution.py:666
  331.5 28.6 %collective-permute-start.28 = (f32[128,1536]{1,0:T(8,128)}, f32[128,1536]{1,0:T(8,128)}, u32[]{:S(2)}, u32[]{:S(2)}) collective-permute-start(f32[128,1536]{1,0:T(8,128)} %get-tuple-element.340), channel_id=1, source_target_pairs={{0,1},{1,0},{2,3},{3,2},{4,5},{5,4},{6,7},{7,6},{8,9},{9,8},{10,11... | collective-permute-start | bytes 2359304 | tf_op jit(solution)/shard_map/ppermute | solution.py:666
  350.8 11.4 %collective-permute-start.25 = (f32[128,1536]{1,0:T(8,128)}, f32[128,1536]{1,0:T(8,128)}, u32[]{:S(2)}, u32[]{:S(2)}) collective-permute-start(f32[128,1536]{1,0:T(8,128)} %get-tuple-element.329), channel_id=1, source_target_pairs={{0,1},{1,0},{2,3},{3,2},{4,5},{5,4},{6,7},{7,6},{8,9},{9,8},{10,11... | collective-permute-start | bytes 2359304 | tf_op jit(solution)/shard_map/ppermute | solution.py:666
  356.4 291.8 %reduce-scatter.9.cloned.1.call-start = ((), (), s32[]{:S(2)}) async-start(), calls=%async_computation.8 | async-start | bytes 2654208 | tf_op jit(solution)/shard_map/reduce_scatter | solution.py:809
  357.8 12.0 %collective-permute-start.35 = (bf16[128,1536]{1,0:T(8,128)(2,1)S(1)}, bf16[128,1536]{1,0:T(8,128)(2,1)S(1)}, u32[]{:S(2)}, u32[]{:S(2)}) collective-permute-start(bf16[128,1536]{1,0:T(8,128)(2,1)S(1)} %add_convert_fusion.4), channel_id=1, source_target_pairs={{0,2},{1,3},{2,0},{3,1},{4,6},{5,7},{6,4},{7,5},{8,10},{9,11},{10,... | collective-permute-start | bytes 1179656 | tf_op jit(solution)/shard_map/ppermute | solution.py:668
  358.5 19.7 %collective-permute-start.32 = (bf16[128,1536]{1,0:T(8,128)(2,1)S(1)}, bf16[128,1536]{1,0:T(8,128)(2,1)S(1)}, u32[]{:S(2)}, u32[]{:S(2)}) collective-permute-start(bf16[128,1536]{1,0:T(8,128)(2,1)S(1)} %add_convert_fusion.5), channel_id=1, source_target_pairs={{0,2},{1,3},{2,0},{3,1},{4,6},{5,7},{6,4},{7,5},{8,10},{9,11},{10,... | collective-permute-start | bytes 1179656 | tf_op jit(solution)/shard_map/ppermute | solution.py:668
  361.5 25.1 %collective-permute-start.29 = (bf16[128,1536]{1,0:T(8,128)(2,1)S(1)}, bf16[128,1536]{1,0:T(8,128)(2,1)S(1)}, u32[]{:S(2)}, u32[]{:S(2)}) collective-permute-start(bf16[128,1536]{1,0:T(8,128)(2,1)S(1)} %add_convert_fusion.6), channel_id=1, source_target_pairs={{0,2},{1,3},{2,0},{3,1},{4,6},{5,7},{6,4},{7,5},{8,10},{9,11},{10,... | collective-permute-start | bytes 1179656 | tf_op jit(solution)/shard_map/ppermute | solution.py:668
  363.4 31.2 %collective-permute-start.26 = (bf16[128,1536]{1,0:T(8,128)(2,1)S(1)}, bf16[128,1536]{1,0:T(8,128)(2,1)S(1)}, u32[]{:S(2)}, u32[]{:S(2)}) collective-permute-start(bf16[128,1536]{1,0:T(8,128)(2,1)S(1)} %add_convert_fusion.7), channel_id=1, source_target_pairs={{0,2},{1,3},{2,0},{3,1},{4,6},{5,7},{6,4},{7,5},{8,10},{9,11},{10,... | collective-permute-start | bytes 1179656 | tf_op jit(solution)/shard_map/ppermute | solution.py:668
  369.9 24.8 %collective-permute-start.36 = (f32[128,1536]{1,0:T(8,128)S(1)}, f32[128,1536]{1,0:T(8,128)S(1)}, u32[]{:S(2)}, u32[]{:S(2)}) collective-permute-start(f32[128,1536]{1,0:T(8,128)S(1)} %convert_add_fusion.12.refs_2_), channel_id=1, source_target_pairs={{0,1},{1,0},{2,3},{3,2},{4,5},{5,4},{6,7},{7,6},{8,9},{9,8},{10,11... | collective-permute-start | bytes 2359304 | tf_op jit(solution)/shard_map/ppermute | solution.py:673
  378.4 35.0 %collective-permute-start.33 = (f32[128,1536]{1,0:T(8,128)S(1)}, f32[128,1536]{1,0:T(8,128)S(1)}, u32[]{:S(2)}, u32[]{:S(2)}) collective-permute-start(f32[128,1536]{1,0:T(8,128)S(1)} %convert_add_fusion.13.refs_2_), channel_id=1, source_target_pairs={{0,1},{1,0},{2,3},{3,2},{4,5},{5,4},{6,7},{7,6},{8,9},{9,8},{10,11... | collective-permute-start | bytes 2359304 | tf_op jit(solution)/shard_map/ppermute | solution.py:673
  386.8 45.2 %collective-permute-start.30 = (f32[128,1536]{1,0:T(8,128)S(1)}, f32[128,1536]{1,0:T(8,128)S(1)}, u32[]{:S(2)}, u32[]{:S(2)}) collective-permute-start(f32[128,1536]{1,0:T(8,128)S(1)} %convert_add_fusion.14.refs_2_), channel_id=1, source_target_pairs={{0,1},{1,0},{2,3},{3,2},{4,5},{5,4},{6,7},{7,6},{8,9},{9,8},{10,11... | collective-permute-start | bytes 2359304 | tf_op jit(solution)/shard_map/ppermute | solution.py:673
  394.7 56.1 %collective-permute-start.27 = (f32[128,1536]{1,0:T(8,128)S(1)}, f32[128,1536]{1,0:T(8,128)S(1)}, u32[]{:S(2)}, u32[]{:S(2)}) collective-permute-start(f32[128,1536]{1,0:T(8,128)S(1)} %convert_add_fusion.15.refs_2_), channel_id=1, source_target_pairs={{0,1},{1,0},{2,3},{3,2},{4,5},{5,4},{6,7},{7,6},{8,9},{9,8},{10,11... | collective-permute-start | bytes 2359304 | tf_op jit(solution)/shard_map/ppermute | solution.py:673
  475.2 216.6 %reduce-scatter.7.cloned.1.call-start = ((), (), s32[]{:S(2)}) async-start(), calls=%async_computation.7 | async-start | bytes 6635520 | tf_op jit(solution)/shard_map/reduce_scatter | solution.py:809
  490.6 316.4 %reduce-scatter.5.cloned.1.call-start = ((), (), s32[]{:S(2)}) async-start(), calls=%async_computation.6 | async-start | bytes 6635520 | tf_op jit(solution)/shard_map/reduce_scatter | solution.py:809
  512.7 12.0 %collective-permute-start.44 = (bf16[128,1536]{1,0:T(8,128)(2,1)S(1)}, bf16[128,1536]{1,0:T(8,128)(2,1)S(1)}, u32[]{:S(2)}, u32[]{:S(2)}) collective-permute-start(bf16[128,1536]{1,0:T(8,128)(2,1)S(1)} %add_convert_fusion), channel_id=1, source_target_pairs={{0,2},{1,3},{2,0},{3,1},{4,6},{5,7},{6,4},{7,5},{8,10},{9,11},{10,... | collective-permute-start | bytes 1179656 | tf_op jit(solution)/shard_map/ppermute | solution.py:668
  513.4 19.8 %collective-permute-start.42 = (bf16[128,1536]{1,0:T(8,128)(2,1)S(1)}, bf16[128,1536]{1,0:T(8,128)(2,1)S(1)}, u32[]{:S(2)}, u32[]{:S(2)}) collective-permute-start(bf16[128,1536]{1,0:T(8,128)(2,1)S(1)} %add_convert_fusion.1), channel_id=1, source_target_pairs={{0,2},{1,3},{2,0},{3,1},{4,6},{5,7},{6,4},{7,5},{8,10},{9,11},{10,... | collective-permute-start | bytes 1179656 | tf_op jit(solution)/shard_map/ppermute | solution.py:668
  515.1 26.5 %collective-permute-start.40 = (bf16[128,1536]{1,0:T(8,128)(2,1)S(1)}, bf16[128,1536]{1,0:T(8,128)(2,1)S(1)}, u32[]{:S(2)}, u32[]{:S(2)}) collective-permute-start(bf16[128,1536]{1,0:T(8,128)(2,1)S(1)} %add_convert_fusion.2), channel_id=1, source_target_pairs={{0,2},{1,3},{2,0},{3,1},{4,6},{5,7},{6,4},{7,5},{8,10},{9,11},{10,... | collective-permute-start | bytes 1179656 | tf_op jit(solution)/shard_map/ppermute | solution.py:668
  515.8 33.5 %collective-permute-start.38 = (bf16[128,1536]{1,0:T(8,128)(2,1)S(1)}, bf16[128,1536]{1,0:T(8,128)(2,1)S(1)}, u32[]{:S(2)}, u32[]{:S(2)}) collective-permute-start(bf16[128,1536]{1,0:T(8,128)(2,1)S(1)} %add_convert_fusion.3), channel_id=1, source_target_pairs={{0,2},{1,3},{2,0},{3,1},{4,6},{5,7},{6,4},{7,5},{8,10},{9,11},{10,... | collective-permute-start | bytes 1179656 | tf_op jit(solution)/shard_map/ppermute | solution.py:668
  553.9 78.6 %all-to-all-start.1 = ((bf16[8,64,1536]{2,1,0:T(8,128)(2,1)}), bf16[8,64,1536]{2,1,0:T(8,128)(2,1)S(1)}, u32[]{:S(2)}, u32[]{:S(2)}) async-start(bf16[8,64,1536]{2,1,0:T(8,128)(2,1)} %multiply_convert_fusion), calls=%async_computation.1 | async-start | bytes 3145728 | tf_op jit(solution)/shard_map/all_to_all | solution.py:827
  564.7 67.8 %collective-permute-start.49 = (f32[144,128]{1,0:T(8,128)S(1)}, f32[144,128]{1,0:T(8,128)S(1)}, u32[]{:S(2)}, u32[]{:S(2)}) collective-permute-start(f32[144,128]{1,0:T(8,128)S(1)} %maximum_bitcast_fusion.2), channel_id=1, source_target_pairs={{0,4},{4,0},{8,12},{12,8},{16,20},{20,16},{24,28},{28,24},{1,5},{5... | collective-permute-start | bytes 221192 | tf_op jit(solution)/shard_map/ppermute | solution.py:651
  632.4 17.9 %collective-permute-start.45 = (bf16[8,64,1536]{2,1,0:T(8,128)(2,1)S(1)}, bf16[8,64,1536]{2,1,0:T(8,128)(2,1)S(1)}, u32[]{:S(2)}, u32[]{:S(2)}) collective-permute-start(bf16[8,64,1536]{2,1,0:T(8,128)(2,1)S(1)} %all-to-all-done.1), channel_id=1, source_target_pairs={{0,1},{1,0},{2,3},{3,2},{4,5},{5,4},{6,7},{7,6},{8,9},{9,8},{10,11... | collective-permute-start | bytes 4718600 | tf_op jit(solution)/shard_map/ppermute | solution.py:673
  632.5 5.7 collective-permute-start.50
  638.1 6.1 collective-permute-start.51
  812.6 11.8 %collective-permute-start.53 = (f32[2,192,256]{2,1,0:T(8,128)}, f32[2,192,256]{2,1,0:T(8,128)}, u32[]{:S(2)}, u32[]{:S(2)}) collective-permute-start(f32[2,192,256]{2,1,0:T(8,128)} %fusion.124), channel_id=1, source_target_pairs={{0,2},{1,3},{2,0},{3,1},{4,6},{5,7},{6,4},{7,5},{8,10},{9,11},{10,... | collective-permute-start | bytes 1179656 | tf_op jit(solution)/shard_map/ppermute | solution.py:651
  (103 other events, 1178.6 us)
Sparse Core Ops, SparseCore 0:
  356.5 67.3 reduce-scatter.10
  475.3 67.1 reduce-scatter.8
  546.2 145.5 reduce-scatter.6
  695.3 111.5 reduce-scatter.4

commit v2 on v1

v2 whole, which is shorter than its diff:
```python
import functools

import jax
import jax.numpy as jnp
from jax import lax
from jax.experimental import pallas as pl
from jax.experimental.pallas import tpu as pltpu
from jax.sharding import PartitionSpec as P

P_SIZE = 64
Q = 256
GC = 256
HG = GC // P_SIZE
LANES = 128
EPS = 1e-05
CHUNKS = 1
VMEM_LIMIT = 56 * 1024 * 1024

F32 = jnp.float32
BF16 = jnp.bfloat16


def nn(a, b):
    return jnp.dot(a, b, preferred_element_type=F32)


def nt(a, b):
    return lax.dot_general(a, b, (((1,), (1,)), ((), ())), preferred_element_type=F32)


def tn(a, b):
    return lax.dot_general(a, b, (((0,), (0,)), ((), ())), preferred_element_type=F32)


def exact(a, b):
    return jnp.dot(a, b, preferred_element_type=F32, precision=lax.Precision.HIGHEST)


def sigmoid(v):
    return 1.0 / (1.0 + jnp.exp(-v))


def softplus(v):
    return jnp.maximum(v, 0.0) + jnp.log1p(jnp.exp(-jnp.abs(v)))


def triangle(lower):
    rows = lax.broadcasted_iota(jnp.int32, (Q, Q), 0)
    cols = lax.broadcasted_iota(jnp.int32, (Q, Q), 1)
    return rows >= cols if lower else cols >= rows


def row_mean(v):
    return jnp.mean(v, axis=1, keepdims=True)


def col_sum(v):
    return jnp.sum(v, axis=0, keepdims=True)


def join_halves(dst, mine, theirs, core, half):
    width = mine[0].shape[-1]
    for m in range(Q // (2 * half)):
        rows = slice(half * m, half * m + half)
        for terms, side in ((mine, core), (theirs, 1 - core)):
            total = terms[0][rows, :].astype(F32)
            for term in terms[1:]:
                total = total + term[rows, :].astype(F32)
            dst[pl.ds(pl.multiple_of(2 * half * m + half * side, 8), half), :width] = total


def split_halves(src, keep, send, core, half):
    width = keep.shape[-1]
    for m in range(Q // (2 * half)):
        own = pl.multiple_of(2 * half * m + half * core, 8)
        keep[half * m : half * m + half, :] = src[pl.ds(own, half), :width].astype(keep.dtype)
        if send is not None:
            other = pl.multiple_of(2 * half * m + half * (1 - core), 8)
            send[half * m : half * m + half, :] = src[pl.ds(other, half), :width].astype(send.dtype)


def spread(per_head):
    rows = per_head.shape[0]
    lane = lax.broadcasted_iota(jnp.int32, (rows, LANES), 1)
    tiles = []
    for q in range(GC // LANES):
        left = jnp.broadcast_to(per_head[:, 2 * q : 2 * q + 1], (rows, LANES))
        right = jnp.broadcast_to(per_head[:, 2 * q + 1 : 2 * q + 2], (rows, LANES))
        tiles.append(jnp.where(lane < P_SIZE, left, right))
    return jnp.concatenate(tiles, axis=1)


def to_group(per_head, group):
    return pltpu.roll(per_head, lax.rem(LANES - group * HG, LANES), 1)


def skip_row(heads_p, group):
    return spread(to_group(jnp.broadcast_to(heads_p[2:3, :], (8, LANES)), group))[0:1, :]


def head_part(tile, parity):
    lane = lax.broadcasted_iota(jnp.int32, tile.shape, 1)
    return jnp.where((lane < P_SIZE) == (parity == 0), tile, jnp.zeros_like(tile))


def gather_heads(acc, cols, group):
    lane = lax.broadcasted_iota(jnp.int32, (cols.shape[0], LANES), 1)
    for j in range(HG):
        tile = head_part(cols[:, (j // 2) * LANES : (j // 2 + 1) * LANES], j % 2)
        total = jnp.sum(tile, axis=1, keepdims=True)
        acc = acc + jnp.where(lane == group * HG + j, total, 0.0)
    return acc


def conv_rows(buf, taps):
    out = taps[4:5, :] + taps[0:1, :] * buf[5 : 5 + Q, :]
    for k in range(1, 4):
        out = out + taps[k : k + 1, :] * buf[5 + k : 5 + k + Q, :]
    return out


def forward_kernel(first_layer, fresh, n_skip, l, half, base, inner, scal, *refs):
    it = iter(refs)
    if not first_layer:
        hid_prev = next(it)
    count = 1 if first_layer else 2
    mine = [next(it) for _ in range(count)]
    theirs = [next(it) for _ in range(count)]
    gains = next(it)
    w_gate, w_value, w_state, w_step, w_out = (next(it) for _ in range(5))
    taps_v, taps_s, heads_p, gain_in = (next(it) for _ in range(4))
    if not fresh:
        h_in, vt_in, st_in = (next(it) for _ in range(3))
    for _ in range(n_skip):
        next(it)
    hid_out, low_out, u_out = next(it), next(it), next(it)
    gate_out, vin_out, cv_out, y_out, sin_out, cs_out, dt_out, hs_out = (next(it) for _ in range(8))
    h_last, vt_last, st_last, keep, send = (next(it) for _ in range(5))
    buf, acc, sq, vbuf, sbuf, b_s, c_s, bt_s, s_s, step_s, cum_s, cumt_s = (
        next(it) for _ in range(12)
    )
    gain = gains[l : l + 1, :]
    bias, decay_log = heads_p[0:1, :], heads_p[1:2, :]

    i, g = pl.program_id(0), pl.program_id(1)
    core = scal[0]
    width = low_out.shape[1]

    @pl.when(g == 0)
    def _():
        @pl.when(i == 0)
        def _():
            if fresh:
                h_last[...] = jnp.zeros_like(h_last)
                vt_last[...] = jnp.zeros_like(vt_last)
                st_last[...] = jnp.zeros_like(st_last)
            else:
                h_last[...] = h_in[...]
                vt_last[...] = vt_in[...]
                st_last[...] = st_in[...]

        join_halves(buf, mine, theirs, core, half)
        if first_layer:
            token = base + i * Q + lax.broadcasted_iota(jnp.int32, (Q, 1), 0)
            hid = jnp.where(token < scal[1], buf[:, :width], 0.0)
        else:
            total = buf[:, width : width + 1] + buf[:, width + P_SIZE : width + P_SIZE + 1]
            hid = hid_prev[...] + lax.rsqrt(total / inner + EPS) * buf[:, :width]
        hid_out[...] = hid
        low_out[...] = (hid * lax.rsqrt(row_mean(hid * hid) + EPS) * gain).astype(BF16)
        low = low_out[...]
        s_in = nn(low, w_state[...])
        sin_out[...] = s_in.astype(BF16)
        sbuf[0:8, :] = st_last[...]
        sbuf[8 : 8 + Q, :] = s_in
        st_last[...] = s_in[Q - 8 : Q, :]
        cs = conv_rows(sbuf, taps_s)
        cs_out[...] = cs
        states = cs * sigmoid(cs)
        b_val, c_val = states[:, :LANES], states[:, LANES:]
        b_s[...] = b_val.astype(BF16)
        c_s[...] = c_val.astype(BF16)
        bt_s[...] = b_val.T.astype(BF16)
        s_s[...] = nt(c_s[...], b_s[...])
        dt = nn(low, w_step[...])
        dt_out[...] = dt
        step = softplus(dt + bias)
        cum = -exact(triangle(True).astype(F32), step * jnp.exp(decay_log))
        step_s[...] = step
        cum_s[...] = cum
        cumt_s[...] = cum.T
        acc[...] = jnp.zeros_like(acc)
        sq[...] = jnp.zeros_like(sq)

    low = low_out[...]
    gate = nn(low, w_gate[...])
    gate_out[...] = gate
    v_in = nn(low, w_value[...])
    vin_out[...] = v_in.astype(BF16)
    vbuf[0:8, :] = vt_last[g]
    vbuf[8 : 8 + Q, :] = v_in
    vt_last[g] = v_in[Q - 8 : Q, :]
    cv = conv_rows(vbuf, taps_v)
    cv_out[...] = cv
    val = cv * sigmoid(cv)
    cum_g = to_group(cum_s[...], g)
    step_g = to_group(step_s[...], g)
    cum_e = spread(cum_g)
    scaled = spread(step_g) * val
    scaled_b = scaled.astype(BF16)
    h_enter = h_last[g]
    hs_out[...] = h_enter
    y = nn(c_s[...], h_enter.astype(BF16)) * jnp.exp(cum_e)
    end = cum_e[Q - 1 : Q, :]
    to_end = (scaled * jnp.exp(end - cum_e)).astype(BF16)
    h_last[g] = h_enter * jnp.exp(end) + nn(bt_s[...], to_end)
    causal = triangle(True)
    tiles = []
    for q in range(GC // LANES):
        tile = jnp.zeros((Q, LANES), F32)
        for parity in range(2):
            j = 2 * q + parity
            gaps = cum_g[:, j : j + 1] - cumt_s[pl.ds(g * HG + j, 1), :]
            weights = jnp.exp(jnp.where(causal, gaps, -1e30))
            mix = (s_s[...] * weights).astype(BF16)
            tile = tile + nn(mix, head_part(scaled_b[:, q * LANES : (q + 1) * LANES], parity))
        tiles.append(tile)
    y = y + jnp.concatenate(tiles, axis=1)
    y_out[...] = y
    gated = (y + skip_row(heads_p, g) * val) * (gate * sigmoid(gate))
    sq[...] += jnp.sum(gated * gated, axis=1, keepdims=True)
    u_out[...] = (gated * gain_in[...]).astype(BF16)
    acc[:, :width] += nt(u_out[...], w_out[...])

    @pl.when(g == pl.num_programs(1) - 1)
    def _():
        acc[:, width:] = jnp.broadcast_to(sq[:, 0:1], (Q, LANES))
        split_halves(acc, keep, send, core, half)


def norm_kernel(top, bottom, fresh, n_skip, l, half, base, inner, scal, *refs):
    it = iter(refs)
    hid_ref = next(it)
    if top:
        cot = next(it)
    else:
        dh_prev = next(it)
        dl_mine, dl_theirs = ([next(it), next(it)] for _ in range(2))
    br_mine, br_theirs = ([next(it), next(it)] for _ in range(2))
    gains = next(it)
    if not fresh:
        gain_c = next(it)
    for _ in range(n_skip):
        next(it)
    if top:
        result = next(it)
    dh_out, gb_out, gbs_out, rows_out, gain_acc, buf, low = (next(it) for _ in range(7))
    core = scal[0]
    width = gb_out.shape[1]
    gain = gains[l + 1 : l + 2, :]

    @pl.when(pl.program_id(0) == 0)
    def _():
        gain_acc[...] = jnp.zeros_like(gain_acc) if fresh else gain_c[...]

    join_halves(buf, br_mine, br_theirs, core, half)
    total = buf[:, width : width + 1] + buf[:, width + P_SIZE : width + P_SIZE + 1]
    scale = lax.rsqrt(total / inner + EPS)
    hid = hid_ref[...]
    if top:
        hid = hid + scale * buf[:, :width]
    r = lax.rsqrt(row_mean(hid * hid) + EPS)
    normed = hid * r
    if top:
        token = base + pl.program_id(0) * Q + lax.broadcasted_iota(jnp.int32, (Q, 1), 0)
        valid = token < scal[1]
        result[...] = jnp.where(valid, normed * gain, 0.0).astype(BF16)
        upper = jnp.where(valid, cot[...].astype(F32), 0.0)
    else:
        join_halves(low, dl_mine, dl_theirs, core, half)
        upper = low[...]
    gain_acc[0:1, :] += col_sum(upper * normed)
    dn = upper * gain
    dh = r * (dn - normed * row_mean(dn * normed))
    if not top:
        dh = dh + dh_prev[...]
    gb = dh.astype(BF16)
    gb_out[...] = gb
    gbs_out[...] = (dh * scale).astype(BF16)
    stat = jnp.sum(gb.astype(F32) * buf[:, :width], axis=1, keepdims=True)
    lane = lax.broadcasted_iota(jnp.int32, (Q, LANES), 1)
    rows_out[...] = jnp.where(lane == 0, scale, scale * scale * scale * stat / inner)
    if bottom:
        low[...] = dh
        split_halves(low, dh_out, None, core, half)
    else:
        dh_out[...] = dh


def backward_kernel(fresh, n_skip, l, half, scal, *refs):
    it = iter(refs)
    gb_ref, rows_ref = next(it), next(it)
    w_gate, w_value, w_state, w_step, w_out = (next(it) for _ in range(5))
    taps_v, taps_s, heads_p, gain_in = (next(it) for _ in range(4))
    gate_ref, vin_ref, cv_ref, y_ref, sin_ref, cs_ref, dt_ref, hs_ref = (next(it) for _ in range(8))
    if not fresh:
        dh_c, av_c, as_c, ah_c = (next(it) for _ in range(4))
    for _ in range(n_skip):
        next(it)
    dgate_out, dval_out, dst_out, dstep_out = (next(it) for _ in range(4))
    keep, send = next(it), next(it)
    d_state, acc_v, acc_s, acc_h = (next(it) for _ in range(4))
    acc, dst_s, db_s, dc_s, vbuf, sbuf = (next(it) for _ in range(6))
    b_s, c_s, ct_s, st_s, step_s, cum_s, cumt_s, dcum_s, dstep_s, end_s = (
        next(it) for _ in range(10)
    )

    i, g = pl.program_id(0), pl.program_id(1)
    core = scal[0]
    bias, decay_log = heads_p[0:1, :], heads_p[1:2, :]

    @pl.when(g == 0)
    def _():
        @pl.when(i == 0)
        def _():
            if fresh:
                d_state[...] = jnp.zeros_like(d_state)
                acc_v[...] = jnp.zeros_like(acc_v)
                acc_s[...] = jnp.zeros_like(acc_s)
                acc_h[...] = jnp.zeros_like(acc_h)
            else:
                d_state[...] = dh_c[...]
                acc_v[...] = av_c[...]
                acc_s[...] = as_c[...]
                acc_h[...] = ah_c[...]

        cs = cs_ref[...]
        states = cs * sigmoid(cs)
        b_val, c_val = states[:, :LANES], states[:, LANES:]
        b_s[...] = b_val.astype(BF16)
        c_s[...] = c_val.astype(BF16)
        ct_s[...] = c_val.T.astype(BF16)
        st_s[...] = nt(b_s[...], c_s[...])
        step = softplus(dt_ref[...] + bias)
        cum = -exact(triangle(True).astype(F32), step * jnp.exp(decay_log))
        step_s[...] = step
        cum_s[...] = cum
        cumt_s[...] = cum.T
        acc[...] = jnp.zeros_like(acc)
        dst_s[...] = jnp.zeros_like(dst_s)
        db_s[...] = jnp.zeros_like(db_s)
        dc_s[...] = jnp.zeros_like(dc_s)
        dcum_s[...] = jnp.zeros_like(dcum_s)
        dstep_s[...] = jnp.zeros_like(dstep_s)
        end_s[...] = jnp.zeros_like(end_s)

    scale, coef = rows_ref[:, 0:1], rows_ref[:, 1:2]
    skip = skip_row(heads_p, g)
    d_go = nn(gb_ref[...], w_out[...])
    cv = cv_ref[...]
    sig_v = sigmoid(cv)
    val = cv * sig_v
    gate = gate_ref[...]
    sig_g = sigmoid(gate)
    silu_g = gate * sig_g
    y = y_ref[...]
    mixed = y + skip * val
    gated = mixed * silu_g
    normed_gate = gated * scale
    acc_v[g, 5:6, :] += col_sum(d_go * normed_gate)
    d_gated = scale * (d_go * gain_in[...]) - gated * coef
    d_gate = (d_gated * mixed * (sig_g * (1.0 + gate * (1.0 - sig_g)))).astype(BF16)
    dgate_out[...] = d_gate
    d_y = d_gated * silu_g
    acc_v[g, 6:7, :] += col_sum(d_y * val)
    d_y_b = d_y.astype(BF16)
    d_y_r = d_y_b.astype(F32)

    cum_g = to_group(cum_s[...], g)
    step_g = to_group(step_s[...], g)
    cum_e = spread(cum_g)
    step_e = spread(step_g)
    scaled = step_e * val
    scaled_b = scaled.astype(BF16)
    scaled_r = scaled_b.astype(F32)
    causal_t = triangle(False)
    tiles = []
    for q in range(GC // LANES):
        tile = jnp.zeros((Q, LANES), F32)
        x_tile = scaled_b[:, q * LANES : (q + 1) * LANES]
        g_tile = d_y_b[:, q * LANES : (q + 1) * LANES]
        for parity in range(2):
            j = 2 * q + parity
            gaps = cumt_s[pl.ds(g * HG + j, 1), :] - cum_g[:, j : j + 1]
            weights = jnp.exp(jnp.where(causal_t, gaps, -1e30))
            mix = (st_s[...] * weights).astype(BF16)
            part = head_part(g_tile, parity)
            tile = tile + nn(mix, part)
            dst_s[...] += nt(x_tile, part) * weights
        tiles.append(tile)
    d_x = jnp.concatenate(tiles, axis=1)
    end = cum_e[Q - 1 : Q, :]
    exp_end = jnp.exp(end)
    to_end = jnp.exp(end - cum_e)
    h_enter = hs_ref[...]
    d_out = d_state[g]
    d_out_b = d_out.astype(BF16)
    d_across = (d_y * jnp.exp(cum_e)).astype(BF16)
    dc_s[...] += nt(d_across, h_enter.astype(BF16))
    db_s[...] += nt((scaled * to_end).astype(BF16), d_out_b)
    d_x_end = to_end * nn(b_s[...], d_out_b)
    d_state[g] = nn(ct_s[...], d_across) + exp_end * d_out
    end_s[...] = gather_heads(
        end_s[...],
        jnp.broadcast_to(col_sum(scaled_r * d_x_end) + exp_end * col_sum(h_enter * d_out), (8, GC)),
        g,
    )
    d_x = d_x + d_x_end
    dcum_s[...] = gather_heads(dcum_s[...], d_y_r * y - scaled_r * d_x, g)
    dstep_s[...] = gather_heads(dstep_s[...], val * d_x, g)
    d_val = skip * d_y + step_e * d_x
    d_cv = d_val * (sig_v * (1.0 + cv * (1.0 - sig_v)))
    vbuf[0:Q, :] = d_cv
    vbuf[Q : Q + 8, :] = acc_v[g, 8:16, :]
    acc_v[g, 8:16, :] = d_cv[0:8, :]
    v_in = vin_ref[...].astype(F32)
    d_vin = taps_v[3:4, :] * d_cv
    acc_v[g, 3:4, :] += col_sum(v_in * d_cv)
    acc_v[g, 4:5, :] += col_sum(d_cv)
    for k in range(3):
        shifted = vbuf[3 - k : 3 - k + Q, :]
        d_vin = d_vin + taps_v[k : k + 1, :] * shifted
        acc_v[g, k : k + 1, :] += col_sum(v_in * shifted)
    d_vin_b = d_vin.astype(BF16)
    dval_out[...] = d_vin_b
    acc[...] += nt(d_gate, w_gate[...]) + nt(d_vin_b, w_value[...])

    @pl.when(g == pl.num_programs(1) - 1)
    def _():
        decay = jnp.exp(decay_log)
        step = step_s[...]
        d_log = exact(triangle(False).astype(F32), dcum_s[...]) + end_s[0:1, :]
        acc_h[1:2, :] += col_sum(d_log * step) * (-decay)
        d_step = (dstep_s[...] - decay * d_log) * sigmoid(dt_ref[...] + bias)
        acc_h[0:1, :] += col_sum(d_step)
        d_step_b = d_step.astype(BF16)
        dstep_out[...] = d_step_b
        d_scores = dst_s[...]
        d_b = db_s[...] + nn(d_scores.astype(BF16), c_s[...])
        d_c = dc_s[...] + nn(d_scores.T.astype(BF16), b_s[...])
        cs = cs_ref[...]
        sig_s = sigmoid(cs)
        d_cs = jnp.concatenate([d_b, d_c], axis=1) * (sig_s * (1.0 + cs * (1.0 - sig_s)))
        sbuf[0:Q, :] = d_cs
        sbuf[Q : Q + 8, :] = acc_s[8:16, :]
        acc_s[8:16, :] = d_cs[0:8, :]
        s_in = sin_ref[...].astype(F32)
        d_sin = taps_s[3:4, :] * d_cs
        acc_s[3:4, :] += col_sum(s_in * d_cs)
        acc_s[4:5, :] += col_sum(d_cs)
        for k in range(3):
            shifted = sbuf[3 - k : 3 - k + Q, :]
            d_sin = d_sin + taps_s[k : k + 1, :] * shifted
            acc_s[k : k + 1, :] += col_sum(s_in * shifted)
        d_sin_b = d_sin.astype(BF16)
        dst_out[...] = d_sin_b
        acc[...] += nt(d_sin_b, w_state[...]) + nt(d_step_b, w_step[...])
        split_halves(acc, keep, send, core, half)


def weight_kernel(half, bit, pieces, scal, a_ref, *refs):
    ds = refs[:pieces]
    at = 0
    if bit is None:
        out = refs[-1]
        for d in ds:
            out[:, at : at + d.shape[1]] = tn(a_ref[...], d[...]).astype(BF16)
            at += d.shape[1]
        return
    keep, send, buf = refs[-3:]
    for d in ds:
        buf[:, at : at + d.shape[1]] = tn(a_ref[...], d[...])
        at += d.shape[1]
    mine = scal[bit]
    for m in range(buf.shape[0] // (2 * half)):
        own = pl.multiple_of(2 * half * m + half * mine, 8)
        other = pl.multiple_of(2 * half * m + half * (1 - mine), 8)
        keep[half * m : half * m + half, :] = buf[pl.ds(own, half), :].astype(BF16)
        send[half * m : half * m + half, :] = buf[pl.ds(other, half), :].astype(BF16)


def layer_specs(l, width):
    return [
        pl.BlockSpec((None, width, GC), lambda i, g: (l, 0, g)),
        pl.BlockSpec((None, width, GC), lambda i, g: (l, 0, g)),
        pl.BlockSpec((None, width, 2 * LANES), lambda i, g: (l, 0, 0)),
        pl.BlockSpec((None, width, LANES), lambda i, g: (l, 0, 0)),
        pl.BlockSpec((None, width, GC), lambda i, g: (l, 0, g)),
        pl.BlockSpec((None, 5, GC), lambda i, g: (l, 0, g)),
        pl.BlockSpec((None, 5, 2 * LANES), lambda i, g: (l, 0, 0)),
        pl.BlockSpec((None, 8, LANES), lambda i, g: (l, 0, 0)),
        pl.BlockSpec((None, 1, GC), lambda i, g: (l, 0, g)),
    ]


class Call:
    def __init__(self):
        self.in_specs, self.args, self.out_specs, self.out_shape = [], [], [], []
        self.aliases, self.tail = {}, []

    def take(self, spec, arg):
        self.in_specs.append(spec)
        self.args.append(arg)

    def give(self, spec, dims, dtype=F32, into=None):
        if into is not None:
            self.tail.append((into, len(self.out_specs)))
        self.out_specs.append(spec)
        self.out_shape.append(jax.ShapeDtypeStruct(dims, dtype))

    def run(self, kernel, grid, scratch, after, micros, name):
        for arg, out in self.tail:
            self.aliases[len(self.args)] = out
            self.take(pl.BlockSpec(memory_space=pl.ANY), arg)
        for arg in after:
            self.take(pl.BlockSpec(memory_space=pl.ANY), arg)
        return pl.pallas_call(
            functools.partial(kernel, len(self.tail) + len(after)),
            grid=grid,
            in_specs=self.in_specs,
            out_specs=self.out_specs,
            out_shape=self.out_shape,
            scratch_shapes=scratch,
            input_output_aliases=self.aliases,
            compiler_params=pltpu.CompilerParams(
                dimension_semantics=("arbitrary",) * len(grid), vmem_limit_bytes=VMEM_LIMIT
            ),
            cost_estimate=pl.CostEstimate(
                flops=int(micros * 1.1e9), bytes_accessed=1_000_000, transcendentals=0
            ),
            name=name,
        )(*self.args)


def full(dims, count):
    return pl.BlockSpec(dims, lambda *at: (0,) * count)


def smem():
    return pl.BlockSpec(memory_space=pltpu.SMEM)


def forward_call(l, chunk, chunks, half, inner, rows_all, scal, hid_prev, halves, halves_at, gains, weights, carry, filled, after):
    first, fresh = hid_prev is None, carry is None
    width = weights[0].shape[1]
    groups = weights[0].shape[2] // GC
    cols = groups * GC
    rows = chunks * Q

    def block(h, w, at=chunk):
        return pl.BlockSpec((h, w), lambda i, g: (at + i, 0))

    def grouped(h, w, at=chunk):
        return pl.BlockSpec((h, w), lambda i, g: (at + i, g))

    call = Call()
    call.take(smem(), scal)
    if not first:
        call.take(block(Q, width), hid_prev)
    for term in halves:
        call.take(block(Q // 2, term.shape[1], halves_at), term)
    call.take(full(gains.shape, 2), gains)
    for spec, arg in zip(layer_specs(l, width), weights):
        call.take(spec, arg)
    carry_shapes = [(groups, LANES, GC), (groups, 8, GC), (8, 2 * LANES)]
    if not fresh:
        for dims, arg in zip(carry_shapes, carry):
            call.take(full(dims, len(dims)), arg)
    into = filled if filled is not None else (None,) * 3
    call.give(block(Q, width), (rows_all, width), F32, into[0])
    call.give(block(Q, width), (rows_all, width), BF16, into[1])
    call.give(grouped(Q, GC), (rows_all, cols), BF16, into[2])
    call.give(grouped(Q, GC, 0), (rows, cols))
    call.give(grouped(Q, GC, 0), (rows, cols), BF16)
    call.give(grouped(Q, GC, 0), (rows, cols))
    call.give(grouped(Q, GC, 0), (rows, cols))
    call.give(block(Q, 2 * LANES, 0), (rows, 2 * LANES), BF16)
    call.give(block(Q, 2 * LANES, 0), (rows, 2 * LANES))
    call.give(block(Q, LANES, 0), (rows, LANES))
    call.give(
        pl.BlockSpec((None, None, LANES, GC), lambda i, g: (i, g, 0, 0)), (chunks, groups, LANES, GC)
    )
    for dims in carry_shapes:
        call.give(full(dims, len(dims)), dims)
    for _ in range(2):
        call.give(block(Q // 2, width + LANES, 0), (rows // 2, width + LANES))
    scratch = [
        pltpu.VMEM((Q, width + LANES), F32),
        pltpu.VMEM((Q, width + LANES), F32),
        pltpu.VMEM((Q, LANES), F32),
        pltpu.VMEM((Q + 8, GC), F32),
        pltpu.VMEM((Q + 8, 2 * LANES), F32),
        pltpu.VMEM((Q, LANES), BF16),
        pltpu.VMEM((Q, LANES), BF16),
        pltpu.VMEM((LANES, Q), BF16),
        pltpu.VMEM((Q, Q), F32),
        pltpu.VMEM((Q, LANES), F32),
        pltpu.VMEM((Q, LANES), F32),
        pltpu.VMEM((LANES, Q), F32),
    ]

    def kernel(n_skip, *refs):
        forward_kernel(first, fresh, n_skip, l, half, chunk * Q, inner, *refs)

    outs = call.run(kernel, (chunks, groups), scratch, after, 12 * chunks, "layer_forward")
    return tuple(outs[:3]), tuple(outs[3:11]), tuple(outs[11:14]), outs[14], outs[15]


def norm_call(l, top, bottom, chunk, chunks, half, inner, scal, hid, lead, lows, branch, gains, gain_c, filled, after):
    rows_all, width = hid.shape
    fresh = gain_c is None

    def block(h, w, at=chunk):
        return pl.BlockSpec((h, w), lambda i: (at + i, 0))

    call = Call()
    call.take(smem(), scal)
    call.take(block(Q, width), hid)
    call.take(block(Q, width), lead)
    if not top:
        for side in lows:
            call.take(block(Q // 2, width, 0), side)
    for side in branch:
        call.take(block(Q // 2, width + LANES, 0), side)
    call.take(full(gains.shape, 2), gains)
    if not fresh:
        call.take(full((8, width), 2), gain_c)
    into = filled if filled is not None else (None,) * 5
    if top:
        call.give(block(Q, width), (rows_all, width), BF16, into[4])
    part = 2 if bottom else 1
    call.give(block(Q // part, width), (rows_all // part, width), F32, into[0])
    call.give(block(Q, width), (rows_all, width), BF16, into[1])
    call.give(block(Q, width), (rows_all, width), BF16, into[2])
    call.give(block(Q, LANES), (rows_all, LANES), F32, into[3])
    call.give(full((8, width), 2), (8, width))
    scratch = [pltpu.VMEM((Q, width + LANES), F32), pltpu.VMEM((Q, width), F32)]

    def kernel(n_skip, *refs):
        norm_kernel(top, bottom, fresh, n_skip, l, half, chunk * Q, inner, *refs)

    outs = call.run(kernel, (chunks,), scratch, after, 4 * chunks, "norm_backward")
    result = None
    if top:
        result, outs = outs[0], outs[1:]
    return tuple(outs[:4]) + (result,), outs[4]


def backward_call(l, chunk, chunks, half, scal, gb, rows_f, weights, saved, carry, filled, after):
    width = weights[0].shape[1]
    groups = weights[0].shape[2] // GC
    cols = groups * GC
    rows, rows_all = chunks * Q, gb.shape[0]
    fresh = carry is None

    def block(h, w, at=chunk):
        return pl.BlockSpec((h, w), lambda i, g: (at + chunks - 1 - i, 0))

    def grouped(h, w, at=chunk):
        return pl.BlockSpec((h, w), lambda i, g: (at + chunks - 1 - i, g))

    call = Call()
    call.take(smem(), scal)
    call.take(block(Q, width), gb)
    call.take(block(Q, LANES), rows_f)
    for spec, arg in zip(layer_specs(l, width), weights):
        call.take(spec, arg)
    specs = [
        grouped(Q, GC, 0),
        grouped(Q, GC, 0),
        grouped(Q, GC, 0),
        grouped(Q, GC, 0),
        block(Q, 2 * LANES, 0),
        block(Q, 2 * LANES, 0),
        block(Q, LANES, 0),
        pl.BlockSpec((None, None, LANES, GC), lambda i, g: (chunks - 1 - i, g, 0, 0)),
    ]
    for spec, arg in zip(specs, saved):
        call.take(spec, arg)
    carry_shapes = [(groups, LANES, GC), (groups, 16, GC), (16, 2 * LANES), (8, LANES)]
    if not fresh:
        for dims, arg in zip(carry_shapes, carry):
            call.take(full(dims, len(dims)), arg)
    into = filled if filled is not None else (None,) * 4
    call.give(grouped(Q, GC), (rows_all, cols), BF16, into[0])
    call.give(grouped(Q, GC), (rows_all, cols), BF16, into[1])
    call.give(block(Q, 2 * LANES), (rows_all, 2 * LANES), BF16, into[2])
    call.give(block(Q, LANES), (rows_all, LANES), BF16, into[3])
    for _ in range(2):
        call.give(block(Q // 2, width, 0), (rows // 2, width))
    for dims in carry_shapes:
        call.give(full(dims, len(dims)), dims)
    scratch = [
        pltpu.VMEM((Q, width), F32),
        pltpu.VMEM((Q, Q), F32),
        pltpu.VMEM((Q, LANES), F32),
        pltpu.VMEM((Q, LANES), F32),
        pltpu.VMEM((Q + 8, GC), F32),
        pltpu.VMEM((Q + 8, 2 * LANES), F32),
        pltpu.VMEM((Q, LANES), BF16),
        pltpu.VMEM((Q, LANES), BF16),
        pltpu.VMEM((LANES, Q), BF16),
        pltpu.VMEM((Q, Q), F32),
        pltpu.VMEM((Q, LANES), F32),
        pltpu.VMEM((Q, LANES), F32),
        pltpu.VMEM((LANES, Q), F32),
        pltpu.VMEM((Q, LANES), F32),
        pltpu.VMEM((Q, LANES), F32),
        pltpu.VMEM((8, LANES), F32),
    ]

    def kernel(n_skip, *refs):
        backward_kernel(fresh, n_skip, l, half, *refs)

    outs = call.run(kernel, (chunks, groups), scratch, after, 16 * chunks, "layer_backward")
    return tuple(outs[:4]), outs[4], outs[5], tuple(outs[6:])


def weight_call(a, ds, piece, scal, bit, after):
    tokens, width = a.shape
    total = sum(d.shape[1] for d in ds)
    unit = piece * (bit or 1)
    step = 2 * unit
    while step < 384 and width % (2 * step) == 0:
        step *= 2
    call = Call()
    call.take(smem(), scal)
    call.take(pl.BlockSpec((tokens, step), lambda r: (0, r)), a)
    for d in ds:
        call.take(full(d.shape, 2), d)
    parts = 1 if bit is None else 2
    for _ in range(parts):
        call.give(pl.BlockSpec((step // parts, total), lambda r: (r, 0)), (width // parts, total), BF16)
    scratch = [] if bit is None else [pltpu.VMEM((step, total), F32)]

    def kernel(n_skip, *refs):
        weight_kernel(unit, None if bit is None else place_of(bit), len(ds), *refs)

    return call.run(kernel, (width // step,), scratch, after, total // 128, "weight_grad")


def pack_call(rows, wide, moves, after):
    call = Call()
    for src, _, _ in moves:
        call.take(pl.BlockSpec(memory_space=pltpu.VMEM), src)
    call.give(pl.BlockSpec(memory_space=pltpu.VMEM), (rows, wide))

    def kernel(n_skip, *refs):
        out = refs[-1]
        out[...] = jnp.zeros_like(out)
        for ref, (_, index, at) in zip(refs, moves):
            piece = ref[index]
            if piece.shape[1] <= wide:
                out[at : at + piece.shape[0], : piece.shape[1]] = piece
            else:
                for m in range(piece.shape[1] // wide):
                    out[at + m : at + m + 1, :] = piece[:, m * wide : (m + 1) * wide]

    return call.run(kernel, (), [], after, 2, "pack_small")[0]


def sum_call(a, b, after):
    call = Call()
    for arg in (a, b):
        call.take(pl.BlockSpec(memory_space=pltpu.VMEM), arg)
    call.give(pl.BlockSpec(memory_space=pltpu.VMEM), a.shape)

    def kernel(n_skip, x, y, *refs):
        refs[-1][...] = x[...] + y[...]

    return call.run(kernel, (), [], after, 1, "sum_small")[0]


def take_call(value, index, after):
    call = Call()
    call.take(smem(), index)
    call.take(pl.BlockSpec(memory_space=pltpu.VMEM), value)
    call.give(pl.BlockSpec(memory_space=pltpu.VMEM), value.shape, value.dtype)

    def kernel(n_skip, at, src, *refs):
        for k in range(value.shape[0]):
            refs[-1][k] = src[at[k]]

    return call.run(kernel, (), [], after, 2, "take_parts")[0]


class Butterfly:
    def __init__(self, value, steps):
        self.value, self.steps = value, list(steps)
        self.send()

    def send(self):
        if self.steps:
            self.came = swap(self.value, *self.steps.pop(0))
        else:
            self.came = None

    def step(self, after):
        self.value = sum_call(self.value, self.came, after)
        self.send()
        return self.value


def pairs(axis, bit):
    return [(i, i ^ bit) for i in range(lax.axis_size(axis))]


def swap(value, axis, bit):
    return lax.ppermute(value, axis, pairs(axis, bit))


def sum_pairs(value, axis, bit):
    return value + swap(value, axis, bit)


def place_of(bit):
    return 1 + bit.bit_length() + (bit >= 4)


class Scatter:
    def __init__(self, keep, send, piece, order):
        self.keep, self.recv, self.piece = keep, swap(send, "dp", order[0]), piece
        self.order, self.left = list(order[1:]), sorted(order[1:])

    def step(self, scal, after):
        bit = self.order.pop(0)
        unit = self.piece << self.left.index(bit)
        self.left.remove(bit)
        self.keep, send = scatter_call(self.keep, self.recv, unit, place_of(bit), scal, after)
        self.recv = swap(send, "dp", bit)
        return send


def finish_call(items, after):
    call = Call()
    count = 0
    for scatter, upper, parts in items:
        rows = scatter.keep.shape[0]
        for arg in (scatter.keep, scatter.recv):
            call.take(pl.BlockSpec(arg.shape, lambda r: (0, 0)), arg)
        for wide, at in parts:
            call.take(pl.BlockSpec((rows, wide), lambda r, j=at // wide: (0, j)), upper)
            call.give(pl.BlockSpec((2, rows, wide), lambda r: (0, 0, 0)), (2, rows, wide))
            count += 1

    def kernel(n_skip, *refs):
        it, out = iter(refs), iter(refs[len(refs) - count :])
        for _, _, parts in items:
            a, b, at = next(it), next(it), 0
            for wide, _ in parts:
                cols = slice(at, at + wide)
                dst = next(out)
                dst[0] = a[:, cols].astype(F32) + b[:, cols].astype(F32)
                dst[1] = next(it)[...].astype(F32)
                at += wide

    return call.run(kernel, (1,), [], after, 3, "finish")


def own_part(rows, half, place):
    parts = rows.reshape(-1, 2, half // 2, rows.shape[1])
    return lax.dynamic_index_in_dim(parts, place, axis=1, keepdims=False).reshape(-1, rows.shape[1])


def add_call(keep, recv, width, after):
    rows, wide = keep.shape
    call = Call()
    spec = pl.BlockSpec((rows // 2, wide), lambda r: (r, 0))
    call.take(spec, keep)
    call.take(spec, recv)
    call.give(spec, (rows, wide), BF16)

    def kernel(n_skip, a, b, *refs):
        out = refs[-1]
        total = a[...] + b[...]
        if wide == width:
            out[...] = total.astype(BF16)
        else:
            out[:, :width] = total[:, :width].astype(BF16)
            tail = total[:, width:]
            lead = tail.astype(BF16).astype(F32)
            lane = lax.broadcasted_iota(jnp.int32, tail.shape, 1)
            out[:, width:] = jnp.where(lane < P_SIZE, lead, tail - lead).astype(BF16)

    return call.run(kernel, (2,), [], after, 2, "add_pair")[0]


def add_quarter_call(keep, recv, half, scal, after):
    rows, wide = keep.shape
    unit = half // 2
    call = Call()
    call.take(smem(), scal)
    for arg in (keep, recv):
        call.take(pl.BlockSpec(memory_space=pltpu.VMEM), arg)
    call.give(pl.BlockSpec(memory_space=pltpu.VMEM), (rows // 2, wide))
    call.give(pl.BlockSpec(memory_space=pltpu.VMEM), (rows // 2, wide), BF16)

    def kernel(n_skip, place_ref, a, b, *refs):
        mine, other, buf = refs[-3:]
        place = place_ref[4]
        for m in range(rows // half):
            for dst, side in ((mine, place), (buf, 1 - place)):
                at = pl.multiple_of(half * m + unit * side, 8)
                dst[unit * m : unit * m + unit, :] = a[pl.ds(at, unit), :] + b[pl.ds(at, unit), :]
        other[...] = buf[...].astype(BF16)

    return call.run(kernel, (), [pltpu.VMEM((rows // 2, wide), F32)], after, 2, "add_quarter")


def last_call(mine, other, d_hid, x_mine, chunk, half, scal, gains, gain_c, filled, after):
    rows, wide = mine.shape
    unit = half // 2
    fresh = gain_c is None
    call = Call()
    call.take(smem(), scal)
    part = pl.BlockSpec((rows, wide), lambda r: (0, 0))
    whole = pl.BlockSpec((2 * rows, wide), lambda r: (chunk, 0))
    for spec, arg in ((part, mine), (part, other), (whole, d_hid), (whole, x_mine)):
        call.take(spec, arg)
    call.take(full(gains.shape, 2), gains)
    if not fresh:
        call.take(full((8, wide), 2), gain_c)
    call.give(pl.BlockSpec((rows, wide), lambda r: (chunk, 0)), (d_hid.shape[0] // 2, wide), BF16, filled)
    call.give(full((8, wide), 2), (8, wide))

    def kernel(n_skip, place_ref, a, b, dh_ref, x_ref, gain_ref, *refs):
        out, gain_acc, x_s, x_q, dh_q = refs[-5:]
        place = place_ref[4]
        x_s[...] = x_ref[...].astype(F32)
        for m in range(rows // unit):
            at = pl.multiple_of(half * m + unit * place, 8)
            dst = slice(unit * m, unit * m + unit)
            token = chunk * Q + (2 * half) * m + half * place_ref[0] + unit * place
            token = token + lax.broadcasted_iota(jnp.int32, (unit, 1), 0)
            x_q[dst, :] = jnp.where(token < place_ref[1], x_s[pl.ds(at, unit), :], 0.0)
            dh_q[dst, :] = jnp.where(token < place_ref[1], dh_ref[pl.ds(at, unit), :], 0.0)
        hid = x_q[...]
        r = lax.rsqrt(row_mean(hid * hid) + EPS)
        normed = hid * r
        upper = a[...] + b[...].astype(F32)
        gain_acc[...] = jnp.zeros_like(gain_acc) if fresh else refs[0][...]
        gain_acc[0:1, :] += col_sum(upper * normed)
        dn = upper * gain_ref[0:1, :]
        back = r * (dn - normed * row_mean(dn * normed))
        out[...] = (dh_q[...] + back).astype(BF16)

    scratch = [
        pltpu.VMEM((2 * rows, wide), F32),
        pltpu.VMEM((rows, wide), F32),
        pltpu.VMEM((rows, wide), F32),
    ]
    return call.run(kernel, (1,), scratch, after, 4, "norm_last")


def scatter_call(keep, recv, unit, place_at, scal, after):
    rows, wide = keep.shape
    call = Call()
    call.take(smem(), scal)
    spec = pl.BlockSpec((2 * unit, wide), lambda r: (r, 0))
    call.take(spec, keep)
    call.take(spec, recv)
    for _ in range(2):
        call.give(pl.BlockSpec((unit, wide), lambda r: (r, 0)), (rows // 2, wide), BF16)

    def kernel(n_skip, place_ref, a, b, *refs):
        own = place_ref[place_at]
        for dst, side in ((refs[-2], own), (refs[-1], 1 - own)):
            at = pl.ds(pl.multiple_of(unit * side, 16), unit)
            dst[...] = (a[at, :].astype(F32) + b[at, :].astype(F32)).astype(BF16)

    return call.run(kernel, (rows // (2 * unit),), [], after, 3, "add_scatter")


class Offload:
    def __init__(self, value):
        self.value = lax.psum_scatter(value, "dp", scatter_dimension=0, tiled=True)


class Sums:
    def __init__(self, width, half, scal):
        self.width, self.half, self.scal, self.open = width, half, scal, []

    def start(self, keep, send):
        self.open.insert(0, [keep, swap(send, "tensor", 1), None, None])

    def add(self, entry, after):
        keep, recv = entry[0], entry[1]
        own = add_call(keep, recv, self.width, after)
        other = swap(own, "tensor", 2)
        entry[2] = own
        entry[3] = (own, other, swap(own, "tensor", 1), swap(other, "tensor", 1))
        return own

    def add_quarter(self, entry, after):
        mine, other = add_quarter_call(entry[0], entry[1], self.half, self.scal, after)
        entry[2] = other
        entry[3] = (mine, swap(other, "tensor", 2))
        return other


def per_device(
    x_in,
    cotangent,
    lengths,
    deal_order,
    norm_gains,
    proj_gate,
    proj_value,
    proj_state,
    proj_step,
    proj_out,
    conv_value,
    conv_state,
    step_bias,
    decay_log,
    skip_gain,
    inner_gain,
):
    _, slot_len, width = cotangent.shape
    layers = proj_gate.shape[0]
    cols = proj_gate.shape[2]
    heads = step_bias.shape[1]
    inner = cols * lax.axis_size("tensor")
    dp = lax.axis_size("dp")
    half = x_in.shape[1] // 2
    piece = width // dp
    me = lax.axis_index("dp")
    core = lax.rem(lax.axis_index("tensor"), 2)
    length = jnp.take(lengths, lax.dynamic_index_in_dim(deal_order, me, keepdims=False))
    place = lax.axis_index("tensor") // 2
    bits = [1 << k for k in range(dp.bit_length() - 1)]
    parts = [lax.rem(me // bit, 2) for bit in bits]
    scal = jnp.stack([core, length] + parts[:2] + [place] + parts[2:]).astype(jnp.int32)

    x_half = lax.dynamic_slice_in_dim(x_in, core * half, half, axis=1)
    x_dealt = jnp.take(x_half, deal_order, axis=0)
    x_mine = lax.all_to_all(x_dealt, "dp", split_axis=0, concat_axis=0, tiled=True)
    x_mine = x_mine.reshape(slot_len // 2, width)
    x_theirs = swap(x_mine, "tensor", 1)

    heads_p = jnp.pad(
        jnp.stack([step_bias, decay_log, skip_gain], axis=1), ((0, 0), (0, 5), (0, LANES - heads))
    )
    weights = (
        proj_gate,
        proj_value,
        proj_state,
        jnp.pad(proj_step, ((0, 0), (0, 0), (0, LANES - heads))),
        proj_out,
        conv_value,
        conv_state,
        heads_p,
        inner_gain[:, None, :],
    )
    cot = cotangent.reshape(slot_len, width)
    sums = Sums(width, half, scal)
    calls = slot_len // (Q * CHUNKS)

    def due(entries, prior):
        if len(entries) > 1 and entries[1][2] is None:
            entries_add(entries[1], [prior])
        return [entries[1][2]] if len(entries) > 1 else []

    entries_add = sums.add
    filled_f, saves, branches = [], [], []
    prior = None
    for l in range(layers):
        carry, filled, save_l, branch_l = None, None, [], []
        for c in range(calls):
            if l == 0:
                lead = (None, (x_mine, x_theirs), c * CHUNKS)
            else:
                lead = (filled_f[l - 1][0], branches[l - 1][c][3], 0)
            after = due(sums.open, prior)
            if len(sums.open) > 2:
                after.append(sums.open[2][3][1])
            filled, saved, carry, keep, send = forward_call(
                l, c * CHUNKS, CHUNKS, half, inner, slot_len, scal, *lead, norm_gains, weights, carry, filled, after
            )
            prior = keep
            save_l.append(saved)
            sums.start(keep, send)
            branch_l.append(sums.open[0])
        filled_f.append(filled)
        saves.append(save_l)
        branches.append(branch_l)
    for entry in (sums.open[1], sums.open[0]):
        if entry[2] is None:
            prior = sums.add(entry, [prior])

    swapped = [bits[1], bits[0]] + bits[2:]
    lows = [(None,) * 4] * calls
    filled_n = None
    smalls, g_outs, g_ins = [], [], []
    for l in reversed(range(layers)):
        top, bottom = l == layers - 1, l == 0
        order = list(range(calls)) if top else list(reversed(range(calls)))
        lead = cot if top else filled_n[0]
        hid = filled_f[l][0] if top else filled_f[l + 1][0]
        filled_n, gain_c = None, None
        for c in order:
            after = [prior] if c == order[0] else []
            filled_n, gain_c = norm_call(
                l, top, bottom, c * CHUNKS, CHUNKS, half, inner, scal, hid, lead, lows[c][3] if not top else None, branches[l][c][3], norm_gains, gain_c, filled_n, after
            )
        if top:
            result = filled_n[4]
        _, low_all, u_all = filled_f[l]
        carry, filled, new_lows = None, None, [None] * calls
        sums.open = []
        if bottom:
            out_keep, out_send = weight_call(filled_n[2], [u_all], piece, scal, bits[0], [])
            out = Scatter(out_keep, out_send, piece, bits)
            entries_add = sums.add_quarter
            last, gain_first = None, None
        else:
            out_send = weight_call(filled_n[2], [u_all], piece, scal, None, [])[0]
            out = Offload(out_send)
        g_outs.insert(0, out)
        prior = out_send
        for at, c in enumerate(reversed(range(calls))):
            after = due(sums.open, prior)
            if not sums.open:
                after = [out_send]
            if bottom:
                if at >= 3:
                    after.append(out.step(scal, [after[0]]))
                if at >= 2 and len(sums.open) > 2:
                    last, gain_first = last_call(
                        *sums.open[2][3], filled_n[0], x_mine, (c + 3) * CHUNKS, half, scal, norm_gains, gain_first, last, [prior]
                    )
                    after.append(gain_first)
            elif len(sums.open) > 2:
                after.append(sums.open[2][3][1])
            filled, keep, send, carry = backward_call(
                l, c * CHUNKS, CHUNKS, half, scal, filled_n[1], filled_n[3], weights, saves[l][c], carry, filled, after
            )
            prior = keep
            sums.start(keep, send)
            new_lows[c] = sums.open[0]
        lows = new_lows
        _, acc_v, acc_s, acc_h = carry
        smalls.insert(0, (acc_v, acc_s, acc_h, gain_c))
        d_gate, d_val, d_st, d_step = filled
        if not bottom:
            prior = sums.add(sums.open[1], [prior])
            prior = sums.add(sums.open[0], [prior])
            after = [prior, out.value]
            prior = weight_call(low_all, [d_val, d_gate, d_st, d_step], piece, scal, None, after)[0]
            g_ins.insert(0, Offload(prior))

    def finish_rows(entry, chunk, after):
        return last_call(
            *entry[3], filled_n[0], x_mine, chunk * CHUNKS, half, scal, norm_gains, gain_first, last, after
        )

    groups = cols // GC
    gain_rows = width // GC
    dp_steps = [("dp", bit) for bit in bits]
    prior = sums.add_quarter(sums.open[1], [prior])
    last, gain_first = finish_rows(sums.open[2], 2, [prior])
    per_layer = groups * 8 + 8 + 8 * ((gain_rows + 7) // 8)
    moves = []
    for l, (acc_v, _, acc_h, gain) in enumerate(smalls):
        for g in range(groups):
            moves.append((acc_v, (g, slice(0, 8)), l * per_layer + 8 * g))
        moves.append((acc_h, slice(0, 8), l * per_layer + 8 * groups))
        moves.append((gain, slice(0, 1), l * per_layer + 8 * groups + 8))
    small = Butterfly(pack_call(layers * per_layer, GC, moves, [gain_first]), dp_steps)
    prior = sums.add_quarter(sums.open[0], [small.value])
    prior = small.step([prior])
    while out.order:
        prior = out.step(scal, [prior])
    val_keep, val_send = weight_call(low_all, [d_val], piece, scal, bits[0], [prior])
    val = Scatter(val_keep, val_send, piece, bits)
    last, gain_first = finish_rows(sums.open[1], 1, [val_send])
    prior = small.step([gain_first])
    last, gain_first = finish_rows(sums.open[0], 0, [prior])
    rows = 8 * layers
    moves = [(acc_s, slice(0, 8), 8 * l) for l, (_, acc_s, _, _) in enumerate(smalls)]
    moves.append((gain_first, slice(0, 1), rows))
    rest_small = Butterfly(
        pack_call(rows + 8 * ((gain_rows + 7) // 8), GC, moves, []),
        [("tensor", 1), ("tensor", 2)] + dp_steps,
    )
    misc_keep, misc_send = weight_call(low_all, [d_st, d_step], piece, scal, swapped[0], [rest_small.value])
    misc = Scatter(misc_keep, misc_send, piece, swapped)
    prior = rest_small.step([misc_send])
    while small.came is not None:
        prior = small.step([prior])
    gate_keep, gate_send = weight_call(low_all, [d_gate], piece, scal, swapped[0], [prior])
    gate = Scatter(gate_keep, gate_send, piece, swapped)
    quarter = half // 2
    grad_in = last.reshape(dp, quarter, width)
    returned = lax.all_to_all(grad_in, "dp", split_axis=0, concat_axis=0, tiled=True)
    places = jnp.arange(dp)
    inverse = jnp.sum(jnp.where(deal_order[None, :] == places[:, None], places[None, :], 0), axis=1)
    arrived = take_call(returned, inverse.astype(jnp.int32), [gate_send])
    prior = misc.step(scal, [arrived])
    prior = val.step(scal, [prior])
    prior = rest_small.step([prior])
    prior = gate.step(scal, [prior])

    def side_by_side(mine, theirs, first):
        return jnp.where(
            first == 0,
            jnp.concatenate([mine, theirs], axis=1),
            jnp.concatenate([theirs, mine], axis=1),
        )

    joined = side_by_side(arrived, swap(arrived, "tensor", 2), place)
    grad_x = side_by_side(joined, swap(joined, "tensor", 1), core)

    upper = g_ins[0].value
    prior = misc.step(scal, [prior, joined])
    prior = val.step(scal, [prior])
    prior = gate.step(scal, [prior])
    prior = rest_small.step([prior])
    while gate.order:
        for scatter in (misc, val, gate):
            prior = scatter.step(scal, [prior])
    g_state, g_step = finish_call(
        [(misc, upper, [(2 * LANES, 2 * cols), (LANES, 2 * cols + 2 * LANES)])], [prior]
    )
    for bit in (1, 2):
        g_state = sum_pairs(g_state, "tensor", bit)
    prior = g_step
    while rest_small.came is not None:
        prior = rest_small.step([prior])
    g_out, g_value, g_gate = finish_call(
        [(out, g_outs[1].value, [(cols, 0)]), (val, upper, [(cols, 0)]), (gate, upper, [(cols, cols)])],
        [prior],
    )
    small, rest_small = small.value, rest_small.value
    small = small.reshape(layers, per_layer, GC)
    v_sum = jnp.swapaxes(small[:, : groups * 8].reshape(layers, groups, 8, GC), 1, 2)
    v_sum = v_sum.reshape(layers, 8, cols)
    h_sum = small[:, groups * 8 : groups * 8 + 2, :heads]
    gain_sum = small[:, groups * 8 + 8 : groups * 8 + 8 + gain_rows].reshape(layers, width)
    s_sum = rest_small[:rows].reshape(layers, 8, GC)[:, :5]
    gain_first = rest_small[rows : rows + gain_rows].reshape(1, width)
    gain_own = lax.dynamic_slice_in_dim(
        jnp.concatenate([gain_first, gain_sum], axis=0), me * piece, piece, axis=1
    )

    skip_grad = v_sum[:, 6].reshape(layers, heads, P_SIZE).sum(axis=2)
    return (
        result[None],
        grad_x,
        gain_own,
        g_gate,
        g_value,
        g_state,
        g_step[:, :, :heads],
        g_out,
        v_sum[:, :5],
        s_sum,
        h_sum[:, 0],
        h_sum[:, 1],
        skip_grad,
        v_sum[:, 5],
    )


def solution(mesh):
    return jax.shard_map(
        per_device,
        mesh=mesh,
        in_specs=(
            P(None, "dp", None),
            P("dp", None, None),
            P(),
            P(),
            P(),
            P(None, None, "tensor"),
            P(None, None, "tensor"),
            P(),
            P(None, None, "tensor"),
            P(None, None, "tensor"),
            P(None, None, "tensor"),
            P(),
            P(None, "tensor"),
            P(None, "tensor"),
            P(None, "tensor"),
            P(None, "tensor"),
        ),
        out_specs=(
            P("dp", None, None),
            P(None, "dp", None),
            P(None, "dp"),
            P(None, "dp", "tensor"),
            P(None, "dp", "tensor"),
            P(None, "dp", None),
            P(None, "dp", "tensor"),
            P(None, "dp", "tensor"),
            P(None, None, "tensor"),
            P(),
            P(None, "tensor"),
            P(None, "tensor"),
            P(None, "tensor"),
            P(None, "tensor"),
        ),
        check_vma=False,
    )
```

time: 841 us -> 652 us (0.78)
  waiting for transfers between devices: 358 us -> 72.6 us
  Pallas kernels: 247 us -> 396 us
  matrix products: 41.5 us -> 0 us
  other arithmetic: 42.1 us -> 9.61 us
  starting transfers between devices: 33.4 us -> 55.2 us
    reduce_scatter x4 -> x2, waiting for transfers between devices: 152 us -> 0.01 us  [__init__(): self.value = lax.psum_scatter(value, 'dp', scatter_dimension=0, tiled=True)]
    pallas_call x16 -> x71, Pallas kernels: 247 us -> 396 us  [run(): pl.pallas_call(functools.partial(kernel, len(self.tail) + len(after)), gr...]
    ppermute x54 -> x81, waiting for transfers between devices: 140 us -> 68.3 us  [swap(): return lax.ppermute(value, axis, pairs(axis, bit))]
    all_to_all x1, waiting for transfers between devices: 65.7 us -> 4.25 us  [per_device(): lax.all_to_all(grad_in, 'dp', split_axis=0, concat_axis=0, tiled=True)]
    dot_general x4 -> x0, matrix products: 41.5 us -> none  [tn(): lax.dot_general(a, b, (((0,), (0,)), ((), ())), preferred_element_type=F32)]
    ppermute x54 -> x81, starting transfers between devices: 29.3 us -> 51.6 us  [swap(): return lax.ppermute(value, axis, pairs(axis, bit))]
    unnamed x191 -> x203, local copies, waits for them, and re-layouts: 20.3 us -> 38.1 us
    convert_element_type x15 -> x0, other arithmetic: 11.1 us -> none  [the longest x8 4.43 us: two_terms(): main = wide[:, :width].astype(BF16)]
  transfers between devices with their start and end apart: 59 -> 84, of which waited for: 24 -> 14; matrix products, arithmetic and copies ran while one was open for 12% -> 3% of each run, Pallas kernels for 28% -> 58%
where the time goes in v2:
time: 652 us; the launch traced here: 642 us
  Pallas kernels  396 us (61%)
  waiting for transfers between devices  72.6 us (11%)
  starting transfers between devices  55.2 us (8%)
  local copies, waits for them, and re-layouts  46.4 us (7%)
  blocking collectives  44.2 us (7%)
  between operations  18.1 us (3%)
  other arithmetic  9.61 us (1%)
    pallas_call x71, Pallas kernels, run(): pl.pallas_call(functools.partial(kernel, len(self.tail) + len(after)), gr...  396 us
    ppermute x81, waiting for transfers between devices, swap(): return lax.ppermute(value, axis, pairs(axis, bit))  68.3 us
    ppermute x81, starting transfers between devices, swap(): return lax.ppermute(value, axis, pairs(axis, bit))  51.6 us
    all_to_all x1, blocking collectives, per_device(): lax.all_to_all(x_dealt, 'dp', split_axis=0, concat_axis=0, tiled=True)  44.2 us
    unnamed x203, local copies, waits for them, and re-layouts  38.1 us
  transfers between devices with their start and end apart: 84, of which 14 were waited for; matrix products, arithmetic and copies ran while one was open for 3% of the time, Pallas kernels for 58%

profile of v2, /device:TPU:0, one launch (start us, length us, event | category | flops | bytes accessed | tf_op | source)
XLA Modules:
  0.0 642.4 jit_solution(2108427871631598170)
XLA Ops:
  12.7 44.2 %all_to_all.10 = bf16[8,64,1536]{2,1,0:T(8,128)(2,1)S(1)} all-to-all(bf16[8,64,1536]{2,1,0:T(8,128)(2,1)S(1)} %broadcast_select_fusion), channel_id=1, replica_groups=mesh['dp'=8,'tensor'=4] {'dp'}, dimensions={0} | all-to-all | bytes 3145728 | tf_op jit(solution)/shard_map/all_to_all | solution.py:1047
  65.5 12.7 %layer_forward.8 = (f32[1024,1536]{1,0:T(8,128)}, bf16[1024,1536]{1,0:T(8,128)(2,1)}, bf16[1024,768]{1,0:T(8,128)(2,1)}, f32[256,768]{1,0:T(8,128)}, bf16[256,76...) custom-call(s32[6]{0:T(128)} %stack.39.refs_0_.place_ref, ...), custom_call_target="tpu_custom_call" | custom-call | flops 13200000000 | bytes 1000000 | tf_op jit(solution)/shard_map/layer_forward/pallas_call | solution.py:527
  78.6 12.9 %layer_forward.9 = (f32[1024,1536]{1,0:T(8,128)}, bf16[1024,1536]{1,0:T(8,128)(2,1)}, bf16[1024,768]{1,0:T(8,128)(2,1)}, f32[256,768]{1,0:T(8,128)}, bf16[256,76...) custom-call(s32[6]{0:T(128)} %stack.39.refs_0_.place_ref, ...), custom_call_target="tpu_custom_call", output_to_operand_aliasing={{0}: (16, {}), {1}: (17, {}), {2}: (18, {})} | custom-call | flops 13200000000 | bytes 1000000 | tf_op jit(solution)/shard_map/layer_forward/pallas_call | solution.py:527
  96.4 13.1 %layer_forward.10 = (f32[1024,1536]{1,0:T(8,128)}, bf16[1024,1536]{1,0:T(8,128)(2,1)}, bf16[1024,768]{1,0:T(8,128)(2,1)}, f32[256,768]{1,0:T(8,128)}, bf16[256,7...) custom-call(s32[6]{0:T(128)} %stack.39.refs_0_.place_ref, ...), custom_call_target="tpu_custom_call", output_to_operand_aliasing={{0}: (16, {}), {1}: (17, {}), {2}: (18, {})} | custom-call | flops 13200000000 | bytes 1000000 | tf_op jit(solution)/shard_map/layer_forward/pallas_call | solution.py:527
  114.4 12.9 %layer_forward.11 = (f32[1024,1536]{1,0:T(8,128)}, bf16[1024,1536]{1,0:T(8,128)(2,1)}, bf16[1024,768]{1,0:T(8,128)(2,1)}, f32[256,768]{1,0:T(8,128)}, bf16[256,7...) custom-call(s32[6]{0:T(128)} %stack.39.refs_0_.place_ref, ...), custom_call_target="tpu_custom_call", output_to_operand_aliasing={{0}: (16, {}), {1}: (17, {}), {2}: (18, {})} | custom-call | flops 13200000000 | bytes 1000000 | tf_op jit(solution)/shard_map/layer_forward/pallas_call | solution.py:527
  132.8 14.1 %layer_forward.12 = (f32[1024,1536]{1,0:T(8,128)}, bf16[1024,1536]{1,0:T(8,128)(2,1)}, bf16[1024,768]{1,0:T(8,128)(2,1)}, f32[256,768]{1,0:T(8,128)}, bf16[256,7...) custom-call(s32[6]{0:T(128)} %stack.39.refs_0_.place_ref, ...), custom_call_target="tpu_custom_call" | custom-call | flops 13200000000 | bytes 1000000 | tf_op jit(solution)/shard_map/layer_forward/pallas_call | solution.py:527
  151.4 13.9 %layer_forward.13 = (f32[1024,1536]{1,0:T(8,128)}, bf16[1024,1536]{1,0:T(8,128)(2,1)}, bf16[1024,768]{1,0:T(8,128)(2,1)}, f32[256,768]{1,0:T(8,128)}, bf16[256,7...) custom-call(s32[6]{0:T(128)} %stack.39.refs_0_.place_ref, ...), custom_call_target="tpu_custom_call", output_to_operand_aliasing={{0}: (19, {}), {1}: (20, {}), {2}: (21, {})} | custom-call | flops 13200000000 | bytes 1000000 | tf_op jit(solution)/shard_map/layer_forward/pallas_call | solution.py:527
  171.2 13.9 %layer_forward.14 = (f32[1024,1536]{1,0:T(8,128)}, bf16[1024,1536]{1,0:T(8,128)(2,1)}, bf16[1024,768]{1,0:T(8,128)(2,1)}, f32[256,768]{1,0:T(8,128)}, bf16[256,7...) custom-call(s32[6]{0:T(128)} %stack.39.refs_0_.place_ref, ...), custom_call_target="tpu_custom_call", output_to_operand_aliasing={{0}: (19, {}), {1}: (20, {}), {2}: (21, {})} | custom-call | flops 13200000000 | bytes 1000000 | tf_op jit(solution)/shard_map/layer_forward/pallas_call | solution.py:527
  189.4 14.3 %layer_forward.15 = (f32[1024,1536]{1,0:T(8,128)}, bf16[1024,1536]{1,0:T(8,128)(2,1)}, bf16[1024,768]{1,0:T(8,128)(2,1)}, f32[256,768]{1,0:T(8,128)}, bf16[256,7...) custom-call(s32[6]{0:T(128)} %stack.39.refs_0_.place_ref, ...), custom_call_target="tpu_custom_call", output_to_operand_aliasing={{0}: (19, {}), {1}: (20, {}), {2}: (21, {})} | custom-call | flops 13200000000 | bytes 1000000 | tf_op jit(solution)/shard_map/layer_forward/pallas_call | solution.py:527
  213.5 4.0 collective-permute-done.28.refs_4_
  218.0 8.5 %collective-permute-done.25.refs_4_ = bf16[128,1664]{1,0:T(8,128)(2,1)S(1)} collective-permute-done((bf16[128,1664]{1,0:T(8,128)(2,1)}, bf16[128,1664]{1,0:T(8,128)(2,1)S(1)}, u32[]{:S(2)}, u32[]{:S(2)}) %collective-permute-start.25) | collective-permute-done | bytes 426016 | tf_op jit(solution)/shard_map/ppermute | solution.py:819
  226.6 5.7 norm_backward.8
  235.7 5.8 norm_backward.9
  242.4 5.8 norm_backward.10
  249.2 5.8 norm_backward.11
  255.0 6.4 %weight_grad.6.refs_20_ = bf16[1536,768]{1,0:T(8,128)(2,1)} custom-call(s32[6]{0:T(128)} %stack.39.refs_0_.place_ref, bf16[1024,1536]{1,0:T(8,128)(2,1)} %get-tuple-element.411.refs_1_, bf16[1024,768]{1,0:T(8,128)(2,1)} %get-tuple-element.412.refs_2_), custom_call_target="tpu_custom_call" | custom-call | flops 6600000000 | bytes 1000000 | tf_op jit(solution)/shard_map/weight_grad/pallas_call | solution.py:527
  261.5 14.3 %layer_backward.8 = (bf16[1024,768]{1,0:T(8,128)(2,1)}, bf16[1024,768]{1,0:T(8,128)(2,1)}, bf16[1024,256]{1,0:T(8,128)(2,1)}, bf16[1024,128]{1,0:T(8,128)(2,1)},...) custom-call(s32[6]{0:T(128)} %stack.39.refs_0_.place_ref, ...), custom_call_target="tpu_custom_call" | custom-call | flops 17600000000 | bytes 1000000 | tf_op jit(solution)/shard_map/layer_backward/pallas_call | solution.py:527
  276.4 14.3 %layer_backward.9 = (bf16[1024,768]{1,0:T(8,128)(2,1)}, bf16[1024,768]{1,0:T(8,128)(2,1)}, bf16[1024,256]{1,0:T(8,128)(2,1)}, bf16[1024,128]{1,0:T(8,128)(2,1)},...) custom-call(s32[6]{0:T(128)} %stack.39.refs_0_.place_ref, ...), custom_call_target="tpu_custom_call", output_to_operand_aliasing={{0}: (24, {}), {1}: (25, {}), {2}: (26, {}), {3}: (27, {})} | custom-call | flops 17600000000 | bytes 1000000 | tf_op jit(solution)/shard_map/layer_backward/pallas_call | solution.py:527
  294.5 14.5 %layer_backward.10 = (bf16[1024,768]{1,0:T(8,128)(2,1)}, bf16[1024,768]{1,0:T(8,128)(2,1)}, bf16[1024,256]{1,0:T(8,128)(2,1)}, bf16[1024,128]{1,0:T(8,128)(2,1)}...) custom-call(s32[6]{0:T(128)} %stack.39.refs_0_.place_ref, ...), custom_call_target="tpu_custom_call", output_to_operand_aliasing={{0}: (24, {}), {1}: (25, {}), {2}: (26, {}), {3}: (27, {})} | custom-call | flops 17600000000 | bytes 1000000 | tf_op jit(solution)/shard_map/layer_backward/pallas_call | solution.py:527
  313.0 14.5 %layer_backward.11 = (bf16[1024,768]{1,0:T(8,128)(2,1)}, bf16[1024,768]{1,0:T(8,128)(2,1)}, bf16[1024,256]{1,0:T(8,128)(2,1)}, bf16[1024,128]{1,0:T(8,128)(2,1)}...) custom-call(s32[6]{0:T(128)} %stack.39.refs_0_.place_ref, ...), custom_call_target="tpu_custom_call", output_to_operand_aliasing={{0}: (24, {}), {1}: (25, {}), {2}: (26, {}), {3}: (27, {})} | custom-call | flops 17600000000 | bytes 1000000 | tf_op jit(solution)/shard_map/layer_backward/pallas_call | solution.py:527
  330.6 8.5 %collective-permute-done.44.refs_4_ = bf16[128,1536]{1,0:T(8,128)(2,1)S(1)} collective-permute-done((bf16[128,1536]{1,0:T(8,128)(2,1)S(1)}, bf16[128,1536]{1,0:T(8,128)(2,1)S(1)}, u32[]{:S(2)}, u32[]{:S(2)}) %collective-permute-start.44) | collective-permute-done | bytes 393248 | tf_op jit(solution)/shard_map/ppermute | solution.py:819
  345.4 11.2 %weight_grad.7.refs_12_ = bf16[1536,1920]{1,0:T(8,128)(2,1)} custom-call(s32[6]{0:T(128)} %stack.39.refs_0_.place_ref, bf16[1024,1536]{1,0:T(8,128)(2,1)} %get-tuple-element.445.refs_1_, bf16[1024,768]{1,0:T(8,128)(2,1)} %get-tuple-element.446.refs_2_, bf16[1024,768]{1,0:T(8,128)(2,1)} %get-tuple-element.447.refs_3_, ...), custom_call_target="tpu_custom_call" | custom-call | flops 16499999744 | bytes 1000000 | tf_op jit(solution)/shard_map/weight_grad/pallas_call | solution.py:527
  358.3 5.8 norm_backward.12
  364.7 4.5 collective-permute-done.38.refs_4_
  369.9 5.8 norm_backward.13
  376.7 5.9 norm_backward.14
  383.5 6.0 norm_backward.15
  389.4 6.7 %weight_grad.8 = (bf16[768,768]{1,0:T(8,128)(2,1)}, bf16[768,768]{1,0:T(8,128)(2,1)}) custom-call(s32[6]{0:T(128)} %stack.39.refs_0_.place_ref, bf16[1024,1536]{1,0:T(8,128)(2,1)} %get-tuple-element.499.refs_1_, bf16[1024,768]{1,0:T(8,128)(2,1)} %get-tuple-element.500.refs_2_), custom_call_target="tpu_custom_call" | custom-call | flops 6600000000 | bytes 1000000 | tf_op jit(solution)/shard_map/weight_grad/pallas_call | solution.py:527
  397.6 14.4 %layer_backward.12 = (bf16[1024,768]{1,0:T(8,128)(2,1)}, bf16[1024,768]{1,0:T(8,128)(2,1)}, bf16[1024,256]{1,0:T(8,128)(2,1)}, bf16[1024,128]{1,0:T(8,128)(2,1)}...) custom-call(s32[6]{0:T(128)} %stack.39.refs_0_.place_ref, ...), custom_call_target="tpu_custom_call" | custom-call | flops 17600000000 | bytes 1000000 | tf_op jit(solution)/shard_map/layer_backward/pallas_call | solution.py:527
  412.1 14.4 %layer_backward.13 = (bf16[1024,768]{1,0:T(8,128)(2,1)}, bf16[1024,768]{1,0:T(8,128)(2,1)}, bf16[1024,256]{1,0:T(8,128)(2,1)}, bf16[1024,128]{1,0:T(8,128)(2,1)}...) custom-call(s32[6]{0:T(128)} %stack.39.refs_0_.place_ref, ...), custom_call_target="tpu_custom_call", output_to_operand_aliasing={{0}: (24, {}), {1}: (25, {}), {2}: (26, {}), {3}: (27, {})} | custom-call | flops 17600000000 | bytes 1000000 | tf_op jit(solution)/shard_map/layer_backward/pallas_call | solution.py:527
  430.6 14.6 %layer_backward.14 = (bf16[1024,768]{1,0:T(8,128)(2,1)}, bf16[1024,768]{1,0:T(8,128)(2,1)}, bf16[1024,256]{1,0:T(8,128)(2,1)}, bf16[1024,128]{1,0:T(8,128)(2,1)}...) custom-call(s32[6]{0:T(128)} %stack.39.refs_0_.place_ref, ...), custom_call_target="tpu_custom_call", output_to_operand_aliasing={{0}: (24, {}), {1}: (25, {}), {2}: (26, {}), {3}: (27, {})} | custom-call | flops 17600000000 | bytes 1000000 | tf_op jit(solution)/shard_map/layer_backward/pallas_call | solution.py:527
  456.8 14.4 %layer_backward.15 = (bf16[1024,768]{1,0:T(8,128)(2,1)}, bf16[1024,768]{1,0:T(8,128)(2,1)}, bf16[1024,256]{1,0:T(8,128)(2,1)}, bf16[1024,128]{1,0:T(8,128)(2,1)}...) custom-call(s32[6]{0:T(128)} %stack.39.refs_0_.place_ref, ...), custom_call_target="tpu_custom_call", output_to_operand_aliasing={{0}: (24, {}), {1}: (25, {}), {2}: (26, {}), {3}: (27, {})} | custom-call | flops 17600000000 | bytes 1000000 | tf_op jit(solution)/shard_map/layer_backward/pallas_call | solution.py:527
  475.8 2.6 norm_last.5
  493.7 6.8 %weight_grad.9 = (bf16[768,768]{1,0:T(8,128)(2,1)}, bf16[768,768]{1,0:T(8,128)(2,1)}) custom-call(s32[6]{0:T(128)} %stack.39.refs_0_.place_ref, bf16[1024,1536]{1,0:T(8,128)(2,1)} %get-tuple-element.555.refs_1_, bf16[1024,768]{1,0:T(8,128)(2,1)} %get-tuple-element.556.refs_2_, bf16[192,768]{1,0:T(8,128)(2,1)} %get-tuple-element.558.refs_3_), custom_call_target="tpu_custom_call" | custom-call | flops 6600000000 | bytes 1000000 | tf_op jit(solution)/shard_map/weight_grad/pallas_call | solution.py:527
  513.5 3.5 all-to-all-start.1
  517.0 4.6 weight_grad.10
  527.8 6.0 weight_grad.11
  533.9 4.2 all-to-all-done.1.src
  552.8 8.2 %collective-permute-done.65.y = f32[24,256]{1,0:T(8,128)S(1)} collective-permute-done((f32[24,256]{1,0:T(8,128)S(1)}, f32[24,256]{1,0:T(8,128)S(1)}, u32[]{:S(2)}, u32[]{:S(2)}) %collective-permute-start.65) | collective-permute-done | bytes 24608 | tf_op jit(solution)/shard_map/ppermute | solution.py:819
  565.0 6.0 collective-permute-done.69.b
  577.2 6.3 collective-permute-done.71.b
  583.5 2.5 collective-permute-start.74
  589.6 2.8 collective-permute-start.77
  599.3 6.3 collective-permute-done.73.y
  609.6 3.8 maximum_select_fusion
  615.0 5.0 collective-permute-done.75.y
  624.7 3.7 finish.3
  628.4 5.9 collective-permute-done.80
  (421 shorter events, 182.3 us)
Async XLA Ops:
  7.2 338.2 %reduce-scatter.3.cloned.1.call-start = ((), (), s32[]{:S(2)}) async-start(), calls=%async_computation.4 | async-start | bytes 2654208 | tf_op jit(solution)/shard_map/reduce_scatter | solution.py:986
  94.7 18.9 %collective-permute-start.3 = (bf16[128,1664]{1,0:T(8,128)(2,1)}, bf16[128,1664]{1,0:T(8,128)(2,1)S(1)}, u32[]{:S(2)}, u32[]{:S(2)}) collective-permute-start(bf16[128,1664]{1,0:T(8,128)(2,1)} %add_pair.12.refs_19_.refs_2_.refs_7_), channel_id=1, source_target_pairs={{0,2},{1,3},{2,0},{3,1},{4,6},{5,7},{6,4},{7,5},{8,10},{9,11},{10,... | collective-permute-start | bytes 1277960 | tf_op jit(solution)/shard_map/ppermute | solution.py:819
  96.2 34.2 %collective-permute-start.5 = (bf16[128,1664]{1,0:T(8,128)(2,1)}, bf16[128,1664]{1,0:T(8,128)(2,1)S(1)}, u32[]{:S(2)}, u32[]{:S(2)}) collective-permute-start(bf16[128,1664]{1,0:T(8,128)(2,1)} %add_pair.12.refs_19_.refs_2_.refs_7_), channel_id=1, source_target_pairs={{0,1},{1,0},{2,3},{3,2},{4,5},{5,4},{6,7},{7,6},{8,9},{9,8},{10,11... | collective-permute-start | bytes 1277960 | tf_op jit(solution)/shard_map/ppermute | solution.py:819
  113.1 36.8 %collective-permute-start.15 = (bf16[128,1664]{1,0:T(8,128)(2,1)}, bf16[128,1664]{1,0:T(8,128)(2,1)S(1)}, u32[]{:S(2)}, u32[]{:S(2)}) collective-permute-start(bf16[128,1664]{1,0:T(8,128)(2,1)} %add_pair.13.refs_19_.refs_2_.refs_7_), channel_id=1, source_target_pairs={{0,1},{1,0},{2,3},{3,2},{4,5},{5,4},{6,7},{7,6},{8,9},{9,8},{10,11... | collective-permute-start | bytes 1277960 | tf_op jit(solution)/shard_map/ppermute | solution.py:819
  127.3 19.6 %collective-permute-start.4 = (f32[128,1664]{1,0:T(8,128)}, f32[128,1664]{1,0:T(8,128)S(1)}, u32[]{:S(2)}, u32[]{:S(2)}) collective-permute-start(f32[128,1664]{1,0:T(8,128)} %get-tuple-element.328), channel_id=1, source_target_pairs={{0,1},{1,0},{2,3},{3,2},{4,5},{5,4},{6,7},{7,6},{8,9},{9,8},{10,11... | collective-permute-start | bytes 2555912 | tf_op jit(solution)/shard_map/ppermute | solution.py:819
  127.4 23.1 %collective-permute-start.16 = (bf16[128,1664]{1,0:T(8,128)(2,1)S(1)}, bf16[128,1664]{1,0:T(8,128)(2,1)S(1)}, u32[]{:S(2)}, u32[]{:S(2)}) collective-permute-start(bf16[128,1664]{1,0:T(8,128)(2,1)S(1)} %collective-permute-done.8.refs_17_.refs_3_.refs_8_), channel_id=1, source_target_pairs={{0,1},{1,0},{2,3},{3,2},{4,5},{5,4},{6,7},{7,6},{8,9},{9,8},{10,11... | collective-permute-start | bytes 1277960 | tf_op jit(solution)/shard_map/ppermute | solution.py:819
  130.5 20.0 %collective-permute-start.12 = (bf16[128,1664]{1,0:T(8,128)(2,1)}, bf16[128,1664]{1,0:T(8,128)(2,1)S(1)}, u32[]{:S(2)}, u32[]{:S(2)}) collective-permute-start(bf16[128,1664]{1,0:T(8,128)(2,1)} %add_pair.14.refs_16_.refs_2_.refs_7_), channel_id=1, source_target_pairs={{0,2},{1,3},{2,0},{3,1},{4,6},{5,7},{6,4},{7,5},{8,10},{9,11},{10,... | collective-permute-start | bytes 1277960 | tf_op jit(solution)/shard_map/ppermute | solution.py:819
  132.0 36.8 %collective-permute-start.13 = (bf16[128,1664]{1,0:T(8,128)(2,1)}, bf16[128,1664]{1,0:T(8,128)(2,1)S(1)}, u32[]{:S(2)}, u32[]{:S(2)}) collective-permute-start(bf16[128,1664]{1,0:T(8,128)(2,1)} %add_pair.14.refs_16_.refs_2_.refs_7_), channel_id=1, source_target_pairs={{0,1},{1,0},{2,3},{3,2},{4,5},{5,4},{6,7},{7,6},{8,9},{9,8},{10,11... | collective-permute-start | bytes 1277960 | tf_op jit(solution)/shard_map/ppermute | solution.py:819
  146.9 18.9 %collective-permute-start.17 = (f32[128,1664]{1,0:T(8,128)}, f32[128,1664]{1,0:T(8,128)S(1)}, u32[]{:S(2)}, u32[]{:S(2)}) collective-permute-start(f32[128,1664]{1,0:T(8,128)} %get-tuple-element.343), channel_id=1, source_target_pairs={{0,1},{1,0},{2,3},{3,2},{4,5},{5,4},{6,7},{7,6},{8,9},{9,8},{10,11... | collective-permute-start | bytes 2555912 | tf_op jit(solution)/shard_map/ppermute | solution.py:819
  150.5 37.8 %collective-permute-start.10 = (bf16[128,1664]{1,0:T(8,128)(2,1)}, bf16[128,1664]{1,0:T(8,128)(2,1)S(1)}, u32[]{:S(2)}, u32[]{:S(2)}) collective-permute-start(bf16[128,1664]{1,0:T(8,128)(2,1)} %add_pair.15.refs_22_.refs_2_.refs_7_), channel_id=1, source_target_pairs={{0,1},{1,0},{2,3},{3,2},{4,5},{5,4},{6,7},{7,6},{8,9},{9,8},{10,11... | collective-permute-start | bytes 1277960 | tf_op jit(solution)/shard_map/ppermute | solution.py:819
  150.5 19.9 %collective-permute-start.14 = (bf16[128,1664]{1,0:T(8,128)(2,1)S(1)}, bf16[128,1664]{1,0:T(8,128)(2,1)S(1)}, u32[]{:S(2)}, u32[]{:S(2)}) collective-permute-start(bf16[128,1664]{1,0:T(8,128)(2,1)S(1)} %collective-permute-done.12.refs_23_.refs_3_.refs_8_), channel_id=1, source_target_pairs={{0,1},{1,0},{2,3},{3,2},{4,5},{5,4},{6,7},{7,6},{8,9},{9,8},{10,11... | collective-permute-start | bytes 1277960 | tf_op jit(solution)/shard_map/ppermute | solution.py:819
  165.4 19.9 %collective-permute-start.18 = (f32[128,1664]{1,0:T(8,128)}, f32[128,1664]{1,0:T(8,128)S(1)}, u32[]{:S(2)}, u32[]{:S(2)}) collective-permute-start(f32[128,1664]{1,0:T(8,128)} %get-tuple-element.351), channel_id=1, source_target_pairs={{0,1},{1,0},{2,3},{3,2},{4,5},{5,4},{6,7},{7,6},{8,9},{9,8},{10,11... | collective-permute-start | bytes 2555912 | tf_op jit(solution)/shard_map/ppermute | solution.py:819
  165.8 22.5 %collective-permute-start.11 = (bf16[128,1664]{1,0:T(8,128)(2,1)S(1)}, bf16[128,1664]{1,0:T(8,128)(2,1)S(1)}, u32[]{:S(2)}, u32[]{:S(2)}) collective-permute-start(bf16[128,1664]{1,0:T(8,128)(2,1)S(1)} %collective-permute-done.9.refs_23_.refs_3_.refs_8_), channel_id=1, source_target_pairs={{0,1},{1,0},{2,3},{3,2},{4,5},{5,4},{6,7},{7,6},{8,9},{9,8},{10,11... | collective-permute-start | bytes 1277960 | tf_op jit(solution)/shard_map/ppermute | solution.py:819
  168.9 19.4 %collective-permute-start.19 = (bf16[128,1664]{1,0:T(8,128)(2,1)}, bf16[128,1664]{1,0:T(8,128)(2,1)S(1)}, u32[]{:S(2)}, u32[]{:S(2)}) collective-permute-start(bf16[128,1664]{1,0:T(8,128)(2,1)} %add_pair.16.refs_22_.refs_3_), channel_id=1, source_target_pairs={{0,2},{1,3},{2,0},{3,1},{4,6},{5,7},{6,4},{7,5},{8,10},{9,11},{10,... | collective-permute-start | bytes 1277960 | tf_op jit(solution)/shard_map/ppermute | solution.py:819
  185.2 20.1 %collective-permute-start.21 = (f32[128,1664]{1,0:T(8,128)}, f32[128,1664]{1,0:T(8,128)S(1)}, u32[]{:S(2)}, u32[]{:S(2)}) collective-permute-start(f32[128,1664]{1,0:T(8,128)} %get-tuple-element.356), channel_id=1, source_target_pairs={{0,1},{1,0},{2,3},{3,2},{4,5},{5,4},{6,7},{7,6},{8,9},{9,8},{10,11... | collective-permute-start | bytes 2555912 | tf_op jit(solution)/shard_map/ppermute | solution.py:819
  209.8 22.5 %collective-permute-start.29 = (bf16[128,1664]{1,0:T(8,128)(2,1)S(1)}, bf16[128,1664]{1,0:T(8,128)(2,1)S(1)}, u32[]{:S(2)}, u32[]{:S(2)}) collective-permute-start(bf16[128,1664]{1,0:T(8,128)(2,1)S(1)} %copy-done.19), channel_id=1, source_target_pairs={{0,1},{1,0},{2,3},{3,2},{4,5},{5,4},{6,7},{7,6},{8,9},{9,8},{10,11... | collective-permute-start | bytes 1277960 | tf_op jit(solution)/shard_map/ppermute | solution.py:819
  212.9 22.0 %collective-permute-start.22 = (bf16[128,1664]{1,0:T(8,128)(2,1)}, bf16[128,1664]{1,0:T(8,128)(2,1)S(1)}, u32[]{:S(2)}, u32[]{:S(2)}) collective-permute-start(bf16[128,1664]{1,0:T(8,128)(2,1)} %add_pair.19.refs_8_.refs_3_), channel_id=1, source_target_pairs={{0,2},{1,3},{2,0},{3,1},{4,6},{5,7},{6,4},{7,5},{8,10},{9,11},{10,... | collective-permute-start | bytes 1277960 | tf_op jit(solution)/shard_map/ppermute | solution.py:819
  217.5 24.0 %collective-permute-start.26 = (bf16[128,1664]{1,0:T(8,128)(2,1)S(1)}, bf16[128,1664]{1,0:T(8,128)(2,1)S(1)}, u32[]{:S(2)}, u32[]{:S(2)}) collective-permute-start(bf16[128,1664]{1,0:T(8,128)(2,1)S(1)} %copy-done.22), channel_id=1, source_target_pairs={{0,1},{1,0},{2,3},{3,2},{4,5},{5,4},{6,7},{7,6},{8,9},{9,8},{10,11... | collective-permute-start | bytes 1277960 | tf_op jit(solution)/shard_map/ppermute | solution.py:819
  261.5 336.0 %reduce-scatter.5.cloned.1.call-start = ((), (), s32[]{:S(2)}) async-start(), calls=%async_computation.5 | async-start | bytes 6635520 | tf_op jit(solution)/shard_map/reduce_scatter | solution.py:986
  290.8 18.5 %collective-permute-start.34 = (f32[128,1536]{1,0:T(8,128)}, f32[128,1536]{1,0:T(8,128)S(1)}, u32[]{:S(2)}, u32[]{:S(2)}) collective-permute-start(f32[128,1536]{1,0:T(8,128)} %get-tuple-element.440), channel_id=1, source_target_pairs={{0,1},{1,0},{2,3},{3,2},{4,5},{5,4},{6,7},{7,6},{8,9},{9,8},{10,11... | collective-permute-start | bytes 2359304 | tf_op jit(solution)/shard_map/ppermute | solution.py:819
  309.0 30.2 %collective-permute-start.37 = (f32[128,1536]{1,0:T(8,128)}, f32[128,1536]{1,0:T(8,128)}, u32[]{:S(2)}, u32[]{:S(2)}) collective-permute-start(f32[128,1536]{1,0:T(8,128)} %get-tuple-element.444), channel_id=1, source_target_pairs={{0,1},{1,0},{2,3},{3,2},{4,5},{5,4},{6,7},{7,6},{8,9},{9,8},{10,11... | collective-permute-start | bytes 2359304 | tf_op jit(solution)/shard_map/ppermute | solution.py:819
  330.1 26.5 %collective-permute-start.47 = (bf16[128,1536]{1,0:T(8,128)(2,1)S(1)}, bf16[128,1536]{1,0:T(8,128)(2,1)S(1)}, u32[]{:S(2)}, u32[]{:S(2)}) collective-permute-start(bf16[128,1536]{1,0:T(8,128)(2,1)S(1)} %copy-done.32), channel_id=1, source_target_pairs={{0,1},{1,0},{2,3},{3,2},{4,5},{5,4},{6,7},{7,6},{8,9},{9,8},{10,11... | collective-permute-start | bytes 1179656 | tf_op jit(solution)/shard_map/ppermute | solution.py:819
  330.1 34.0 %collective-permute-start.45 = (bf16[128,1536]{1,0:T(8,128)(2,1)S(1)}, bf16[128,1536]{1,0:T(8,128)(2,1)S(1)}, u32[]{:S(2)}, u32[]{:S(2)}) collective-permute-start(bf16[128,1536]{1,0:T(8,128)(2,1)S(1)} %copy-done.34), channel_id=1, source_target_pairs={{0,1},{1,0},{2,3},{3,2},{4,5},{5,4},{6,7},{7,6},{8,9},{9,8},{10,11... | collective-permute-start | bytes 1179656 | tf_op jit(solution)/shard_map/ppermute | solution.py:819
  339.1 18.4 %collective-permute-start.48 = (bf16[128,1536]{1,0:T(8,128)(2,1)}, bf16[128,1536]{1,0:T(8,128)(2,1)}, u32[]{:S(2)}, u32[]{:S(2)}) collective-permute-start(bf16[128,1536]{1,0:T(8,128)(2,1)} %copy-done.33), channel_id=1, source_target_pairs={{0,1},{1,0},{2,3},{3,2},{4,5},{5,4},{6,7},{7,6},{8,9},{9,8},{10,11... | collective-permute-start | bytes 1179656 | tf_op jit(solution)/shard_map/ppermute | solution.py:819
  339.2 30.0 %collective-permute-start.46 = (bf16[128,1536]{1,0:T(8,128)(2,1)S(1)}, bf16[128,1536]{1,0:T(8,128)(2,1)S(1)}, u32[]{:S(2)}, u32[]{:S(2)}) collective-permute-start(bf16[128,1536]{1,0:T(8,128)(2,1)S(1)} %collective-permute-done.44.refs_4_), channel_id=1, source_target_pairs={{0,1},{1,0},{2,3},{3,2},{4,5},{5,4},{6,7},{7,6},{8,9},{9,8},{10,11... | collective-permute-start | bytes 1179656 | tf_op jit(solution)/shard_map/ppermute | solution.py:819
  341.7 22.5 %collective-permute-start.41 = (bf16[128,1536]{1,0:T(8,128)(2,1)}, bf16[128,1536]{1,0:T(8,128)(2,1)S(1)}, u32[]{:S(2)}, u32[]{:S(2)}) collective-permute-start(bf16[128,1536]{1,0:T(8,128)(2,1)} %add_pair.22.refs_0_.refs_3_), channel_id=1, source_target_pairs={{0,2},{1,3},{2,0},{3,1},{4,6},{5,7},{6,4},{7,5},{8,10},{9,11},{10,... | collective-permute-start | bytes 1179656 | tf_op jit(solution)/shard_map/ppermute | solution.py:819
  364.1 18.4 %collective-permute-start.39 = (bf16[128,1536]{1,0:T(8,128)(2,1)S(1)}, bf16[128,1536]{1,0:T(8,128)(2,1)S(1)}, u32[]{:S(2)}, u32[]{:S(2)}) collective-permute-start(bf16[128,1536]{1,0:T(8,128)(2,1)S(1)} %copy-done.35), channel_id=1, source_target_pairs={{0,1},{1,0},{2,3},{3,2},{4,5},{5,4},{6,7},{7,6},{8,9},{9,8},{10,11... | collective-permute-start | bytes 1179656 | tf_op jit(solution)/shard_map/ppermute | solution.py:819
  396.1 57.1 %collective-permute-start.51 = (bf16[768,768]{1,0:T(8,128)(2,1)}, bf16[768,768]{1,0:T(8,128)(2,1)S(1)}, u32[]{:S(2)}, u32[]{:S(2)}) collective-permute-start(bf16[768,768]{1,0:T(8,128)(2,1)} %get-tuple-element.501.refs_20_), channel_id=1, source_target_pairs={{0,4},{4,0},{8,12},{12,8},{16,20},{20,16},{24,28},{28,24},{1,5},{5... | collective-permute-start | bytes 3538952 | tf_op jit(solution)/shard_map/ppermute | solution.py:819
  426.5 18.7 %collective-permute-start.50 = (f32[128,1536]{1,0:T(8,128)}, f32[128,1536]{1,0:T(8,128)S(1)}, u32[]{:S(2)}, u32[]{:S(2)}) collective-permute-start(f32[128,1536]{1,0:T(8,128)} %get-tuple-element.530), channel_id=1, source_target_pairs={{0,1},{1,0},{2,3},{3,2},{4,5},{5,4},{6,7},{7,6},{8,9},{9,8},{10,11... | collective-permute-start | bytes 2359304 | tf_op jit(solution)/shard_map/ppermute | solution.py:819
  430.2 19.8 %collective-permute-start.52 = (bf16[64,1536]{1,0:T(8,128)(2,1)}, bf16[64,1536]{1,0:T(8,128)(2,1)S(1)}, u32[]{:S(2)}, u32[]{:S(2)}) collective-permute-start(bf16[64,1536]{1,0:T(8,128)(2,1)} %get-tuple-element.521.refs_28_), channel_id=1, source_target_pairs={{0,2},{1,3},{2,0},{3,1},{4,6},{5,7},{6,4},{7,5},{8,10},{9,11},{10,... | collective-permute-start | bytes 589832 | tf_op jit(solution)/shard_map/ppermute | solution.py:819
  445.2 26.2 %collective-permute-start.55 = (f32[128,1536]{1,0:T(8,128)}, f32[128,1536]{1,0:T(8,128)S(1)}, u32[]{:S(2)}, u32[]{:S(2)}) collective-permute-start(f32[128,1536]{1,0:T(8,128)} %get-tuple-element.548), channel_id=1, source_target_pairs={{0,1},{1,0},{2,3},{3,2},{4,5},{5,4},{6,7},{7,6},{8,9},{9,8},{10,11... | collective-permute-start | bytes 2359304 | tf_op jit(solution)/shard_map/ppermute | solution.py:819
  448.4 26.7 %collective-permute-start.54 = (bf16[64,1536]{1,0:T(8,128)(2,1)}, bf16[64,1536]{1,0:T(8,128)(2,1)S(1)}, u32[]{:S(2)}, u32[]{:S(2)}) collective-permute-start(bf16[64,1536]{1,0:T(8,128)(2,1)} %get-tuple-element.532.refs_0_.refs_28_), channel_id=1, source_target_pairs={{0,2},{1,3},{2,0},{3,1},{4,6},{5,7},{6,4},{7,5},{8,10},{9,11},{10,... | collective-permute-start | bytes 589832 | tf_op jit(solution)/shard_map/ppermute | solution.py:819
  456.7 32.5 %collective-permute-start.58 = (bf16[384,768]{1,0:T(8,128)(2,1)}, bf16[384,768]{1,0:T(8,128)(2,1)S(1)}, u32[]{:S(2)}, u32[]{:S(2)}) collective-permute-start(bf16[384,768]{1,0:T(8,128)(2,1)} %get-tuple-element.534.refs_29_), channel_id=1, source_target_pairs={{0,8},{4,12},{8,0},{12,4},{16,24},{20,28},{24,16},{28,20},{1,9},{5... | collective-permute-start | bytes 1769480 | tf_op jit(solution)/shard_map/ppermute | solution.py:819
  474.6 26.4 %collective-permute-start.57 = (bf16[64,1536]{1,0:T(8,128)(2,1)}, bf16[64,1536]{1,0:T(8,128)(2,1)S(1)}, u32[]{:S(2)}, u32[]{:S(2)}) collective-permute-start(bf16[64,1536]{1,0:T(8,128)(2,1)} %get-tuple-element.549.refs_2_), channel_id=1, source_target_pairs={{0,2},{1,3},{2,0},{3,1},{4,6},{5,7},{6,4},{7,5},{8,10},{9,11},{10,... | collective-permute-start | bytes 589832 | tf_op jit(solution)/shard_map/ppermute | solution.py:819
  485.0 23.8 %collective-permute-start.56 = (bf16[64,1536]{1,0:T(8,128)(2,1)}, bf16[64,1536]{1,0:T(8,128)(2,1)S(1)}, u32[]{:S(2)}, u32[]{:S(2)}) collective-permute-start(bf16[64,1536]{1,0:T(8,128)(2,1)} %get-tuple-element.552.refs_0_), channel_id=1, source_target_pairs={{0,2},{1,3},{2,0},{3,1},{4,6},{5,7},{6,4},{7,5},{8,10},{9,11},{10,... | collective-permute-start | bytes 589832 | tf_op jit(solution)/shard_map/ppermute | solution.py:819
  492.2 132.4 %collective-permute-start.76 = (bf16[192,768]{1,0:T(8,128)(2,1)}, bf16[192,768]{1,0:T(8,128)(2,1)}, u32[]{:S(2)}, u32[]{:S(2)}) collective-permute-start(bf16[192,768]{1,0:T(8,128)(2,1)} %get-tuple-element.558.refs_3_), channel_id=1, source_target_pairs={{0,16},{4,20},{8,24},{12,28},{16,0},{20,4},{24,8},{28,12},{1,17},{... | collective-permute-start | bytes 884744 | tf_op jit(solution)/shard_map/ppermute | solution.py:819
  500.5 48.0 %collective-permute-start.66 = (bf16[768,768]{1,0:T(8,128)(2,1)}, bf16[768,768]{1,0:T(8,128)(2,1)}, u32[]{:S(2)}, u32[]{:S(2)}) collective-permute-start(bf16[768,768]{1,0:T(8,128)(2,1)} %get-tuple-element.559.refs_2_), channel_id=1, source_target_pairs={{0,4},{4,0},{8,12},{12,8},{16,20},{20,16},{24,28},{28,24},{1,5},{5... | collective-permute-start | bytes 3538952 | tf_op jit(solution)/shard_map/ppermute | solution.py:819
  506.4 19.1 %collective-permute-start.61 = (f32[80,256]{1,0:T(8,128)}, f32[80,256]{1,0:T(8,128)S(1)}, u32[]{:S(2)}, u32[]{:S(2)}) collective-permute-start(f32[80,256]{1,0:T(8,128)} %sum_small.9.refs_2_.x), channel_id=1, source_target_pairs={{0,16},{4,20},{8,24},{12,28},{16,0},{20,4},{24,8},{28,12},{1,17},{... | collective-permute-start | bytes 245768 | tf_op jit(solution)/shard_map/ppermute | solution.py:819
  513.5 24.7 %all-to-all-start.1 = ((bf16[8,32,1536]{2,1,0:T(8,128)(2,1)}), bf16[8,32,1536]{2,1,0:T(8,128)(2,1)S(1)}, u32[]{:S(2)}, u32[]{:S(2)}) async-start(bf16[8,32,1536]{2,1,0:T(8,128)(2,1)} %bitcast.16), calls=%async_computation.2 | async-start | bytes 1572864 | tf_op jit(solution)/shard_map/all_to_all | solution.py:1205
  521.7 24.0 %collective-permute-start.67 = (bf16[768,384]{1,0:T(8,128)(2,1)}, bf16[768,384]{1,0:T(8,128)(2,1)S(1)}, u32[]{:S(2)}, u32[]{:S(2)}) collective-permute-start(bf16[768,384]{1,0:T(8,128)(2,1)} %get-tuple-element.569.refs_0_), channel_id=1, source_target_pairs={{0,8},{4,12},{8,0},{12,4},{16,24},{20,28},{24,16},{28,20},{1,9},{5... | collective-permute-start | bytes 1769480 | tf_op jit(solution)/shard_map/ppermute | solution.py:819
  533.8 37.3 %collective-permute-start.69 = (bf16[768,768]{1,0:T(8,128)(2,1)}, bf16[768,768]{1,0:T(8,128)(2,1)}, u32[]{:S(2)}, u32[]{:S(2)}) collective-permute-start(bf16[768,768]{1,0:T(8,128)(2,1)} %get-tuple-element.570.refs_0_), channel_id=1, source_target_pairs={{0,8},{4,12},{8,0},{12,4},{16,24},{20,28},{24,16},{28,20},{1,9},{5... | collective-permute-start | bytes 3538952 | tf_op jit(solution)/shard_map/ppermute | solution.py:819
  541.2 21.8 %collective-permute-start.63 = (bf16[8,32,1536]{2,1,0:T(8,128)(2,1)}, bf16[8,32,1536]{2,1,0:T(8,128)(2,1)S(1)}, u32[]{:S(2)}, u32[]{:S(2)}) collective-permute-start(bf16[8,32,1536]{2,1,0:T(8,128)(2,1)} %take_parts.1.refs_0_), channel_id=1, source_target_pairs={{0,2},{1,3},{2,0},{3,1},{4,6},{5,7},{6,4},{7,5},{8,10},{9,11},{10,... | collective-permute-start | bytes 2359304 | tf_op jit(solution)/shard_map/ppermute | solution.py:819
  548.5 25.1 %collective-permute-start.72 = (bf16[384,384]{1,0:T(8,128)(2,1)}, bf16[384,384]{1,0:T(8,128)(2,1)S(1)}, u32[]{:S(2)}, u32[]{:S(2)}) collective-permute-start(bf16[384,384]{1,0:T(8,128)(2,1)} %get-tuple-element.573.refs_0_), channel_id=1, source_target_pairs={{0,4},{4,0},{8,12},{12,8},{16,20},{20,16},{24,28},{28,24},{1,5},{5... | collective-permute-start | bytes 884744 | tf_op jit(solution)/shard_map/ppermute | solution.py:819
  561.0 22.5 %collective-permute-start.71 = (bf16[384,768]{1,0:T(8,128)(2,1)}, bf16[384,768]{1,0:T(8,128)(2,1)S(1)}, u32[]{:S(2)}, u32[]{:S(2)}) collective-permute-start(bf16[384,768]{1,0:T(8,128)(2,1)} %get-tuple-element.574.refs_0_), channel_id=1, source_target_pairs={{0,8},{4,12},{8,0},{12,4},{16,24},{20,28},{24,16},{28,20},{1,9},{5... | collective-permute-start | bytes 1769480 | tf_op jit(solution)/shard_map/ppermute | solution.py:819
  563.0 31.6 %collective-permute-start.68 = (f32[24,256]{1,0:T(8,128)}, f32[24,256]{1,0:T(8,128)S(1)}, u32[]{:S(2)}, u32[]{:S(2)}) collective-permute-start(f32[24,256]{1,0:T(8,128)} %sum_small.12.refs_0_.x), channel_id=1, source_target_pairs={{0,4},{4,0},{8,12},{12,8},{16,20},{20,16},{24,28},{28,24},{1,5},{5... | collective-permute-start | bytes 73736 | tf_op jit(solution)/shard_map/ppermute | solution.py:819
  571.0 38.5 %collective-permute-start.64 = (bf16[8,64,1536]{2,1,0:T(8,128)(2,1)S(1)}, bf16[8,64,1536]{2,1,0:T(8,128)(2,1)}, u32[]{:S(2)}, u32[]{:S(2)}) collective-permute-start(bf16[8,64,1536]{2,1,0:T(8,128)(2,1)S(1)} %maximum_select_fusion.1.refs_1_), channel_id=1, source_target_pairs={{0,1},{1,0},{2,3},{3,2},{4,5},{5,4},{6,7},{7,6},{8,9},{9,8},{10,11... | collective-permute-start | bytes 4718600 | tf_op jit(solution)/shard_map/ppermute | solution.py:819
  589.6 35.0 %collective-permute-start.77 = (bf16[192,768]{1,0:T(8,128)(2,1)}, bf16[192,768]{1,0:T(8,128)(2,1)}, u32[]{:S(2)}, u32[]{:S(2)}) collective-permute-start(bf16[192,768]{1,0:T(8,128)(2,1)} %get-tuple-element.581.refs_0_), channel_id=1, source_target_pairs={{0,16},{4,20},{8,24},{12,28},{16,0},{20,4},{24,8},{28,12},{1,17},{... | collective-permute-start | bytes 884744 | tf_op jit(solution)/shard_map/ppermute | solution.py:819
  594.6 30.1 %collective-permute-start.78 = (bf16[192,768]{1,0:T(8,128)(2,1)}, bf16[192,768]{1,0:T(8,128)(2,1)}, u32[]{:S(2)}, u32[]{:S(2)}) collective-permute-start(bf16[192,768]{1,0:T(8,128)(2,1)} %get-tuple-element.582.refs_0_), channel_id=1, source_target_pairs={{0,16},{4,20},{8,24},{12,28},{16,0},{20,4},{24,8},{28,12},{1,17},{... | collective-permute-start | bytes 884744 | tf_op jit(solution)/shard_map/ppermute | solution.py:819
  (132 other events, 1234.2 us)
Sparse Core Ops, SparseCore 0:
  261.6 67.2 reduce-scatter.2
  356.7 129.6 reduce-scatter.4

commit v3 on v2

--- a/solution.py
+++ b/solution.py
@@ -9,12 +9,14 @@
 
 P_SIZE = 64
 Q = 256
+R = 128
 GC = 256
 HG = GC // P_SIZE
 LANES = 128
 EPS = 1e-05
 CHUNKS = 1
-VMEM_LIMIT = 56 * 1024 * 1024
+VMEM_LIMIT = 44 * 1024 * 1024
+VMEM_SMALL = 24 * 1024 * 1024
 
 F32 = jnp.float32
 BF16 = jnp.bfloat16
@@ -60,7 +62,7 @@
 
 def join_halves(dst, mine, theirs, core, half):
     width = mine[0].shape[-1]
-    for m in range(Q // (2 * half)):
+    for m in range(dst.shape[0] // (2 * half)):
         rows = slice(half * m, half * m + half)
         for terms, side in ((mine, core), (theirs, 1 - core)):
             total = terms[0][rows, :].astype(F32)
@@ -69,9 +71,19 @@
             dst[pl.ds(pl.multiple_of(2 * half * m + half * side, 8), half), :width] = total
 
 
+def join_quarters(dst, parts, core, place, half):
+    width, unit = parts[0].shape[-1], half // 2
+    for m in range(dst.shape[0] // (2 * half)):
+        for k, part in enumerate(parts):
+            side = (core, 1 - core)[k // 2]
+            along = (place, 1 - place)[k % 2]
+            at = pl.multiple_of(2 * half * m + half * side + unit * along, 8)
+            dst[pl.ds(at, unit), :width] = part[unit * m : unit * m + unit, :].astype(F32)
+
+
 def split_halves(src, keep, send, core, half):
     width = keep.shape[-1]
-    for m in range(Q // (2 * half)):
+    for m in range(src.shape[0] // (2 * half)):
         own = pl.multiple_of(2 * half * m + half * core, 8)
         keep[half * m : half * m + half, :] = src[pl.ds(own, half), :width].astype(keep.dtype)
         if send is not None:
@@ -112,6 +124,12 @@
     return acc
 
 
+def two_terms(column):
+    lead = column.astype(BF16).astype(F32)
+    lane = lax.broadcasted_iota(jnp.int32, (column.shape[0], LANES), 1)
+    return jnp.where(lane < P_SIZE, lead, column - lead)
+
+
 def conv_rows(buf, taps):
     out = taps[4:5, :] + taps[0:1, :] * buf[5 : 5 + Q, :]
     for k in range(1, 4):
@@ -119,13 +137,47 @@
     return out
 
 
+class Fetch:
+    def __init__(self, l, refs, bufs, sems):
+        self.l, self.refs, self.bufs, self.sems = l, refs, bufs, sems
+        self.groups = bufs[0].shape[0]
+
+    def grouped(self, kind, group):
+        src = self.refs[kind].at[self.l, :, pl.ds(pl.multiple_of(group * GC, GC), GC)]
+        return pltpu.make_async_copy(src, self.bufs[kind].at[group], self.sems.at[kind, group])
+
+    def single(self, kind):
+        return pltpu.make_async_copy(self.refs[kind].at[self.l], self.bufs[kind], self.sems.at[kind, 0])
+
+    def start(self, order, singles_first):
+        if singles_first:
+            for kind in (3, 4):
+                self.single(kind).start()
+        for group in range(self.groups):
+            for kind in order:
+                self.grouped(kind, group).start()
+        if not singles_first:
+            for kind in (3, 4):
+                self.single(kind).start()
+
+
+def fetch_scratch(width, groups):
+    return [
+        pltpu.VMEM((groups, width, GC), BF16),
+        pltpu.VMEM((groups, width, GC), BF16),
+        pltpu.VMEM((groups, width, GC), BF16),
+        pltpu.VMEM((width, 2 * LANES), BF16),
+        pltpu.VMEM((width, LANES), BF16),
+        pltpu.SemaphoreType.DMA((5, groups)),
+    ]
+
+
 def forward_kernel(first_layer, fresh, n_skip, l, half, base, inner, scal, *refs):
     it = iter(refs)
     if not first_layer:
         hid_prev = next(it)
-    count = 1 if first_layer else 2
-    mine = [next(it) for _ in range(count)]
-    theirs = [next(it) for _ in range(count)]
+    mine = [next(it), next(it)]
+    theirs = [next(it), next(it)]
     gains = next(it)
     w_gate, w_value, w_state, w_step, w_out = (next(it) for _ in range(5))
     taps_v, taps_s, heads_p, gain_in = (next(it) for _ in range(4))
@@ -133,23 +185,36 @@
         h_in, vt_in, st_in = (next(it) for _ in range(3))
     for _ in range(n_skip):
         next(it)
-    hid_out, low_out, u_out = next(it), next(it), next(it)
+    hid_hbm, low_hbm, u_out = next(it), next(it), next(it)
+    if not first_layer:
+        br_out = next(it)
     gate_out, vin_out, cv_out, y_out, sin_out, cs_out, dt_out, hs_out = (next(it) for _ in range(8))
     h_last, vt_last, st_last, keep, send = (next(it) for _ in range(5))
     buf, acc, sq, vbuf, sbuf, b_s, c_s, bt_s, s_s, step_s, cum_s, cumt_s = (
         next(it) for _ in range(12)
     )
+    low_out, out_sems = next(it), next(it)
+    bufs = [next(it) for _ in range(5)]
+    fetch = Fetch(l, (w_gate, w_value, w_out, w_state, w_step), bufs, next(it))
     gain = gains[l : l + 1, :]
     bias, decay_log = heads_p[0:1, :], heads_p[1:2, :]
 
     i, g = pl.program_id(0), pl.program_id(1)
     core = scal[0]
     width = low_out.shape[1]
+
+    def stores():
+        rows = pl.ds(pl.multiple_of(base + i * Q, Q), Q)
+        return (
+            pltpu.make_async_copy(buf.at[:, pl.ds(0, width)], hid_hbm.at[rows], out_sems.at[0]),
+            pltpu.make_async_copy(low_out, low_hbm.at[rows], out_sems.at[1]),
+        )
 
     @pl.when(g == 0)
     def _():
         @pl.when(i == 0)
         def _():
+            fetch.start((0, 1, 2), True)
             if fresh:
                 h_last[...] = jnp.zeros_like(h_last)
                 vt_last[...] = jnp.zeros_like(vt_last)
@@ -159,17 +224,30 @@
                 vt_last[...] = vt_in[...]
                 st_last[...] = st_in[...]
 
-        join_halves(buf, mine, theirs, core, half)
+        if first_layer:
+            join_quarters(buf, mine + theirs, core, scal[4], half)
+        else:
+            join_halves(buf, mine, theirs, core, half)
         if first_layer:
             token = base + i * Q + lax.broadcasted_iota(jnp.int32, (Q, 1), 0)
             hid = jnp.where(token < scal[1], buf[:, :width], 0.0)
         else:
             total = buf[:, width : width + 1] + buf[:, width + P_SIZE : width + P_SIZE + 1]
+            br_out[:, :width] = buf[:, :width].astype(BF16)
+            br_out[:, width:] = two_terms(total).astype(BF16)
             hid = hid_prev[...] + lax.rsqrt(total / inner + EPS) * buf[:, :width]
-        hid_out[...] = hid
+        buf[:, :width] = hid
         low_out[...] = (hid * lax.rsqrt(row_mean(hid * hid) + EPS) * gain).astype(BF16)
+        for copy in stores():
+            copy.start()
         low = low_out[...]
-        s_in = nn(low, w_state[...])
+
+        @pl.when(i == 0)
+        def _():
+            fetch.single(3).wait()
+            fetch.single(4).wait()
+
+        s_in = nn(low, bufs[3][...])
         sin_out[...] = s_in.astype(BF16)
         sbuf[0:8, :] = st_last[...]
         sbuf[8 : 8 + Q, :] = s_in
@@ -182,7 +260,7 @@
         c_s[...] = c_val.astype(BF16)
         bt_s[...] = b_val.T.astype(BF16)
         s_s[...] = nt(c_s[...], b_s[...])
-        dt = nn(low, w_step[...])
+        dt = nn(low, bufs[4][...])
         dt_out[...] = dt
         step = softplus(dt + bias)
         cum = -exact(triangle(True).astype(F32), step * jnp.exp(decay_log))
@@ -192,10 +270,15 @@
         acc[...] = jnp.zeros_like(acc)
         sq[...] = jnp.zeros_like(sq)
 
+    @pl.when(i == 0)
+    def _():
+        fetch.grouped(0, g).wait()
+        fetch.grouped(1, g).wait()
+
     low = low_out[...]
-    gate = nn(low, w_gate[...])
-    gate_out[...] = gate
-    v_in = nn(low, w_value[...])
+    gate = nn(low, bufs[0][g])
+    gate_out[...] = gate.astype(BF16)
+    v_in = nn(low, bufs[1][g])
     vin_out[...] = v_in.astype(BF16)
     vbuf[0:8, :] = vt_last[g]
     vbuf[8 : 8 + Q, :] = v_in
@@ -230,12 +313,19 @@
     gated = (y + skip_row(heads_p, g) * val) * (gate * sigmoid(gate))
     sq[...] += jnp.sum(gated * gated, axis=1, keepdims=True)
     u_out[...] = (gated * gain_in[...]).astype(BF16)
-    acc[:, :width] += nt(u_out[...], w_out[...])
+
+    @pl.when(i == 0)
+    def _():
+        fetch.grouped(2, g).wait()
+
+    acc[:, :width] += nt(u_out[...], bufs[2][g])
 
     @pl.when(g == pl.num_programs(1) - 1)
     def _():
-        acc[:, width:] = jnp.broadcast_to(sq[:, 0:1], (Q, LANES))
+        acc[:, width:] = two_terms(sq[:, 0:1])
         split_halves(acc, keep, send, core, half)
+        for copy in stores():
+            copy.wait()
 
 
 def norm_kernel(top, bottom, fresh, n_skip, l, half, base, inner, scal, *refs):
@@ -246,7 +336,10 @@
     else:
         dh_prev = next(it)
         dl_mine, dl_theirs = ([next(it), next(it)] for _ in range(2))
-    br_mine, br_theirs = ([next(it), next(it)] for _ in range(2))
+    if top:
+        br_mine, br_theirs = ([next(it), next(it)] for _ in range(2))
+    else:
+        br_ref = next(it)
     gains = next(it)
     if not fresh:
         gain_c = next(it)
@@ -263,7 +356,10 @@
     def _():
         gain_acc[...] = jnp.zeros_like(gain_acc) if fresh else gain_c[...]
 
-    join_halves(buf, br_mine, br_theirs, core, half)
+    if top:
+        join_halves(buf, br_mine, br_theirs, core, half)
+    else:
+        buf[...] = br_ref[...].astype(F32)
     total = buf[:, width : width + 1] + buf[:, width + P_SIZE : width + P_SIZE + 1]
     scale = lax.rsqrt(total / inner + EPS)
     hid = hid_ref[...]
@@ -272,7 +368,7 @@
     r = lax.rsqrt(row_mean(hid * hid) + EPS)
     normed = hid * r
     if top:
-        token = base + pl.program_id(0) * Q + lax.broadcasted_iota(jnp.int32, (Q, 1), 0)
+        token = base + pl.program_id(0) * R + lax.broadcasted_iota(jnp.int32, (R, 1), 0)
         valid = token < scal[1]
         result[...] = jnp.where(valid, normed * gain, 0.0).astype(BF16)
         upper = jnp.where(valid, cot[...].astype(F32), 0.0)
@@ -288,7 +384,7 @@
     gb_out[...] = gb
     gbs_out[...] = (dh * scale).astype(BF16)
     stat = jnp.sum(gb.astype(F32) * buf[:, :width], axis=1, keepdims=True)
-    lane = lax.broadcasted_iota(jnp.int32, (Q, LANES), 1)
+    lane = lax.broadcasted_iota(jnp.int32, (R, LANES), 1)
     rows_out[...] = jnp.where(lane == 0, scale, scale * scale * scale * stat / inner)
     if bottom:
         low[...] = dh
@@ -314,6 +410,8 @@
     b_s, c_s, ct_s, st_s, step_s, cum_s, cumt_s, dcum_s, dstep_s, end_s = (
         next(it) for _ in range(10)
     )
+    bufs = [next(it) for _ in range(5)]
+    fetch = Fetch(l, (w_gate, w_value, w_out, w_state, w_step), bufs, next(it))
 
     i, g = pl.program_id(0), pl.program_id(1)
     core = scal[0]
@@ -323,6 +421,7 @@
     def _():
         @pl.when(i == 0)
         def _():
+            fetch.start((2, 0, 1), False)
             if fresh:
                 d_state[...] = jnp.zeros_like(d_state)
                 acc_v[...] = jnp.zeros_like(acc_v)
@@ -356,11 +455,16 @@
 
     scale, coef = rows_ref[:, 0:1], rows_ref[:, 1:2]
     skip = skip_row(heads_p, g)
-    d_go = nn(gb_ref[...], w_out[...])
+
+    @pl.when(i == 0)
+    def _():
+        fetch.grouped(2, g).wait()
+
+    d_go = nn(gb_ref[...], bufs[2][g])
     cv = cv_ref[...]
     sig_v = sigmoid(cv)
     val = cv * sig_v
-    gate = gate_ref[...]
+    gate = gate_ref[...].astype(F32)
     sig_g = sigmoid(gate)
     silu_g = gate * sig_g
     y = y_ref[...]
@@ -433,7 +537,13 @@
         acc_v[g, k : k + 1, :] += col_sum(v_in * shifted)
     d_vin_b = d_vin.astype(BF16)
     dval_out[...] = d_vin_b
-    acc[...] += nt(d_gate, w_gate[...]) + nt(d_vin_b, w_value[...])
+
+    @pl.when(i == 0)
+    def _():
+        fetch.grouped(0, g).wait()
+        fetch.grouped(1, g).wait()
+
+    acc[...] += nt(d_gate, bufs[0][g]) + nt(d_vin_b, bufs[1][g])
 
     @pl.when(g == pl.num_programs(1) - 1)
     def _():
@@ -464,7 +574,13 @@
             acc_s[k : k + 1, :] += col_sum(s_in * shifted)
         d_sin_b = d_sin.astype(BF16)
         dst_out[...] = d_sin_b
-        acc[...] += nt(d_sin_b, w_state[...]) + nt(d_step_b, w_step[...])
+
+        @pl.when(i == 0)
+        def _():
+            fetch.single(3).wait()
+            fetch.single(4).wait()
+
+        acc[...] += nt(d_sin_b, bufs[3][...]) + nt(d_step_b, bufs[4][...])
         split_halves(acc, keep, send, core, half)
 
 
@@ -489,13 +605,8 @@
         send[half * m : half * m + half, :] = buf[pl.ds(other, half), :].astype(BF16)
 
 
-def layer_specs(l, width):
-    return [
-        pl.BlockSpec((None, width, GC), lambda i, g: (l, 0, g)),
-        pl.BlockSpec((None, width, GC), lambda i, g: (l, 0, g)),
-        pl.BlockSpec((None, width, 2 * LANES), lambda i, g: (l, 0, 0)),
-        pl.BlockSpec((None, width, LANES), lambda i, g: (l, 0, 0)),
-        pl.BlockSpec((None, width, GC), lambda i, g: (l, 0, g)),
+def layer_specs(l):
+    return [pl.BlockSpec(memory_space=pl.ANY)] * 5 + [
         pl.BlockSpec((None, 5, GC), lambda i, g: (l, 0, g)),
         pl.BlockSpec((None, 5, 2 * LANES), lambda i, g: (l, 0, 0)),
         pl.BlockSpec((None, 8, LANES), lambda i, g: (l, 0, 0)),
@@ -503,27 +614,34 @@
     ]
 
 
+class Far:
+    def __init__(self, value):
+        self.value = value
+
+
 class Call:
     def __init__(self):
         self.in_specs, self.args, self.out_specs, self.out_shape = [], [], [], []
         self.aliases, self.tail = {}, []
 
-    def take(self, spec, arg):
+    def take(self, spec, arg, stay=False):
         self.in_specs.append(spec)
-        self.args.append(arg)
-
-    def give(self, spec, dims, dtype=F32, into=None):
+        self.args.append(pltpu.with_memory_space_constraint(arg, pltpu.HBM) if stay else arg)
+
+    def give(self, spec, dims, dtype=F32, into=None, keep=False):
         if into is not None:
             self.tail.append((into, len(self.out_specs)))
         self.out_specs.append(spec)
-        self.out_shape.append(jax.ShapeDtypeStruct(dims, dtype))
+        kind = pltpu.HBM if keep else jax.ShapeDtypeStruct
+        self.out_shape.append(kind(dims, dtype))
 
     def run(self, kernel, grid, scratch, after, micros, name):
         for arg, out in self.tail:
             self.aliases[len(self.args)] = out
             self.take(pl.BlockSpec(memory_space=pl.ANY), arg)
         for arg in after:
-            self.take(pl.BlockSpec(memory_space=pl.ANY), arg)
+            stay = isinstance(arg, Far)
+            self.take(pl.BlockSpec(memory_space=pl.ANY), arg.value if stay else arg, stay)
         return pl.pallas_call(
             functools.partial(kernel, len(self.tail) + len(after)),
             grid=grid,
@@ -533,7 +651,8 @@
             scratch_shapes=scratch,
             input_output_aliases=self.aliases,
             compiler_params=pltpu.CompilerParams(
-                dimension_semantics=("arbitrary",) * len(grid), vmem_limit_bytes=VMEM_LIMIT
+                dimension_semantics=("arbitrary",) * len(grid),
+                vmem_limit_bytes=(VMEM_LIMIT if name.startswith("layer") else VMEM_SMALL),
             ),
             cost_estimate=pl.CostEstimate(
                 flops=int(micros * 1.1e9), bytes_accessed=1_000_000, transcendentals=0
@@ -566,34 +685,38 @@
     call = Call()
     call.take(smem(), scal)
     if not first:
-        call.take(block(Q, width), hid_prev)
+        call.take(block(Q, width), hid_prev, stay=True)
     for term in halves:
-        call.take(block(Q // 2, term.shape[1], halves_at), term)
+        call.take(block(Q // 4 if first else Q // 2, term.shape[1], halves_at), term, stay=first)
     call.take(full(gains.shape, 2), gains)
-    for spec, arg in zip(layer_specs(l, width), weights):
-        call.take(spec, arg)
+    for k, (spec, arg) in enumerate(zip(layer_specs(l), weights)):
+        call.take(spec, arg, stay=k < 5)
     carry_shapes = [(groups, LANES, GC), (groups, 8, GC), (8, 2 * LANES)]
     if not fresh:
         for dims, arg in zip(carry_shapes, carry):
             call.take(full(dims, len(dims)), arg)
     into = filled if filled is not None else (None,) * 3
-    call.give(block(Q, width), (rows_all, width), F32, into[0])
-    call.give(block(Q, width), (rows_all, width), BF16, into[1])
-    call.give(grouped(Q, GC), (rows_all, cols), BF16, into[2])
-    call.give(grouped(Q, GC, 0), (rows, cols))
-    call.give(grouped(Q, GC, 0), (rows, cols), BF16)
-    call.give(grouped(Q, GC, 0), (rows, cols))
-    call.give(grouped(Q, GC, 0), (rows, cols))
-    call.give(block(Q, 2 * LANES, 0), (rows, 2 * LANES), BF16)
-    call.give(block(Q, 2 * LANES, 0), (rows, 2 * LANES))
-    call.give(block(Q, LANES, 0), (rows, LANES))
+    call.give(pl.BlockSpec(memory_space=pl.ANY), (rows_all, width), F32, into[0], keep=True)
+    call.give(pl.BlockSpec(memory_space=pl.ANY), (rows_all, width), BF16, into[1], keep=True)
+    call.give(grouped(Q, GC), (rows_all, cols), BF16, into[2], keep=True)
+    if not first:
+        call.give(block(Q, width + LANES, 0), (rows, width + LANES), BF16, keep=True)
+    call.give(grouped(Q, GC, 0), (rows, cols), BF16, keep=True)
+    call.give(grouped(Q, GC, 0), (rows, cols), BF16, keep=True)
+    call.give(grouped(Q, GC, 0), (rows, cols), keep=True)
+    call.give(grouped(Q, GC, 0), (rows, cols), keep=True)
+    call.give(block(Q, 2 * LANES, 0), (rows, 2 * LANES), BF16, keep=True)
+    call.give(block(Q, 2 * LANES, 0), (rows, 2 * LANES), keep=True)
+    call.give(block(Q, LANES, 0), (rows, LANES), keep=True)
     call.give(
-        pl.BlockSpec((None, None, LANES, GC), lambda i, g: (i, g, 0, 0)), (chunks, groups, LANES, GC)
+        pl.BlockSpec((None, None, LANES, GC), lambda i, g: (i, g, 0, 0)),
+        (chunks, groups, LANES, GC),
+        keep=True,
     )
     for dims in carry_shapes:
         call.give(full(dims, len(dims)), dims)
-    for _ in range(2):
-        call.give(block(Q // 2, width + LANES, 0), (rows // 2, width + LANES))
+    for dtype in (F32, BF16):
+        call.give(block(Q // 2, width + LANES, 0), (rows // 2, width + LANES), dtype)
     scratch = [
         pltpu.VMEM((Q, width + LANES), F32),
         pltpu.VMEM((Q, width + LANES), F32),
@@ -607,49 +730,53 @@
         pltpu.VMEM((Q, LANES), F32),
         pltpu.VMEM((Q, LANES), F32),
         pltpu.VMEM((LANES, Q), F32),
-    ]
+        pltpu.VMEM((Q, width), BF16),
+        pltpu.SemaphoreType.DMA((2,)),
+    ] + fetch_scratch(width, groups)
 
     def kernel(n_skip, *refs):
         forward_kernel(first, fresh, n_skip, l, half, chunk * Q, inner, *refs)
 
     outs = call.run(kernel, (chunks, groups), scratch, after, 12 * chunks, "layer_forward")
-    return tuple(outs[:3]), tuple(outs[3:11]), tuple(outs[11:14]), outs[14], outs[15]
+    outs = list(outs)
+    below = None if first else outs.pop(3)
+    return tuple(outs[:3]), below, tuple(outs[3:11]), tuple(outs[11:14]), outs[14], outs[15]
 
 
 def norm_call(l, top, bottom, chunk, chunks, half, inner, scal, hid, lead, lows, branch, gains, gain_c, filled, after):
     rows_all, width = hid.shape
     fresh = gain_c is None
 
-    def block(h, w, at=chunk):
+    def block(h, w, at=chunk * (Q // R)):
         return pl.BlockSpec((h, w), lambda i: (at + i, 0))
 
     call = Call()
     call.take(smem(), scal)
-    call.take(block(Q, width), hid)
-    call.take(block(Q, width), lead)
+    call.take(block(R, width), hid, stay=True)
+    call.take(block(R, width), lead, stay=True)
     if not top:
         for side in lows:
-            call.take(block(Q // 2, width, 0), side)
+            call.take(block(R // 2, width, 0), side)
     for side in branch:
-        call.take(block(Q // 2, width + LANES, 0), side)
+        call.take(block(R // 2 if top else R, width + LANES, 0), side, stay=not top)
     call.take(full(gains.shape, 2), gains)
     if not fresh:
         call.take(full((8, width), 2), gain_c)
     into = filled if filled is not None else (None,) * 5
     if top:
-        call.give(block(Q, width), (rows_all, width), BF16, into[4])
+        call.give(block(R, width), (rows_all, width), BF16, into[4], keep=True)
     part = 2 if bottom else 1
-    call.give(block(Q // part, width), (rows_all // part, width), F32, into[0])
-    call.give(block(Q, width), (rows_all, width), BF16, into[1])
-    call.give(block(Q, width), (rows_all, width), BF16, into[2])
-    call.give(block(Q, LANES), (rows_all, LANES), F32, into[3])
+    call.give(block(R // part, width), (rows_all // part, width), F32, into[0], keep=True)
+    call.give(block(R, width), (rows_all, width), BF16, into[1], keep=True)
+    call.give(block(R, width), (rows_all, width), BF16, into[2], keep=True)
+    call.give(block(R, LANES), (rows_all, LANES), F32, into[3])
     call.give(full((8, width), 2), (8, width))
-    scratch = [pltpu.VMEM((Q, width + LANES), F32), pltpu.VMEM((Q, width), F32)]
+    scratch = [pltpu.VMEM((R, width + LANES), F32), pltpu.VMEM((R, width), F32)]
 
     def kernel(n_skip, *refs):
         norm_kernel(top, bottom, fresh, n_skip, l, half, chunk * Q, inner, *refs)
 
-    outs = call.run(kernel, (chunks,), scratch, after, 4 * chunks, "norm_backward")
+    outs = call.run(kernel, (chunks * (Q // R),), scratch, after, 12 * chunks, "norm_backward")
     result = None
     if top:
         result, outs = outs[0], outs[1:]
@@ -671,10 +798,10 @@
 
     call = Call()
     call.take(smem(), scal)
-    call.take(block(Q, width), gb)
+    call.take(block(Q, width), gb, stay=True)
     call.take(block(Q, LANES), rows_f)
-    for spec, arg in zip(layer_specs(l, width), weights):
-        call.take(spec, arg)
+    for k, (spec, arg) in enumerate(zip(layer_specs(l), weights)):
+        call.take(spec, arg, stay=k < 5)
     specs = [
         grouped(Q, GC, 0),
         grouped(Q, GC, 0),
@@ -686,18 +813,18 @@
         pl.BlockSpec((None, None, LANES, GC), lambda i, g: (chunks - 1 - i, g, 0, 0)),
     ]
     for spec, arg in zip(specs, saved):
-        call.take(spec, arg)
+        call.take(spec, arg, stay=True)
     carry_shapes = [(groups, LANES, GC), (groups, 16, GC), (16, 2 * LANES), (8, LANES)]
     if not fresh:
         for dims, arg in zip(carry_shapes, carry):
             call.take(full(dims, len(dims)), arg)
     into = filled if filled is not None else (None,) * 4
-    call.give(grouped(Q, GC), (rows_all, cols), BF16, into[0])
-    call.give(grouped(Q, GC), (rows_all, cols), BF16, into[1])
-    call.give(block(Q, 2 * LANES), (rows_all, 2 * LANES), BF16, into[2])
-    call.give(block(Q, LANES), (rows_all, LANES), BF16, into[3])
-    for _ in range(2):
-        call.give(block(Q // 2, width, 0), (rows // 2, width))
+    call.give(grouped(Q, GC), (rows_all, cols), BF16, into[0], keep=True)
+    call.give(grouped(Q, GC), (rows_all, cols), BF16, into[1], keep=True)
+    call.give(block(Q, 2 * LANES), (rows_all, 2 * LANES), BF16, into[2], keep=True)
+    call.give(block(Q, LANES), (rows_all, LANES), BF16, into[3], keep=True)
+    for dtype in (F32, BF16):
+        call.give(block(Q // 2, width, 0), (rows // 2, width), dtype)
     for dims in carry_shapes:
         call.give(full(dims, len(dims)), dims)
     scratch = [
@@ -717,7 +844,7 @@
         pltpu.VMEM((Q, LANES), F32),
         pltpu.VMEM((Q, LANES), F32),
         pltpu.VMEM((8, LANES), F32),
-    ]
+    ] + fetch_scratch(width, groups)
 
     def kernel(n_skip, *refs):
         backward_kernel(fresh, n_skip, l, half, *refs)
@@ -735,12 +862,12 @@
         step *= 2
     call = Call()
     call.take(smem(), scal)
-    call.take(pl.BlockSpec((tokens, step), lambda r: (0, r)), a)
+    call.take(pl.BlockSpec((tokens, step), lambda r: (0, r)), a, stay=True)
     for d in ds:
-        call.take(full(d.shape, 2), d)
+        call.take(full(d.shape, 2), d, stay=True)
     parts = 1 if bit is None else 2
     for _ in range(parts):
-        call.give(pl.BlockSpec((step // parts, total), lambda r: (r, 0)), (width // parts, total), BF16)
+        call.give(pl.BlockSpec((step // parts, total), lambda r: (r, 0)), (width // parts, total), BF16, keep=True)
     scratch = [] if bit is None else [pltpu.VMEM((step, total), F32)]
 
     def kernel(n_skip, *refs):
@@ -794,6 +921,16 @@
     return call.run(kernel, (), [], after, 2, "take_parts")[0]
 
 
+def touch_call(value, after):
+    call = Call()
+    call.give(pl.BlockSpec(memory_space=pl.ANY), value.shape, value.dtype, value)
+
+    def kernel(n_skip, *refs):
+        pass
+
+    return call.run(kernel, (), [], after, 1, "touch")[0]
+
+
 class Butterfly:
     def __init__(self, value, steps):
         self.value, self.steps = value, list(steps)
@@ -838,7 +975,7 @@
         self.left.remove(bit)
         self.keep, send = scatter_call(self.keep, self.recv, unit, place_of(bit), scal, after)
         self.recv = swap(send, "dp", bit)
-        return send
+        return Far(send)
 
 
 def finish_call(items, after):
@@ -847,9 +984,9 @@
     for scatter, upper, parts in items:
         rows = scatter.keep.shape[0]
         for arg in (scatter.keep, scatter.recv):
-            call.take(pl.BlockSpec(arg.shape, lambda r: (0, 0)), arg)
+            call.take(pl.BlockSpec(arg.shape, lambda r: (0, 0)), arg, stay=True)
         for wide, at in parts:
-            call.take(pl.BlockSpec((rows, wide), lambda r, j=at // wide: (0, j)), upper)
+            call.take(pl.BlockSpec((rows, wide), lambda r, j=at // wide: (0, j)), upper, stay=True)
             call.give(pl.BlockSpec((2, rows, wide), lambda r: (0, 0, 0)), (2, rows, wide))
             count += 1
 
@@ -882,15 +1019,11 @@
 
     def kernel(n_skip, a, b, *refs):
         out = refs[-1]
-        total = a[...] + b[...]
-        if wide == width:
-            out[...] = total.astype(BF16)
-        else:
-            out[:, :width] = total[:, :width].astype(BF16)
-            tail = total[:, width:]
-            lead = tail.astype(BF16).astype(F32)
-            lane = lax.broadcasted_iota(jnp.int32, tail.shape, 1)
-            out[:, width:] = jnp.where(lane < P_SIZE, lead, tail - lead).astype(BF16)
+        total = a[...] + b[...].astype(F32)
+        out[:, :width] = total[:, :width].astype(BF16)
+        if wide > width:
+            column = total[:, width : width + 1] + total[:, width + P_SIZE : width + P_SIZE + 1]
+            out[:, width:] = two_terms(column).astype(BF16)
 
     return call.run(kernel, (2,), [], after, 2, "add_pair")[0]
 
@@ -906,18 +1039,20 @@
     call.give(pl.BlockSpec(memory_space=pltpu.VMEM), (rows // 2, wide), BF16)
 
     def kernel(n_skip, place_ref, a, b, *refs):
-        mine, other, buf = refs[-3:]
+        mine, other, buf, came = refs[-4:]
         place = place_ref[4]
+        came[...] = b[...].astype(F32)
         for m in range(rows // half):
             for dst, side in ((mine, place), (buf, 1 - place)):
                 at = pl.multiple_of(half * m + unit * side, 8)
-                dst[unit * m : unit * m + unit, :] = a[pl.ds(at, unit), :] + b[pl.ds(at, unit), :]
+                dst[unit * m : unit * m + unit, :] = a[pl.ds(at, unit), :] + came[pl.ds(at, unit), :]
         other[...] = buf[...].astype(BF16)
 
-    return call.run(kernel, (), [pltpu.VMEM((rows // 2, wide), F32)], after, 2, "add_quarter")
-
-
-def last_call(mine, other, d_hid, x_mine, chunk, half, scal, gains, gain_c, filled, after):
+    scratch = [pltpu.VMEM((rows // 2, wide), F32), pltpu.VMEM((rows, wide), F32)]
+    return call.run(kernel, (), scratch, after, 2, "add_quarter")
+
+
+def last_call(mine, other, d_hid, x_parts, chunk, half, scal, gains, gain_c, filled, after):
     rows, wide = mine.shape
     unit = half // 2
     fresh = gain_c is None
@@ -925,24 +1060,25 @@
     call.take(smem(), scal)
     part = pl.BlockSpec((rows, wide), lambda r: (0, 0))
     whole = pl.BlockSpec((2 * rows, wide), lambda r: (chunk, 0))
-    for spec, arg in ((part, mine), (part, other), (whole, d_hid), (whole, x_mine)):
-        call.take(spec, arg)
+    x_part = pl.BlockSpec((rows, wide), lambda r: (max(chunk - 1, 0), 0))
+    for spec, arg in ((part, mine), (part, other), (whole, d_hid), (x_part, x_parts[min(chunk, 1)][0])):
+        call.take(spec, arg, stay=spec is whole or spec is x_part)
     call.take(full(gains.shape, 2), gains)
     if not fresh:
         call.take(full((8, wide), 2), gain_c)
-    call.give(pl.BlockSpec((rows, wide), lambda r: (chunk, 0)), (d_hid.shape[0] // 2, wide), BF16, filled)
+    call.give(pl.BlockSpec((rows, wide), lambda r: (chunk, 0)), (d_hid.shape[0] // 2, wide), BF16, filled, keep=True)
     call.give(full((8, wide), 2), (8, wide))
 
     def kernel(n_skip, place_ref, a, b, dh_ref, x_ref, gain_ref, *refs):
-        out, gain_acc, x_s, x_q, dh_q = refs[-5:]
+        out, gain_acc, x_q, dh_q = refs[-4:]
         place = place_ref[4]
-        x_s[...] = x_ref[...].astype(F32)
+        x_q[...] = x_ref[...].astype(F32)
         for m in range(rows // unit):
             at = pl.multiple_of(half * m + unit * place, 8)
             dst = slice(unit * m, unit * m + unit)
             token = chunk * Q + (2 * half) * m + half * place_ref[0] + unit * place
             token = token + lax.broadcasted_iota(jnp.int32, (unit, 1), 0)
-            x_q[dst, :] = jnp.where(token < place_ref[1], x_s[pl.ds(at, unit), :], 0.0)
+            x_q[dst, :] = jnp.where(token < place_ref[1], x_q[dst, :], 0.0)
             dh_q[dst, :] = jnp.where(token < place_ref[1], dh_ref[pl.ds(at, unit), :], 0.0)
         hid = x_q[...]
         r = lax.rsqrt(row_mean(hid * hid) + EPS)
@@ -954,11 +1090,7 @@
         back = r * (dn - normed * row_mean(dn * normed))
         out[...] = (dh_q[...] + back).astype(BF16)
 
-    scratch = [
-        pltpu.VMEM((2 * rows, wide), F32),
-        pltpu.VMEM((rows, wide), F32),
-        pltpu.VMEM((rows, wide), F32),
-    ]
+    scratch = [pltpu.VMEM((rows, wide), F32), pltpu.VMEM((rows, wide), F32)]
     return call.run(kernel, (1,), scratch, after, 4, "norm_last")
 
 
@@ -967,10 +1099,10 @@
     call = Call()
     call.take(smem(), scal)
     spec = pl.BlockSpec((2 * unit, wide), lambda r: (r, 0))
-    call.take(spec, keep)
-    call.take(spec, recv)
+    call.take(spec, keep, stay=True)
+    call.take(spec, recv, stay=True)
     for _ in range(2):
-        call.give(pl.BlockSpec((unit, wide), lambda r: (r, 0)), (rows // 2, wide), BF16)
+        call.give(pl.BlockSpec((unit, wide), lambda r: (r, 0)), (rows // 2, wide), BF16, keep=True)
 
     def kernel(n_skip, place_ref, a, b, *refs):
         own = place_ref[place_at]
@@ -1042,11 +1174,15 @@
     parts = [lax.rem(me // bit, 2) for bit in bits]
     scal = jnp.stack([core, length] + parts[:2] + [place] + parts[2:]).astype(jnp.int32)
 
-    x_half = lax.dynamic_slice_in_dim(x_in, core * half, half, axis=1)
-    x_dealt = jnp.take(x_half, deal_order, axis=0)
-    x_mine = lax.all_to_all(x_dealt, "dp", split_axis=0, concat_axis=0, tiled=True)
-    x_mine = x_mine.reshape(slot_len // 2, width)
-    x_theirs = swap(x_mine, "tensor", 1)
+    quarter = half // 2
+    x_own = lax.dynamic_slice_in_dim(x_in, core * half + place * quarter, quarter, axis=1)
+    x_dealt = jnp.take(x_own, deal_order, axis=0)
+    x_own = lax.all_to_all(x_dealt, "dp", split_axis=0, concat_axis=0, tiled=True)
+    x_own = x_own.reshape(slot_len // 4, width)
+    x_first, x_rest = x_own[: Q // 4], x_own[Q // 4 :]
+    along = swap(x_first, "tensor", 2)
+    x_parts = [(x_first, along, swap(x_first, "tensor", 1), swap(along, "tensor", 1))]
+    x_rest_along, x_rest_pair = swap(x_rest, "tensor", 2), swap(x_rest, "tensor", 1)
 
     heads_p = jnp.pad(
         jnp.stack([step_bias, decay_log, skip_gain], axis=1), ((0, 0), (0, 5), (0, LANES - heads))
@@ -1072,31 +1208,33 @@
         return [entries[1][2]] if len(entries) > 1 else []
 
     entries_add = sums.add
-    filled_f, saves, branches = [], [], []
+    filled_f, saves, branches, belows = [], [], [], []
     prior = None
     for l in range(layers):
         carry, filled, save_l, branch_l = None, None, [], []
         for c in range(calls):
             if l == 0:
-                lead = (None, (x_mine, x_theirs), c * CHUNKS)
+                if c == 1:
+                    along = touch_call(x_rest_along, [prior])
+                    x_parts.append((x_rest, along, x_rest_pair, swap(along, "tensor", 1)))
+                lead = (None, x_parts[min(c, 1)], max(c - 1, 0))
             else:
                 lead = (filled_f[l - 1][0], branches[l - 1][c][3], 0)
             after = due(sums.open, prior)
             if len(sums.open) > 2:
                 after.append(sums.open[2][3][1])
-            filled, saved, carry, keep, send = forward_call(
+            filled, below, saved, carry, keep, send = forward_call(
                 l, c * CHUNKS, CHUNKS, half, inner, slot_len, scal, *lead, norm_gains, weights, carry, filled, after
             )
             prior = keep
             save_l.append(saved)
             sums.start(keep, send)
             branch_l.append(sums.open[0])
+            belows.append((below,))
         filled_f.append(filled)
         saves.append(save_l)
         branches.append(branch_l)
-    for entry in (sums.open[1], sums.open[0]):
-        if entry[2] is None:
-            prior = sums.add(entry, [prior])
+    prior = sums.add(sums.open[1], [prior])
 
     swapped = [bits[1], bits[0]] + bits[2:]
     lows = [(None,) * 4] * calls
@@ -1110,8 +1248,10 @@
         filled_n, gain_c = None, None
         for c in order:
             after = [prior] if c == order[0] else []
+            if top and c == order[2]:
+                after = [sums.add(sums.open[0], [gain_c])]
             filled_n, gain_c = norm_call(
-                l, top, bottom, c * CHUNKS, CHUNKS, half, inner, scal, hid, lead, lows[c][3] if not top else None, branches[l][c][3], norm_gains, gain_c, filled_n, after
+                l, top, bottom, c * CHUNKS, CHUNKS, half, inner, scal, hid, lead, lows[c][3] if not top else None, branches[l][c][3] if top else belows[(l + 1) * calls + c], norm_gains, gain_c, filled_n, after
             )
         if top:
             result = filled_n[4]
@@ -1127,17 +1267,17 @@
             out_send = weight_call(filled_n[2], [u_all], piece, scal, None, [])[0]
             out = Offload(out_send)
         g_outs.insert(0, out)
-        prior = out_send
+        prior = Far(out_send)
         for at, c in enumerate(reversed(range(calls))):
             after = due(sums.open, prior)
             if not sums.open:
-                after = [out_send]
+                after = [Far(out_send)]
             if bottom:
                 if at >= 3:
                     after.append(out.step(scal, [after[0]]))
                 if at >= 2 and len(sums.open) > 2:
                     last, gain_first = last_call(
-                        *sums.open[2][3], filled_n[0], x_mine, (c + 3) * CHUNKS, half, scal, norm_gains, gain_first, last, [prior]
+                        *sums.open[2][3], filled_n[0], x_parts, (c + 3) * CHUNKS, half, scal, norm_gains, gain_first, last, [prior]
                     )
                     after.append(gain_first)
             elif len(sums.open) > 2:
@@ -1155,13 +1295,14 @@
         if not bottom:
             prior = sums.add(sums.open[1], [prior])
             prior = sums.add(sums.open[0], [prior])
-            after = [prior, out.value]
-            prior = weight_call(low_all, [d_val, d_gate, d_st, d_step], piece, scal, None, after)[0]
-            g_ins.insert(0, Offload(prior))
+            after = [prior, Far(out.value)]
+            in_send = weight_call(low_all, [d_val, d_gate, d_st, d_step], piece, scal, None, after)[0]
+            g_ins.insert(0, Offload(in_send))
+            prior = Far(in_send)
 
     def finish_rows(entry, chunk, after):
         return last_call(
-            *entry[3], filled_n[0], x_mine, chunk * CHUNKS, half, scal, norm_gains, gain_first, last, after
+            *entry[3], filled_n[0], x_parts, chunk * CHUNKS, half, scal, norm_gains, gain_first, last, after
         )
 
     groups = cols // GC
@@ -1179,11 +1320,9 @@
     small = Butterfly(pack_call(layers * per_layer, GC, moves, [gain_first]), dp_steps)
     prior = sums.add_quarter(sums.open[0], [small.value])
     prior = small.step([prior])
-    while out.order:
-        prior = out.step(scal, [prior])
     val_keep, val_send = weight_call(low_all, [d_val], piece, scal, bits[0], [prior])
     val = Scatter(val_keep, val_send, piece, bits)
-    last, gain_first = finish_rows(sums.open[1], 1, [val_send])
+    last, gain_first = finish_rows(sums.open[1], 1, [Far(val_send)])
     prior = small.step([gain_first])
     last, gain_first = finish_rows(sums.open[0], 0, [prior])
     rows = 8 * layers
@@ -1195,21 +1334,21 @@
     )
     misc_keep, misc_send = weight_call(low_all, [d_st, d_step], piece, scal, swapped[0], [rest_small.value])
     misc = Scatter(misc_keep, misc_send, piece, swapped)
-    prior = rest_small.step([misc_send])
+    prior = rest_small.step([Far(misc_send)])
     while small.came is not None:
         prior = small.step([prior])
     gate_keep, gate_send = weight_call(low_all, [d_gate], piece, scal, swapped[0], [prior])
     gate = Scatter(gate_keep, gate_send, piece, swapped)
-    quarter = half // 2
     grad_in = last.reshape(dp, quarter, width)
     returned = lax.all_to_all(grad_in, "dp", split_axis=0, concat_axis=0, tiled=True)
     places = jnp.arange(dp)
     inverse = jnp.sum(jnp.where(deal_order[None, :] == places[:, None], places[None, :], 0), axis=1)
-    arrived = take_call(returned, inverse.astype(jnp.int32), [gate_send])
+    arrived = take_call(returned, inverse.astype(jnp.int32), [Far(gate_send)])
     prior = misc.step(scal, [arrived])
     prior = val.step(scal, [prior])
+    while out.order:
+        prior = out.step(scal, [prior])
     prior = rest_small.step([prior])
-    prior = gate.step(scal, [prior])
 
     def side_by_side(mine, theirs, first):
         return jnp.where(
@@ -1222,25 +1361,30 @@
     grad_x = side_by_side(joined, swap(joined, "tensor", 1), core)
 
     upper = g_ins[0].value
-    prior = misc.step(scal, [prior, joined])
-    prior = val.step(scal, [prior])
-    prior = gate.step(scal, [prior])
+    while misc.order:
+        prior = misc.step(scal, [prior])
+    prior = gate.step(scal, [prior, joined])
+    g_state, g_step, g_out = finish_call(
+        [
+            (misc, upper, [(2 * LANES, 2 * cols), (LANES, 2 * cols + 2 * LANES)]),
+            (out, g_outs[1].value, [(cols, 0)]),
+        ],
+        [prior],
+    )
+    g_state = Butterfly(g_state.reshape(-1, 2 * LANES), [("tensor", 1), ("tensor", 2)])
+    prior = val.step(scal, [g_step])
+    prior = g_state.step([prior])
     prior = rest_small.step([prior])
     while gate.order:
-        for scatter in (misc, val, gate):
-            prior = scatter.step(scal, [prior])
-    g_state, g_step = finish_call(
-        [(misc, upper, [(2 * LANES, 2 * cols), (LANES, 2 * cols + 2 * LANES)])], [prior]
-    )
-    for bit in (1, 2):
-        g_state = sum_pairs(g_state, "tensor", bit)
-    prior = g_step
+        prior = gate.step(scal, [prior])
+    while val.order:
+        prior = val.step(scal, [prior])
+    prior = g_state.step([prior, Far(grad_x)])
+    g_state = g_state.value.reshape(layers, -1, 2 * LANES)
+    g_value, g_gate = finish_call([(val, upper, [(cols, 0)]), (gate, upper, [(cols, cols)])], [prior])
+    prior = Far(g_gate)
     while rest_small.came is not None:
         prior = rest_small.step([prior])
-    g_out, g_value, g_gate = finish_call(
-        [(out, g_outs[1].value, [(cols, 0)]), (val, upper, [(cols, 0)]), (gate, upper, [(cols, cols)])],
-        [prior],
-    )
     small, rest_small = small.value, rest_small.value
     small = small.reshape(layers, per_layer, GC)
     v_sum = jnp.swapaxes(small[:, : groups * 8].reshape(layers, groups, 8, GC), 1, 2)

time: 652 us -> 545 us (0.84)
  Pallas kernels: 396 us -> 320 us
  local copies, waits for them, and re-layouts: 46.4 us -> 21.9 us
  blocking collectives: 44.2 us -> 27.2 us
  waiting for transfers between devices: 72.6 us -> 80.4 us
    pallas_call x71 -> x74, Pallas kernels: 396 us -> 320 us  [run(): pl.pallas_call(functools.partial(kernel, len(self.tail) + len(after)), gr...]
    unnamed x203 -> x91, local copies, waits for them, and re-layouts: 38.1 us -> 16.1 us
    all_to_all x1, blocking collectives: 44.2 us -> 27.2 us  [per_device(): lax.all_to_all(x_dealt, 'dp', split_axis=0, concat_axis=0, tiled=True)]
    all_to_all x1, waiting for transfers between devices: 4.25 us -> 10.8 us  [per_device(): lax.all_to_all(grad_in, 'dp', split_axis=0, concat_axis=0, tiled=True)]
    ppermute x81 -> x86, starting transfers between devices: 51.6 us -> 56.2 us  [swap(): return lax.ppermute(value, axis, pairs(axis, bit))]
    ppermute x81 -> x86, waiting for transfers between devices: 68.3 us -> 67.5 us  [swap(): return lax.ppermute(value, axis, pairs(axis, bit))]
  transfers between devices with their start and end apart: 84 -> 89, of which waited for: 14 -> 17; matrix products, arithmetic and copies ran while one was open for 3% -> 2% of each run, Pallas kernels for 58% -> 58%
where the time goes in v3:
time: 545 us; the launch traced here: 536 us
  Pallas kernels  320 us (59%)
  waiting for transfers between devices  80.4 us (15%)
  starting transfers between devices  60.5 us (11%)
  blocking collectives  27.2 us (5%)
  local copies, waits for them, and re-layouts  21.9 us (4%)
  between operations  18.1 us (3%)
  other arithmetic  7.57 us (1%)
    pallas_call x74, Pallas kernels, run(): pl.pallas_call(functools.partial(kernel, len(self.tail) + len(after)), gr...  320 us
    ppermute x86, waiting for transfers between devices, swap(): return lax.ppermute(value, axis, pairs(axis, bit))  67.5 us
    ppermute x86, starting transfers between devices, swap(): return lax.ppermute(value, axis, pairs(axis, bit))  56.2 us
    all_to_all x1, blocking collectives, per_device(): lax.all_to_all(x_dealt, 'dp', split_axis=0, concat_axis=0, tiled=True)  27.2 us
    unnamed x91, local copies, waits for them, and re-layouts  16.1 us
  transfers between devices with their start and end apart: 89, of which 17 were waited for; matrix products, arithmetic and copies ran while one was open for 2% of the time, Pallas kernels for 58%

profile of v3, /device:TPU:0, one launch (start us, length us, event | category | flops | bytes accessed | tf_op | source)
XLA Modules:
  0.0 535.7 jit_solution(8059225518516391526)
XLA Ops:
  12.0 27.2 %all_to_all.10 = bf16[8,32,1536]{2,1,0:T(8,128)(2,1)S(1)} all-to-all(bf16[8,32,1536]{2,1,0:T(8,128)(2,1)S(1)} %broadcast_select_fusion), channel_id=1, replica_groups=mesh['dp'=8,'tensor'=4] {'dp'}, dimensions={0} | all-to-all | bytes 1572864 | tf_op jit(solution)/shard_map/all_to_all | solution.py:1180
  40.8 4.2 collective-permute-done.1.refs_2_
  53.7 11.5 %layer_forward.8 = (f32[1024,1536]{1,0:T(8,128)}, bf16[1024,1536]{1,0:T(8,128)(2,1)}, bf16[1024,768]{1,0:T(8,128)(2,1)}, bf16[256,768]{1,0:T(8,128)(2,1)}, bf16[...) custom-call(s32[6]{0:T(128)S(1)} %stack.39.refs_0_.place_ref, ...), custom_call_target="tpu_custom_call" | custom-call | flops 13200000000 | bytes 1000000 | tf_op jit(solution)/shard_map/layer_forward/pallas_call | solution.py:645
  69.2 11.5 %layer_forward.9 = (f32[1024,1536]{1,0:T(8,128)}, bf16[1024,1536]{1,0:T(8,128)(2,1)}, bf16[1024,768]{1,0:T(8,128)(2,1)}, bf16[256,768]{1,0:T(8,128)(2,1)}, bf16[...) custom-call(s32[6]{0:T(128)S(1)} %stack.39.refs_0_.place_ref, ...), custom_call_target="tpu_custom_call", output_to_operand_aliasing={{0}: (18, {}), {1}: (19, {}), {2}: (20, {})} | custom-call | flops 13200000000 | bytes 1000000 | tf_op jit(solution)/shard_map/layer_forward/pallas_call | solution.py:645
  83.2 11.5 %layer_forward.10 = (f32[1024,1536]{1,0:T(8,128)}, bf16[1024,1536]{1,0:T(8,128)(2,1)}, bf16[1024,768]{1,0:T(8,128)(2,1)}, bf16[256,768]{1,0:T(8,128)(2,1)}, bf16...) custom-call(s32[6]{0:T(128)S(1)} %stack.39.refs_0_.place_ref, ...), custom_call_target="tpu_custom_call", output_to_operand_aliasing={{0}: (18, {}), {1}: (19, {}), {2}: (20, {})} | custom-call | flops 13200000000 | bytes 1000000 | tf_op jit(solution)/shard_map/layer_forward/pallas_call | solution.py:645
  96.3 11.7 %layer_forward.11 = (f32[1024,1536]{1,0:T(8,128)}, bf16[1024,1536]{1,0:T(8,128)(2,1)}, bf16[1024,768]{1,0:T(8,128)(2,1)}, bf16[256,768]{1,0:T(8,128)(2,1)}, bf16...) custom-call(s32[6]{0:T(128)S(1)} %stack.39.refs_0_.place_ref, ...), custom_call_target="tpu_custom_call", output_to_operand_aliasing={{0}: (18, {}), {1}: (19, {}), {2}: (20, {})} | custom-call | flops 13200000000 | bytes 1000000 | tf_op jit(solution)/shard_map/layer_forward/pallas_call | solution.py:645
  110.6 12.2 %layer_forward.12 = (f32[1024,1536]{1,0:T(8,128)}, bf16[1024,1536]{1,0:T(8,128)(2,1)}, bf16[1024,768]{1,0:T(8,128)(2,1)}, bf16[256,1664]{1,0:T(8,128)(2,1)}, bf1...) custom-call(s32[6]{0:T(128)S(1)} %stack.39.refs_0_.place_ref, ...), custom_call_target="tpu_custom_call" | custom-call | flops 13200000000 | bytes 1000000 | tf_op jit(solution)/shard_map/layer_forward/pallas_call | solution.py:645
  124.5 11.8 %layer_forward.13 = (f32[1024,1536]{1,0:T(8,128)}, bf16[1024,1536]{1,0:T(8,128)(2,1)}, bf16[1024,768]{1,0:T(8,128)(2,1)}, bf16[256,1664]{1,0:T(8,128)(2,1)}, bf1...) custom-call(s32[6]{0:T(128)S(1)} %stack.39.refs_0_.place_ref, ...), custom_call_target="tpu_custom_call", output_to_operand_aliasing={{0}: (19, {}), {1}: (20, {}), {2}: (21, {})} | custom-call | flops 13200000000 | bytes 1000000 | tf_op jit(solution)/shard_map/layer_forward/pallas_call | solution.py:645
  138.9 12.0 %layer_forward.14 = (f32[1024,1536]{1,0:T(8,128)}, bf16[1024,1536]{1,0:T(8,128)(2,1)}, bf16[1024,768]{1,0:T(8,128)(2,1)}, bf16[256,1664]{1,0:T(8,128)(2,1)}, bf1...) custom-call(s32[6]{0:T(128)S(1)} %stack.39.refs_0_.place_ref, ...), custom_call_target="tpu_custom_call", output_to_operand_aliasing={{0}: (19, {}), {1}: (20, {}), {2}: (21, {})} | custom-call | flops 13200000000 | bytes 1000000 | tf_op jit(solution)/shard_map/layer_forward/pallas_call | solution.py:645
  152.9 12.0 %layer_forward.15 = (f32[1024,1536]{1,0:T(8,128)}, bf16[1024,1536]{1,0:T(8,128)(2,1)}, bf16[1024,768]{1,0:T(8,128)(2,1)}, bf16[256,1664]{1,0:T(8,128)(2,1)}, bf1...) custom-call(s32[6]{0:T(128)S(1)} %stack.39.refs_0_.place_ref, ...), custom_call_target="tpu_custom_call", output_to_operand_aliasing={{0}: (19, {}), {1}: (20, {}), {2}: (21, {})} | custom-call | flops 13200000000 | bytes 1000000 | tf_op jit(solution)/shard_map/layer_forward/pallas_call | solution.py:645
  167.2 4.5 norm_backward.8
  171.7 4.6 norm_backward.9
  178.2 10.7 %collective-permute-done.32.refs_4_ = bf16[128,1664]{1,0:T(8,128)(2,1)S(1)} collective-permute-done((bf16[128,1664]{1,0:T(8,128)(2,1)S(1)}, bf16[128,1664]{1,0:T(8,128)(2,1)S(1)}, u32[]{:S(2)}, u32[]{:S(2)}) %collective-permute-start.32) | collective-permute-done | bytes 426016 | tf_op jit(solution)/shard_map/ppermute | solution.py:956
  188.9 4.8 norm_backward.10
  193.8 4.6 norm_backward.11
  199.0 6.4 %weight_grad.6.refs_20_ = bf16[1536,768]{1,0:T(8,128)(2,1)} custom-call(s32[6]{0:T(128)S(1)} %stack.39.refs_0_.place_ref, bf16[1024,1536]{1,0:T(8,128)(2,1)} %get-tuple-element.415.refs_1_, bf16[1024,768]{1,0:T(8,128)(2,1)} %get-tuple-element.416.refs_2_), custom_call_target="tpu_custom_call" | custom-call | flops 6600000000 | bytes 1000000 | tf_op jit(solution)/shard_map/weight_grad/pallas_call | solution.py:645
  205.5 13.8 %layer_backward.8 = (bf16[1024,768]{1,0:T(8,128)(2,1)}, bf16[1024,768]{1,0:T(8,128)(2,1)}, bf16[1024,256]{1,0:T(8,128)(2,1)}, bf16[1024,128]{1,0:T(8,128)(2,1)},...) custom-call(s32[6]{0:T(128)S(1)} %stack.39.refs_0_.place_ref, ...), custom_call_target="tpu_custom_call" | custom-call | flops 17600000000 | bytes 1000000 | tf_op jit(solution)/shard_map/layer_backward/pallas_call | solution.py:645
  219.9 13.4 %layer_backward.9 = (bf16[1024,768]{1,0:T(8,128)(2,1)}, bf16[1024,768]{1,0:T(8,128)(2,1)}, bf16[1024,256]{1,0:T(8,128)(2,1)}, bf16[1024,128]{1,0:T(8,128)(2,1)},...) custom-call(s32[6]{0:T(128)S(1)} %stack.39.refs_0_.place_ref, ...), custom_call_target="tpu_custom_call", output_to_operand_aliasing={{0}: (24, {}), {1}: (25, {}), {2}: (26, {}), {3}: (27, {})} | custom-call | flops 17600000000 | bytes 1000000 | tf_op jit(solution)/shard_map/layer_backward/pallas_call | solution.py:645
  234.3 13.8 %layer_backward.10 = (bf16[1024,768]{1,0:T(8,128)(2,1)}, bf16[1024,768]{1,0:T(8,128)(2,1)}, bf16[1024,256]{1,0:T(8,128)(2,1)}, bf16[1024,128]{1,0:T(8,128)(2,1)}...) custom-call(s32[6]{0:T(128)S(1)} %stack.39.refs_0_.place_ref, ...), custom_call_target="tpu_custom_call", output_to_operand_aliasing={{0}: (24, {}), {1}: (25, {}), {2}: (26, {}), {3}: (27, {})} | custom-call | flops 17600000000 | bytes 1000000 | tf_op jit(solution)/shard_map/layer_backward/pallas_call | solution.py:645
  249.0 13.7 %layer_backward.11 = (bf16[1024,768]{1,0:T(8,128)(2,1)}, bf16[1024,768]{1,0:T(8,128)(2,1)}, bf16[1024,256]{1,0:T(8,128)(2,1)}, bf16[1024,128]{1,0:T(8,128)(2,1)}...) custom-call(s32[6]{0:T(128)S(1)} %stack.39.refs_0_.place_ref, ...), custom_call_target="tpu_custom_call", output_to_operand_aliasing={{0}: (24, {}), {1}: (25, {}), {2}: (26, {}), {3}: (27, {})} | custom-call | flops 17600000000 | bytes 1000000 | tf_op jit(solution)/shard_map/layer_backward/pallas_call | solution.py:645
  273.5 10.8 %weight_grad.7.refs_9_ = bf16[1536,1920]{1,0:T(8,128)(2,1)} custom-call(s32[6]{0:T(128)S(1)} %stack.39.refs_0_.place_ref, bf16[1024,1536]{1,0:T(8,128)(2,1)} %get-tuple-element.453.refs_1_, bf16[1024,768]{1,0:T(8,128)(2,1)} %get-tuple-element.454.refs_2_, bf16[1024,768]{1,0:T(8,128)(2,1)} %get-tuple-element.455.refs_3_, ...), custom_call_target="tpu_custom_call" | custom-call | flops 16499999744 | bytes 1000000 | tf_op jit(solution)/shard_map/weight_grad/pallas_call | solution.py:645
  286.4 4.3 norm_backward.12
  291.3 4.7 collective-permute-done.43.refs_4_
  296.0 4.1 norm_backward.13
  300.2 4.1 norm_backward.14
  304.3 4.2 norm_backward.15
  308.5 6.6 %weight_grad.8 = (bf16[768,768]{1,0:T(8,128)(2,1)}, bf16[768,768]{1,0:T(8,128)(2,1)}) custom-call(s32[6]{0:T(128)S(1)} %stack.39.refs_0_.place_ref, bf16[1024,1536]{1,0:T(8,128)(2,1)} %get-tuple-element.507.refs_1_, bf16[1024,768]{1,0:T(8,128)(2,1)} %get-tuple-element.508.refs_2_), custom_call_target="tpu_custom_call" | custom-call | flops 6600000000 | bytes 1000000 | tf_op jit(solution)/shard_map/weight_grad/pallas_call | solution.py:645
  315.7 13.4 %layer_backward.12 = (bf16[1024,768]{1,0:T(8,128)(2,1)}, bf16[1024,768]{1,0:T(8,128)(2,1)}, bf16[1024,256]{1,0:T(8,128)(2,1)}, bf16[1024,128]{1,0:T(8,128)(2,1)}...) custom-call(s32[6]{0:T(128)S(1)} %stack.39.refs_0_.place_ref, ...), custom_call_target="tpu_custom_call" | custom-call | flops 17600000000 | bytes 1000000 | tf_op jit(solution)/shard_map/layer_backward/pallas_call | solution.py:645
  329.3 13.6 %layer_backward.13 = (bf16[1024,768]{1,0:T(8,128)(2,1)}, bf16[1024,768]{1,0:T(8,128)(2,1)}, bf16[1024,256]{1,0:T(8,128)(2,1)}, bf16[1024,128]{1,0:T(8,128)(2,1)}...) custom-call(s32[6]{0:T(128)S(1)} %stack.39.refs_0_.place_ref, ...), custom_call_target="tpu_custom_call", output_to_operand_aliasing={{0}: (24, {}), {1}: (25, {}), {2}: (26, {}), {3}: (27, {})} | custom-call | flops 17600000000 | bytes 1000000 | tf_op jit(solution)/shard_map/layer_backward/pallas_call | solution.py:645
  345.5 13.3 %layer_backward.14 = (bf16[1024,768]{1,0:T(8,128)(2,1)}, bf16[1024,768]{1,0:T(8,128)(2,1)}, bf16[1024,256]{1,0:T(8,128)(2,1)}, bf16[1024,128]{1,0:T(8,128)(2,1)}...) custom-call(s32[6]{0:T(128)S(1)} %stack.39.refs_0_.place_ref, ...), custom_call_target="tpu_custom_call", output_to_operand_aliasing={{0}: (24, {}), {1}: (25, {}), {2}: (26, {}), {3}: (27, {})} | custom-call | flops 17600000000 | bytes 1000000 | tf_op jit(solution)/shard_map/layer_backward/pallas_call | solution.py:645
  363.4 2.5 add_scatter.8
  367.6 13.7 %layer_backward.15 = (bf16[1024,768]{1,0:T(8,128)(2,1)}, bf16[1024,768]{1,0:T(8,128)(2,1)}, bf16[1024,256]{1,0:T(8,128)(2,1)}, bf16[1024,128]{1,0:T(8,128)(2,1)}...) custom-call(s32[6]{0:T(128)S(1)} %stack.39.refs_0_.place_ref, ...), custom_call_target="tpu_custom_call", output_to_operand_aliasing={{0}: (24, {}), {1}: (25, {}), {2}: (26, {}), {3}: (27, {})} | custom-call | flops 17600000000 | bytes 1000000 | tf_op jit(solution)/shard_map/layer_backward/pallas_call | solution.py:645
  387.9 2.5 collective-permute-done.63.y
  390.9 6.5 %weight_grad.9 = (bf16[768,768]{1,0:T(8,128)(2,1)}, bf16[768,768]{1,0:T(8,128)(2,1)}) custom-call(s32[6]{0:T(128)S(1)} %stack.39.refs_0_.place_ref, bf16[1024,1536]{1,0:T(8,128)(2,1)} %get-tuple-element.563.refs_1_, bf16[1024,768]{1,0:T(8,128)(2,1)} %get-tuple-element.564.refs_2_, f32[80,256]{1,0:T(8,128)S(1)} %sum_small.10.refs_3_.x), custom_call_target="tpu_custom_call" | custom-call | flops 6600000000 | bytes 1000000 | tf_op jit(solution)/shard_map/weight_grad/pallas_call | solution.py:645
  404.6 4.3 all-to-all-start.1
  409.0 4.6 weight_grad.10
  416.3 6.0 %weight_grad.11 = (bf16[768,768]{1,0:T(8,128)(2,1)}, bf16[768,768]{1,0:T(8,128)(2,1)}) custom-call(s32[6]{0:T(128)S(1)} %stack.39.refs_0_.place_ref, bf16[1024,1536]{1,0:T(8,128)(2,1)} %get-tuple-element.563.refs_1_, bf16[1024,768]{1,0:T(8,128)(2,1)} %get-tuple-element.569.refs_2_, f32[80,256]{1,0:T(8,128)S(1)} %sum_small.13.refs_3_), custom_call_target="tpu_custom_call" | custom-call | flops 6600000000 | bytes 1000000 | tf_op jit(solution)/shard_map/weight_grad/pallas_call | solution.py:645
  422.4 10.8 %all-to-all-done.1.src = bf16[8,32,1536]{2,1,0:T(8,128)(2,1)S(1)} async-done(((bf16[8,32,1536]{2,1,0:T(8,128)(2,1)}), bf16[8,32,1536]{2,1,0:T(8,128)(2,1)S(1)}, u32[]{:S(2)}, u32[]{:S(2)}) %all-to-all-start.1) | async-done | bytes 786464 | tf_op jit(solution)/shard_map/all_to_all | solution.py:1343
  433.8 2.7 collective-permute-done.72.b
  442.8 2.5 collective-permute-start.79
  455.7 15.5 %collective-permute-done.77.b = bf16[768,768]{1,0:T(8,128)(2,1)} collective-permute-done((bf16[768,768]{1,0:T(8,128)(2,1)}, bf16[768,768]{1,0:T(8,128)(2,1)}, u32[]{:S(2)}, u32[]{:S(2)}) %collective-permute-start.77) | collective-permute-done | bytes 1179680 | tf_op jit(solution)/shard_map/ppermute | solution.py:956
  474.6 4.9 collective-permute-done.76.refs_5_
  487.8 3.3 collective-permute-start.81
  494.9 3.8 maximum_select_fusion.refs_1_
  498.6 3.8 collective-permute-start.80
  503.2 8.5 %collective-permute-done.81.refs_1_ = bf16[192,768]{1,0:T(8,128)(2,1)S(1)} collective-permute-done((bf16[192,768]{1,0:T(8,128)(2,1)}, bf16[192,768]{1,0:T(8,128)(2,1)S(1)}, u32[]{:S(2)}, u32[]{:S(2)}) %collective-permute-start.81) | collective-permute-done | bytes 294944 | tf_op jit(solution)/shard_map/ppermute | solution.py:956
  511.7 5.9 %collective-permute-done.83.refs_4_ = bf16[192,768]{1,0:T(8,128)(2,1)S(1)} collective-permute-done((bf16[192,768]{1,0:T(8,128)(2,1)}, bf16[192,768]{1,0:T(8,128)(2,1)S(1)}, u32[]{:S(2)}, u32[]{:S(2)}) %collective-permute-start.83) | collective-permute-done | bytes 294944 | tf_op jit(solution)/shard_map/ppermute | solution.py:956
  519.3 2.9 finish.3
  (322 shorter events, 118.0 us)
Async XLA Ops:
  7.2 266.3 %reduce-scatter.3.cloned.1.call-start = ((), (), s32[]{:S(2)}) async-start(), calls=%async_computation.4 | async-start | bytes 2654208 | tf_op jit(solution)/shard_map/reduce_scatter | solution.py:1118
  50.6 15.8 %collective-permute-start = (bf16[192,1536]{1,0:T(8,128)(2,1)S(1)}, bf16[192,1536]{1,0:T(8,128)(2,1)S(1)}, u32[]{:S(2)}, u32[]{:S(2)}) collective-permute-start(bf16[192,1536]{1,0:T(8,128)(2,1)S(1)} %bitcast.54), channel_id=1, source_target_pairs={{0,2},{1,3},{2,0},{3,1},{4,6},{5,7},{6,4},{7,5},{8,10},{9,11},{10,... | collective-permute-start | bytes 1769480 | tf_op jit(solution)/shard_map/ppermute | solution.py:956
  81.1 14.9 %collective-permute-start.8 = (bf16[128,1664]{1,0:T(8,128)(2,1)S(1)}, bf16[128,1664]{1,0:T(8,128)(2,1)S(1)}, u32[]{:S(2)}, u32[]{:S(2)}) collective-permute-start(bf16[128,1664]{1,0:T(8,128)(2,1)S(1)} %add_pair.12.refs_21_.refs_2_), channel_id=1, source_target_pairs={{0,2},{1,3},{2,0},{3,1},{4,6},{5,7},{6,4},{7,5},{8,10},{9,11},{10,... | collective-permute-start | bytes 1277960 | tf_op jit(solution)/shard_map/ppermute | solution.py:956
  82.7 27.3 %collective-permute-start.10 = (bf16[128,1664]{1,0:T(8,128)(2,1)S(1)}, bf16[128,1664]{1,0:T(8,128)(2,1)S(1)}, u32[]{:S(2)}, u32[]{:S(2)}) collective-permute-start(bf16[128,1664]{1,0:T(8,128)(2,1)S(1)} %add_pair.12.refs_21_.refs_2_), channel_id=1, source_target_pairs={{0,1},{1,0},{2,3},{3,2},{4,5},{5,4},{6,7},{7,6},{8,9},{9,8},{10,11... | collective-permute-start | bytes 1277960 | tf_op jit(solution)/shard_map/ppermute | solution.py:956
  95.2 14.8 %collective-permute-start.13 = (bf16[128,1664]{1,0:T(8,128)(2,1)S(1)}, bf16[128,1664]{1,0:T(8,128)(2,1)S(1)}, u32[]{:S(2)}, u32[]{:S(2)}) collective-permute-start(bf16[128,1664]{1,0:T(8,128)(2,1)S(1)} %add_pair.13.refs_21_.refs_2_), channel_id=1, source_target_pairs={{0,2},{1,3},{2,0},{3,1},{4,6},{5,7},{6,4},{7,5},{8,10},{9,11},{10,... | collective-permute-start | bytes 1277960 | tf_op jit(solution)/shard_map/ppermute | solution.py:956
  95.8 28.2 %collective-permute-start.20 = (bf16[128,1664]{1,0:T(8,128)(2,1)S(1)}, bf16[128,1664]{1,0:T(8,128)(2,1)S(1)}, u32[]{:S(2)}, u32[]{:S(2)}) collective-permute-start(bf16[128,1664]{1,0:T(8,128)(2,1)S(1)} %add_pair.13.refs_21_.refs_2_), channel_id=1, source_target_pairs={{0,1},{1,0},{2,3},{3,2},{4,5},{5,4},{6,7},{7,6},{8,9},{9,8},{10,11... | collective-permute-start | bytes 1277960 | tf_op jit(solution)/shard_map/ppermute | solution.py:956
  108.5 15.4 %collective-permute-start.17 = (bf16[128,1664]{1,0:T(8,128)(2,1)S(1)}, bf16[128,1664]{1,0:T(8,128)(2,1)S(1)}, u32[]{:S(2)}, u32[]{:S(2)}) collective-permute-start(bf16[128,1664]{1,0:T(8,128)(2,1)S(1)} %add_pair.14.refs_16_.refs_2_), channel_id=1, source_target_pairs={{0,2},{1,3},{2,0},{3,1},{4,6},{5,7},{6,4},{7,5},{8,10},{9,11},{10,... | collective-permute-start | bytes 1277960 | tf_op jit(solution)/shard_map/ppermute | solution.py:956
  110.0 28.3 %collective-permute-start.18 = (bf16[128,1664]{1,0:T(8,128)(2,1)S(1)}, bf16[128,1664]{1,0:T(8,128)(2,1)S(1)}, u32[]{:S(2)}, u32[]{:S(2)}) collective-permute-start(bf16[128,1664]{1,0:T(8,128)(2,1)S(1)} %add_pair.14.refs_16_.refs_2_), channel_id=1, source_target_pairs={{0,1},{1,0},{2,3},{3,2},{4,5},{5,4},{6,7},{7,6},{8,9},{9,8},{10,11... | collective-permute-start | bytes 1277960 | tf_op jit(solution)/shard_map/ppermute | solution.py:956
  123.3 15.1 %collective-permute-start.14 = (bf16[128,1664]{1,0:T(8,128)(2,1)S(1)}, bf16[128,1664]{1,0:T(8,128)(2,1)S(1)}, u32[]{:S(2)}, u32[]{:S(2)}) collective-permute-start(bf16[128,1664]{1,0:T(8,128)(2,1)S(1)} %add_pair.15.refs_22_.refs_2_), channel_id=1, source_target_pairs={{0,2},{1,3},{2,0},{3,1},{4,6},{5,7},{6,4},{7,5},{8,10},{9,11},{10,... | collective-permute-start | bytes 1277960 | tf_op jit(solution)/shard_map/ppermute | solution.py:956
  123.9 28.0 %collective-permute-start.15 = (bf16[128,1664]{1,0:T(8,128)(2,1)S(1)}, bf16[128,1664]{1,0:T(8,128)(2,1)S(1)}, u32[]{:S(2)}, u32[]{:S(2)}) collective-permute-start(bf16[128,1664]{1,0:T(8,128)(2,1)S(1)} %add_pair.15.refs_22_.refs_2_), channel_id=1, source_target_pairs={{0,1},{1,0},{2,3},{3,2},{4,5},{5,4},{6,7},{7,6},{8,9},{9,8},{10,11... | collective-permute-start | bytes 1277960 | tf_op jit(solution)/shard_map/ppermute | solution.py:956
  136.8 15.7 %collective-permute-start.24 = (bf16[128,1664]{1,0:T(8,128)(2,1)S(1)}, bf16[128,1664]{1,0:T(8,128)(2,1)S(1)}, u32[]{:S(2)}, u32[]{:S(2)}) collective-permute-start(bf16[128,1664]{1,0:T(8,128)(2,1)S(1)} %add_pair.16.refs_22_.refs_3_), channel_id=1, source_target_pairs={{0,2},{1,3},{2,0},{3,1},{4,6},{5,7},{6,4},{7,5},{8,10},{9,11},{10,... | collective-permute-start | bytes 1277960 | tf_op jit(solution)/shard_map/ppermute | solution.py:956
  138.3 27.2 %collective-permute-start.29 = (bf16[128,1664]{1,0:T(8,128)(2,1)S(1)}, bf16[128,1664]{1,0:T(8,128)(2,1)S(1)}, u32[]{:S(2)}, u32[]{:S(2)}) collective-permute-start(bf16[128,1664]{1,0:T(8,128)(2,1)S(1)} %add_pair.16.refs_22_.refs_3_), channel_id=1, source_target_pairs={{0,1},{1,0},{2,3},{3,2},{4,5},{5,4},{6,7},{7,6},{8,9},{9,8},{10,11... | collective-permute-start | bytes 1277960 | tf_op jit(solution)/shard_map/ppermute | solution.py:956
  151.8 15.2 %collective-permute-start.26 = (bf16[128,1664]{1,0:T(8,128)(2,1)S(1)}, bf16[128,1664]{1,0:T(8,128)(2,1)S(1)}, u32[]{:S(2)}, u32[]{:S(2)}) collective-permute-start(bf16[128,1664]{1,0:T(8,128)(2,1)S(1)} %add_pair.17.refs_22_.refs_3_), channel_id=1, source_target_pairs={{0,2},{1,3},{2,0},{3,1},{4,6},{5,7},{6,4},{7,5},{8,10},{9,11},{10,... | collective-permute-start | bytes 1277960 | tf_op jit(solution)/shard_map/ppermute | solution.py:956
  152.4 19.3 %collective-permute-start.27 = (bf16[128,1664]{1,0:T(8,128)(2,1)S(1)}, bf16[128,1664]{1,0:T(8,128)(2,1)S(1)}, u32[]{:S(2)}, u32[]{:S(2)}) collective-permute-start(bf16[128,1664]{1,0:T(8,128)(2,1)S(1)} %add_pair.17.refs_22_.refs_3_), channel_id=1, source_target_pairs={{0,1},{1,0},{2,3},{3,2},{4,5},{5,4},{6,7},{7,6},{8,9},{9,8},{10,11... | collective-permute-start | bytes 1277960 | tf_op jit(solution)/shard_map/ppermute | solution.py:956
  177.9 15.9 %collective-permute-start.33 = (bf16[128,1664]{1,0:T(8,128)(2,1)S(1)}, bf16[128,1664]{1,0:T(8,128)(2,1)S(1)}, u32[]{:S(2)}, u32[]{:S(2)}) collective-permute-start(bf16[128,1664]{1,0:T(8,128)(2,1)S(1)} %add_pair.19.refs_14_.refs_3_), channel_id=1, source_target_pairs={{0,1},{1,0},{2,3},{3,2},{4,5},{5,4},{6,7},{7,6},{8,9},{9,8},{10,11... | collective-permute-start | bytes 1277960 | tf_op jit(solution)/shard_map/ppermute | solution.py:956
  205.5 275.6 %reduce-scatter.5.cloned.1.call-start = ((), (), s32[]{:S(2)}) async-start(), calls=%async_computation.5 | async-start | bytes 6635520 | tf_op jit(solution)/shard_map/reduce_scatter | solution.py:1118
  233.4 15.0 %collective-permute-start.39 = (bf16[128,1536]{1,0:T(8,128)(2,1)S(1)}, bf16[128,1536]{1,0:T(8,128)(2,1)S(1)}, u32[]{:S(2)}, u32[]{:S(2)}) collective-permute-start(bf16[128,1536]{1,0:T(8,128)(2,1)S(1)} %get-tuple-element.444), channel_id=1, source_target_pairs={{0,1},{1,0},{2,3},{3,2},{4,5},{5,4},{6,7},{7,6},{8,9},{9,8},{10,11... | collective-permute-start | bytes 1179656 | tf_op jit(solution)/shard_map/ppermute | solution.py:956
  233.7 15.3 %collective-permute-start.40 = (bf16[128,1536]{1,0:T(8,128)(2,1)S(1)}, bf16[128,1536]{1,0:T(8,128)(2,1)S(1)}, u32[]{:S(2)}, u32[]{:S(2)}) collective-permute-start(bf16[128,1536]{1,0:T(8,128)(2,1)S(1)} %add_pair.20.refs_28_.refs_3_), channel_id=1, source_target_pairs={{0,2},{1,3},{2,0},{3,1},{4,6},{5,7},{6,4},{7,5},{8,10},{9,11},{10,... | collective-permute-start | bytes 1179656 | tf_op jit(solution)/shard_map/ppermute | solution.py:956
  248.1 18.8 %collective-permute-start.42 = (bf16[128,1536]{1,0:T(8,128)(2,1)S(1)}, bf16[128,1536]{1,0:T(8,128)(2,1)S(1)}, u32[]{:S(2)}, u32[]{:S(2)}) collective-permute-start(bf16[128,1536]{1,0:T(8,128)(2,1)S(1)} %get-tuple-element.448), channel_id=1, source_target_pairs={{0,1},{1,0},{2,3},{3,2},{4,5},{5,4},{6,7},{7,6},{8,9},{9,8},{10,11... | collective-permute-start | bytes 1179656 | tf_op jit(solution)/shard_map/ppermute | solution.py:956
  265.0 19.3 %collective-permute-start.52 = (bf16[128,1536]{1,0:T(8,128)(2,1)S(1)}, bf16[128,1536]{1,0:T(8,128)(2,1)}, u32[]{:S(2)}, u32[]{:S(2)}) collective-permute-start(bf16[128,1536]{1,0:T(8,128)(2,1)S(1)} %add_pair.20.refs_28_.refs_3_), channel_id=1, source_target_pairs={{0,1},{1,0},{2,3},{3,2},{4,5},{5,4},{6,7},{7,6},{8,9},{9,8},{10,11... | collective-permute-start | bytes 1179656 | tf_op jit(solution)/shard_map/ppermute | solution.py:956
  265.5 18.9 %collective-permute-start.49 = (bf16[128,1536]{1,0:T(8,128)(2,1)S(1)}, bf16[128,1536]{1,0:T(8,128)(2,1)S(1)}, u32[]{:S(2)}, u32[]{:S(2)}) collective-permute-start(bf16[128,1536]{1,0:T(8,128)(2,1)S(1)} %add_pair.21.refs_28_.refs_3_), channel_id=1, source_target_pairs={{0,2},{1,3},{2,0},{3,1},{4,6},{5,7},{6,4},{7,5},{8,10},{9,11},{10,... | collective-permute-start | bytes 1179656 | tf_op jit(solution)/shard_map/ppermute | solution.py:956
  267.0 23.8 %collective-permute-start.50 = (bf16[128,1536]{1,0:T(8,128)(2,1)S(1)}, bf16[128,1536]{1,0:T(8,128)(2,1)S(1)}, u32[]{:S(2)}, u32[]{:S(2)}) collective-permute-start(bf16[128,1536]{1,0:T(8,128)(2,1)S(1)} %add_pair.21.refs_28_.refs_3_), channel_id=1, source_target_pairs={{0,1},{1,0},{2,3},{3,2},{4,5},{5,4},{6,7},{7,6},{8,9},{9,8},{10,11... | collective-permute-start | bytes 1179656 | tf_op jit(solution)/shard_map/ppermute | solution.py:956
  269.4 21.5 %collective-permute-start.46 = (bf16[128,1536]{1,0:T(8,128)(2,1)S(1)}, bf16[128,1536]{1,0:T(8,128)(2,1)S(1)}, u32[]{:S(2)}, u32[]{:S(2)}) collective-permute-start(bf16[128,1536]{1,0:T(8,128)(2,1)S(1)} %add_pair.22.refs_0_.refs_3_), channel_id=1, source_target_pairs={{0,2},{1,3},{2,0},{3,1},{4,6},{5,7},{6,4},{7,5},{8,10},{9,11},{10,... | collective-permute-start | bytes 1179656 | tf_op jit(solution)/shard_map/ppermute | solution.py:956
  270.0 14.9 %collective-permute-start.53 = (bf16[128,1536]{1,0:T(8,128)(2,1)S(1)}, bf16[128,1536]{1,0:T(8,128)(2,1)}, u32[]{:S(2)}, u32[]{:S(2)}) collective-permute-start(bf16[128,1536]{1,0:T(8,128)(2,1)S(1)} %collective-permute-done.40.refs_29_.refs_4_), channel_id=1, source_target_pairs={{0,1},{1,0},{2,3},{3,2},{4,5},{5,4},{6,7},{7,6},{8,9},{9,8},{10,11... | collective-permute-start | bytes 1179656 | tf_op jit(solution)/shard_map/ppermute | solution.py:956
  284.4 15.8 %collective-permute-start.47 = (bf16[128,1536]{1,0:T(8,128)(2,1)S(1)}, bf16[128,1536]{1,0:T(8,128)(2,1)S(1)}, u32[]{:S(2)}, u32[]{:S(2)}) collective-permute-start(bf16[128,1536]{1,0:T(8,128)(2,1)S(1)} %add_pair.22.refs_0_.refs_3_), channel_id=1, source_target_pairs={{0,1},{1,0},{2,3},{3,2},{4,5},{5,4},{6,7},{7,6},{8,9},{9,8},{10,11... | collective-permute-start | bytes 1179656 | tf_op jit(solution)/shard_map/ppermute | solution.py:956
  315.1 47.3 %collective-permute-start.56 = (bf16[768,768]{1,0:T(8,128)(2,1)}, bf16[768,768]{1,0:T(8,128)(2,1)S(1)}, u32[]{:S(2)}, u32[]{:S(2)}) collective-permute-start(bf16[768,768]{1,0:T(8,128)(2,1)} %get-tuple-element.509.refs_20_), channel_id=1, source_target_pairs={{0,4},{4,0},{8,12},{12,8},{16,20},{20,16},{24,28},{28,24},{1,5},{5... | collective-permute-start | bytes 3538952 | tf_op jit(solution)/shard_map/ppermute | solution.py:956
  342.9 16.0 %collective-permute-start.55 = (bf16[128,1536]{1,0:T(8,128)(2,1)S(1)}, bf16[128,1536]{1,0:T(8,128)(2,1)S(1)}, u32[]{:S(2)}, u32[]{:S(2)}) collective-permute-start(bf16[128,1536]{1,0:T(8,128)(2,1)S(1)} %get-tuple-element.538), channel_id=1, source_target_pairs={{0,1},{1,0},{2,3},{3,2},{4,5},{5,4},{6,7},{7,6},{8,9},{9,8},{10,11... | collective-permute-start | bytes 1179656 | tf_op jit(solution)/shard_map/ppermute | solution.py:956
  344.0 16.2 %collective-permute-start.57 = (bf16[64,1536]{1,0:T(8,128)(2,1)S(1)}, bf16[64,1536]{1,0:T(8,128)(2,1)S(1)}, u32[]{:S(2)}, u32[]{:S(2)}) collective-permute-start(bf16[64,1536]{1,0:T(8,128)(2,1)S(1)} %get-tuple-element.529.refs_28_), channel_id=1, source_target_pairs={{0,2},{1,3},{2,0},{3,1},{4,6},{5,7},{6,4},{7,5},{8,10},{9,11},{10,... | collective-permute-start | bytes 589832 | tf_op jit(solution)/shard_map/ppermute | solution.py:956
  358.8 22.5 %collective-permute-start.60 = (bf16[128,1536]{1,0:T(8,128)(2,1)S(1)}, bf16[128,1536]{1,0:T(8,128)(2,1)S(1)}, u32[]{:S(2)}, u32[]{:S(2)}) collective-permute-start(bf16[128,1536]{1,0:T(8,128)(2,1)S(1)} %get-tuple-element.556), channel_id=1, source_target_pairs={{0,1},{1,0},{2,3},{3,2},{4,5},{5,4},{6,7},{7,6},{8,9},{9,8},{10,11... | collective-permute-start | bytes 1179656 | tf_op jit(solution)/shard_map/ppermute | solution.py:956
  359.6 24.0 %collective-permute-start.59 = (bf16[64,1536]{1,0:T(8,128)(2,1)S(1)}, bf16[64,1536]{1,0:T(8,128)(2,1)S(1)}, u32[]{:S(2)}, u32[]{:S(2)}) collective-permute-start(bf16[64,1536]{1,0:T(8,128)(2,1)S(1)} %get-tuple-element.540.refs_0_.refs_28_), channel_id=1, source_target_pairs={{0,2},{1,3},{2,0},{3,1},{4,6},{5,7},{6,4},{7,5},{8,10},{9,11},{10,... | collective-permute-start | bytes 589832 | tf_op jit(solution)/shard_map/ppermute | solution.py:956
  365.9 76.9 %collective-permute-start.70 = (bf16[384,768]{1,0:T(8,128)(2,1)}, bf16[384,768]{1,0:T(8,128)(2,1)}, u32[]{:S(2)}, u32[]{:S(2)}) collective-permute-start(bf16[384,768]{1,0:T(8,128)(2,1)} %get-tuple-element.542.refs_29_), channel_id=1, source_target_pairs={{0,8},{4,12},{8,0},{12,4},{16,24},{20,28},{24,16},{28,20},{1,9},{5... | collective-permute-start | bytes 1769480 | tf_op jit(solution)/shard_map/ppermute | solution.py:956
  382.0 16.7 %collective-permute-start.62 = (bf16[64,1536]{1,0:T(8,128)(2,1)S(1)}, bf16[64,1536]{1,0:T(8,128)(2,1)S(1)}, u32[]{:S(2)}, u32[]{:S(2)}) collective-permute-start(bf16[64,1536]{1,0:T(8,128)(2,1)S(1)} %get-tuple-element.557.refs_2_), channel_id=1, source_target_pairs={{0,2},{1,3},{2,0},{3,1},{4,6},{5,7},{6,4},{7,5},{8,10},{9,11},{10,... | collective-permute-start | bytes 589832 | tf_op jit(solution)/shard_map/ppermute | solution.py:956
  387.2 15.2 %collective-permute-start.61 = (bf16[64,1536]{1,0:T(8,128)(2,1)S(1)}, bf16[64,1536]{1,0:T(8,128)(2,1)S(1)}, u32[]{:S(2)}, u32[]{:S(2)}) collective-permute-start(bf16[64,1536]{1,0:T(8,128)(2,1)S(1)} %get-tuple-element.560.refs_0_), channel_id=1, source_target_pairs={{0,2},{1,3},{2,0},{3,1},{4,6},{5,7},{6,4},{7,5},{8,10},{9,11},{10,... | collective-permute-start | bytes 589832 | tf_op jit(solution)/shard_map/ppermute | solution.py:956
  397.5 41.5 %collective-permute-start.71 = (bf16[768,768]{1,0:T(8,128)(2,1)}, bf16[768,768]{1,0:T(8,128)(2,1)}, u32[]{:S(2)}, u32[]{:S(2)}) collective-permute-start(bf16[768,768]{1,0:T(8,128)(2,1)} %get-tuple-element.565.refs_2_), channel_id=1, source_target_pairs={{0,4},{4,0},{8,12},{12,8},{16,20},{20,16},{24,28},{28,24},{1,5},{5... | collective-permute-start | bytes 3538952 | tf_op jit(solution)/shard_map/ppermute | solution.py:956
  401.0 15.4 %collective-permute-start.65 = (f32[80,256]{1,0:T(8,128)S(1)}, f32[80,256]{1,0:T(8,128)S(1)}, u32[]{:S(2)}, u32[]{:S(2)}) collective-permute-start(f32[80,256]{1,0:T(8,128)S(1)} %sum_small.11.refs_2_.x), channel_id=1, source_target_pairs={{0,16},{4,20},{8,24},{12,28},{16,0},{20,4},{24,8},{28,12},{1,17},{... | collective-permute-start | bytes 245768 | tf_op jit(solution)/shard_map/ppermute | solution.py:956
  404.6 28.6 %all-to-all-start.1 = ((bf16[8,32,1536]{2,1,0:T(8,128)(2,1)}), bf16[8,32,1536]{2,1,0:T(8,128)(2,1)S(1)}, u32[]{:S(2)}, u32[]{:S(2)}) async-start(bf16[8,32,1536]{2,1,0:T(8,128)(2,1)} %bitcast.53), calls=%async_computation.2 | async-start | bytes 1572864 | tf_op jit(solution)/shard_map/all_to_all | solution.py:1343
  413.6 22.8 %collective-permute-start.72 = (bf16[768,384]{1,0:T(8,128)(2,1)}, bf16[768,384]{1,0:T(8,128)(2,1)}, u32[]{:S(2)}, u32[]{:S(2)}) collective-permute-start(bf16[768,384]{1,0:T(8,128)(2,1)} %get-tuple-element.575.refs_0_), channel_id=1, source_target_pairs={{0,8},{4,12},{8,0},{12,4},{16,24},{20,28},{24,16},{28,20},{1,9},{5... | collective-permute-start | bytes 1769480 | tf_op jit(solution)/shard_map/ppermute | solution.py:956
  415.7 31.9 %collective-permute-start.69 = (f32[24,256]{1,0:T(8,128)S(1)}, f32[24,256]{1,0:T(8,128)S(1)}, u32[]{:S(2)}, u32[]{:S(2)}) collective-permute-start(f32[24,256]{1,0:T(8,128)S(1)} %sum_small.12.refs_0_.x), channel_id=1, source_target_pairs={{0,2},{1,3},{2,0},{3,1},{4,6},{5,7},{6,4},{7,5},{8,10},{9,11},{10,... | collective-permute-start | bytes 73736 | tf_op jit(solution)/shard_map/ppermute | solution.py:956
  422.3 48.9 %collective-permute-start.77 = (bf16[768,768]{1,0:T(8,128)(2,1)}, bf16[768,768]{1,0:T(8,128)(2,1)}, u32[]{:S(2)}, u32[]{:S(2)}) collective-permute-start(bf16[768,768]{1,0:T(8,128)(2,1)} %get-tuple-element.576.refs_0_), channel_id=1, source_target_pairs={{0,8},{4,12},{8,0},{12,4},{16,24},{20,28},{24,16},{28,20},{1,9},{5... | collective-permute-start | bytes 3538952 | tf_op jit(solution)/shard_map/ppermute | solution.py:956
  436.5 18.5 %collective-permute-start.67 = (bf16[8,32,1536]{2,1,0:T(8,128)(2,1)S(1)}, bf16[8,32,1536]{2,1,0:T(8,128)(2,1)S(1)}, u32[]{:S(2)}, u32[]{:S(2)}) collective-permute-start(bf16[8,32,1536]{2,1,0:T(8,128)(2,1)S(1)} %take_parts.1.refs_0_), channel_id=1, source_target_pairs={{0,2},{1,3},{2,0},{3,1},{4,6},{5,7},{6,4},{7,5},{8,10},{9,11},{10,... | collective-permute-start | bytes 2359304 | tf_op jit(solution)/shard_map/ppermute | solution.py:956
  442.8 42.8 %collective-permute-start.79 = (bf16[384,768]{1,0:T(8,128)(2,1)}, bf16[384,768]{1,0:T(8,128)(2,1)}, u32[]{:S(2)}, u32[]{:S(2)}) collective-permute-start(bf16[384,768]{1,0:T(8,128)(2,1)} %get-tuple-element.581.refs_0_), channel_id=1, source_target_pairs={{0,8},{4,12},{8,0},{12,4},{16,24},{20,28},{24,16},{28,20},{1,9},{5... | collective-permute-start | bytes 1769480 | tf_op jit(solution)/shard_map/ppermute | solution.py:956
  447.5 31.9 %collective-permute-start.76 = (bf16[192,768]{1,0:T(8,128)(2,1)}, bf16[192,768]{1,0:T(8,128)(2,1)S(1)}, u32[]{:S(2)}, u32[]{:S(2)}) collective-permute-start(bf16[192,768]{1,0:T(8,128)(2,1)} %get-tuple-element.582.refs_0_), channel_id=1, source_target_pairs={{0,16},{4,20},{8,24},{12,28},{16,0},{20,4},{24,8},{28,12},{1,17},{... | collective-permute-start | bytes 884744 | tf_op jit(solution)/shard_map/ppermute | solution.py:956
  452.0 29.1 %collective-permute-start.75 = (bf16[192,384]{1,0:T(8,128)(2,1)}, bf16[192,384]{1,0:T(8,128)(2,1)S(1)}, u32[]{:S(2)}, u32[]{:S(2)}) collective-permute-start(bf16[192,384]{1,0:T(8,128)(2,1)} %get-tuple-element.585.refs_0_), channel_id=1, source_target_pairs={{0,16},{4,20},{8,24},{12,28},{16,0},{20,4},{24,8},{28,12},{1,17},{... | collective-permute-start | bytes 442376 | tf_op jit(solution)/shard_map/ppermute | solution.py:956
  455.6 39.2 %collective-permute-start.68 = (bf16[8,64,1536]{2,1,0:T(8,128)(2,1)S(1)}, bf16[8,64,1536]{2,1,0:T(8,128)(2,1)}, u32[]{:S(2)}, u32[]{:S(2)}) collective-permute-start(bf16[8,64,1536]{2,1,0:T(8,128)(2,1)S(1)} %maximum_select_fusion.1.refs_1_), channel_id=1, source_target_pairs={{0,1},{1,0},{2,3},{3,2},{4,5},{5,4},{6,7},{7,6},{8,9},{9,8},{10,11... | collective-permute-start | bytes 4718600 | tf_op jit(solution)/shard_map/ppermute | solution.py:956
  473.7 18.2 %collective-permute-start.82 = (bf16[384,768]{1,0:T(8,128)(2,1)}, bf16[384,768]{1,0:T(8,128)(2,1)S(1)}, u32[]{:S(2)}, u32[]{:S(2)}) collective-permute-start(bf16[384,768]{1,0:T(8,128)(2,1)} %get-tuple-element.588.refs_7_), channel_id=1, source_target_pairs={{0,4},{4,0},{8,12},{12,8},{16,20},{20,16},{24,28},{28,24},{1,5},{5... | collective-permute-start | bytes 1769480 | tf_op jit(solution)/shard_map/ppermute | solution.py:956
  487.8 23.9 %collective-permute-start.81 = (bf16[192,768]{1,0:T(8,128)(2,1)}, bf16[192,768]{1,0:T(8,128)(2,1)S(1)}, u32[]{:S(2)}, u32[]{:S(2)}) collective-permute-start(bf16[192,768]{1,0:T(8,128)(2,1)} %get-tuple-element.592.refs_0_), channel_id=1, source_target_pairs={{0,16},{4,20},{8,24},{12,28},{16,0},{20,4},{24,8},{28,12},{1,17},{... | collective-permute-start | bytes 884744 | tf_op jit(solution)/shard_map/ppermute | solution.py:956
  494.9 22.7 %collective-permute-start.83 = (bf16[192,768]{1,0:T(8,128)(2,1)}, bf16[192,768]{1,0:T(8,128)(2,1)S(1)}, u32[]{:S(2)}, u32[]{:S(2)}) collective-permute-start(bf16[192,768]{1,0:T(8,128)(2,1)} %get-tuple-element.596.refs_0_), channel_id=1, source_target_pairs={{0,16},{4,20},{8,24},{12,28},{16,0},{20,4},{24,8},{28,12},{1,17},{... | collective-permute-start | bytes 884744 | tf_op jit(solution)/shard_map/ppermute | solution.py:956
  498.6 23.6 %collective-permute-start.80 = (f32[24,256]{1,0:T(8,128)S(1)}, f32[24,256]{1,0:T(8,128)S(1)}, u32[]{:S(2)}, u32[]{:S(2)}) collective-permute-start(f32[24,256]{1,0:T(8,128)S(1)} %sum_small.16.refs_0_.x), channel_id=1, source_target_pairs={{0,8},{4,12},{8,0},{12,4},{16,24},{20,28},{24,16},{28,20},{1,9},{5... | collective-permute-start | bytes 73736 | tf_op jit(solution)/shard_map/ppermute | solution.py:956
  (81 other events, 910.1 us)
Sparse Core Ops, SparseCore 0:
  205.6 67.8 reduce-scatter.2
  284.5 124.7 reduce-scatter.4
